TPU v7x, 32 devices: a whole 2x2x4 slice. The times are simulated.
32 devices in a mesh: mode: 8 (over y, x, core), wall: 2 (over z_hi), ckpt: 2 (over z_lo).
Axes of the slice: x: 2, y: 2, z: 4 (z_hi: 2, z_lo: 2; z = z_hi * 2 + z_lo), core: 2. Of those that a mesh axis runs over, the one named last changes fastest.
Arguments:
- adjoint: float32 [2, 5, 1024, 4096], P(None, None, ('wall', 'ckpt'), 'mode'), may hold values from -6 to 6
- forward: float32 [2, 2, 1024, 4096], P('ckpt', None, 'wall', 'mode'), may hold values from -0.09375 to 0.09375
- mode_map: int32 [4096], P('mode'), may hold values from 0 to 4095, as said below
Outputs:
- adjoint_prev: float32 [2, 5, 1024, 4096], P(None, None, ('wall', 'ckpt'), 'mode')
Inputs may be any that keep to these rules, and one draw needn't show every extreme that they name: mode_map is a permutation of the 64 x 64 modes laid out by frequency: for every block b of 64 consecutive slots there is a frequency p(b) such that slot b * 64 + r holds mode p(b) * 64 + r, and p takes every frequency once.
All inputs are finite; a program needn't handle non-finite values.
Results may differ from a plain program's by a relative error of at most 0.0001.
Values sent between devices are 32-bit elements; how exact they have to be, the bound alone decides.
No kernel may reach another device: no remote copies, remote signals or barrier semaphores. Data moves between devices by JAX's collectives and lax.ppermute only.
A program may use at most 128 MiB of HBM per device.

v0:
```python
import math

import jax
import jax.numpy as jnp
from jax import lax
from jax.sharding import PartitionSpec as P

NF = 64
NK = 64
MODES = 4096


KAPPA = 0.2
COUPLING = 0.5
HIGHEST = lax.Precision.HIGHEST


def with_halo(block, sides, width, periodic):
    for axis, dim in sides:
        count = lax.axis_size(axis)
        forward = [(i, i + 1) for i in range(count - 1)]
        if periodic:
            forward.append((count - 1, 0))
        backward = [(target, source) for source, target in forward]
        low = lax.ppermute(
            lax.slice_in_dim(block, block.shape[dim] - width, None, axis=dim), axis, forward
        )
        high = lax.ppermute(lax.slice_in_dim(block, 0, width, axis=dim), axis, backward)
        block = jnp.concatenate([low, block, high], axis=dim)
    return block


def entering(value, axis, join, neutral):
    count, mine = (lax.axis_size(axis), lax.axis_index(axis))
    pieces = lax.all_gather(value, axis)
    so_far = jnp.full_like(value, 0) + jnp.asarray(neutral, value.dtype)

    def turn(position, so_far):
        longer = join(so_far, pieces[position])
        return jnp.where(position < mine, longer, so_far)

    return lax.fori_loop(0, count - 1, turn, so_far)


def add_pair(earlier, later):
    return earlier + later


def rates(grid_index):
    freq_index = grid_index // NK
    span_index = grid_index % NK
    freq_signed = (freq_index + NF // 2) % NF - NF // 2
    span_signed = (span_index + NK // 2) % NK - NK // 2
    return (2.0 / NF * freq_signed.astype(jnp.float32), 2.0 / NK * span_signed.astype(jnp.float32))


def span_tables(direction):
    col_ids = jnp.arange(NK, dtype=jnp.int32)
    phase_cols = 2.0 * math.pi / NK * (col_ids[:, None] * col_ids[None, :] % NK).astype(jnp.float32)
    return (jnp.cos(phase_cols), direction * jnp.sin(phase_cols))


def row_tables(direction, out_ids, in_ids):
    phase_rows = 2.0 * math.pi / NF * (out_ids[:, None] * in_ids[None, :] % NF).astype(jnp.float32)
    return (jnp.cos(phase_rows), direction * jnp.sin(phase_rows))


def span_dft(real_part, imag_part, direction):
    cosine, sine_part = span_tables(direction)
    real_cos = jnp.einsum("...k,kz->...z", real_part, cosine, precision=HIGHEST)
    real_sin = jnp.einsum("...k,kz->...z", real_part, sine_part, precision=HIGHEST)
    imag_cos = jnp.einsum("...k,kz->...z", imag_part, cosine, precision=HIGHEST)
    imag_sin = jnp.einsum("...k,kz->...z", imag_part, sine_part, precision=HIGHEST)
    return (real_cos - imag_sin, real_sin + imag_cos)


def lead_dft(real_part, imag_part, direction, out_ids, in_ids):
    cos_rows, sin_rows = row_tables(direction, out_ids, in_ids)
    lead_shape = real_part.shape
    flat_real = real_part.reshape(lead_shape[0], -1)
    flat_imag = imag_part.reshape(lead_shape[0], -1)
    out_real = jnp.dot(cos_rows, flat_real, precision=HIGHEST) - jnp.dot(
        sin_rows, flat_imag, precision=HIGHEST
    )
    out_imag = jnp.dot(sin_rows, flat_real, precision=HIGHEST) + jnp.dot(
        cos_rows, flat_imag, precision=HIGHEST
    )
    return (out_real.reshape(lead_shape), out_imag.reshape(lead_shape))


def to_physical(real_part, imag_part, out_ids, in_ids):
    shape_front = real_part.shape[:-1] + (NF, NK)
    span_real, span_imag = span_dft(
        real_part.reshape(shape_front), imag_part.reshape(shape_front), 1.0
    )
    span_real = jnp.moveaxis(span_real, -2, 0)
    span_imag = jnp.moveaxis(span_imag, -2, 0)
    return lead_dft(span_real, span_imag, 1.0, out_ids, in_ids)


def to_spectral(real_part, imag_part, out_ids, in_ids):
    lead_real, lead_imag = lead_dft(real_part, imag_part, -1.0, out_ids, in_ids)
    lead_real = jnp.moveaxis(lead_real, 0, -2)
    lead_imag = jnp.moveaxis(lead_imag, 0, -2)
    span_real, span_imag = span_dft(lead_real, lead_imag, -1.0)
    shape_front = span_real.shape[:-2] + (MODES,)
    return (span_real.reshape(shape_front), span_imag.reshape(shape_front))


def coupling_term(adjoint_slots, forward_phys, block_freq, time_ids):
    a_real, a_imag = to_physical(adjoint_slots[0], adjoint_slots[1], time_ids, block_freq)
    w_real = forward_phys[0][:, None]
    w_imag = forward_phys[1][:, None]
    prod_real = w_real * a_real + w_imag * a_imag
    prod_imag = w_real * a_imag - w_imag * a_real
    real_part, imag_part = to_spectral(prod_real, prod_imag, block_freq, time_ids)
    return jnp.stack([real_part, imag_part]) / (NF * NK)


def add_continuity(stepped, running, row_scale):
    updated_v = jnp.stack(
        [stepped[0, 1] + running[1] * row_scale, stepped[1, 1] - running[0] * row_scale]
    )
    return jnp.concatenate([stepped[:, :1], updated_v[:, None], stepped[:, 2:]], 1)


def wall_step_spectral(current, coupled, alpha_rate, beta_rate, row_scale):
    wrapped = with_halo(current, (("mode", 2),), 1, True)
    below_rim = wrapped[:, :, 0]
    above_rim = wrapped[:, :, -1]
    edge_rims = with_halo(jnp.stack([above_rim, below_rim], 2), ((("wall", "ckpt"), 2),), 1, False)
    position = lax.axis_index("mode")
    below_rim = jnp.where(position == 0, edge_rims[:, :, 0], below_rim)
    above_rim = jnp.where(position == lax.axis_size("mode") - 1, edge_rims[:, :, 3], above_rim)
    padded = jnp.concatenate([below_rim[:, :, None], current, above_rim[:, :, None]], 2)
    stepped = (
        current
        + KAPPA * (padded[:, :, 2:] - 2.0 * current + padded[:, :, :-2])
        - COUPLING * coupled
    )
    source = alpha_rate * stepped[:, 0] + beta_rate * stepped[:, 2]
    running = jnp.cumsum(source, axis=1)
    totals = running[:, -1]
    within = entering(totals, "mode", add_pair, jnp.zeros_like(totals))
    block_sum = lax.psum(totals, "mode")
    across = entering(block_sum, ("wall", "ckpt"), add_pair, jnp.zeros_like(totals))
    running = running + (within + across)[:, None]
    return add_continuity(stepped, running, row_scale)


def to_modes(values):
    return lax.all_to_all(values, "mode", split_axis=3, concat_axis=2, tiled=True)


def on_device(adjoint, forward, mode_map):
    station_count = lax.axis_size("ckpt")
    row_scale = 1.0 / math.sqrt(adjoint.shape[2] * lax.axis_size("wall") * lax.axis_size("ckpt"))
    stored = lax.all_gather(forward, "ckpt", axis=0, tiled=True)
    row_count = adjoint.shape[2]
    own_rows = lax.dynamic_slice_in_dim(stored, lax.axis_index("ckpt") * row_count, row_count, 2)
    full_map = lax.all_gather(mode_map, "mode", axis=0, tiled=True)
    block_freq = full_map.reshape(NF, NK)[:, 0] // NK
    time_ids = jnp.arange(NF, dtype=jnp.int32)
    adjoint_cols, forward_cols = (
        lax.all_to_all(adjoint, "mode", split_axis=2, concat_axis=3, tiled=True),
        lax.all_to_all(own_rows, "mode", split_axis=2, concat_axis=3, tiled=True),
    )
    phys_real, phys_imag = to_physical(forward_cols[:, 0], forward_cols[:, 1], time_ids, block_freq)
    grid_alpha, grid_beta = rates(full_map)
    spectral = adjoint_cols
    for station in range(station_count - 1, -1, -1):
        station_phys = (phys_real[:, station], phys_imag[:, station])
        coupled = coupling_term(spectral, station_phys, block_freq, time_ids)
        spectral = wall_step_spectral(spectral, coupled, grid_alpha, grid_beta, row_scale)
    current = to_modes(spectral)
    return current


def solution(mesh):
    placed = (P(None, None, ("wall", "ckpt"), "mode"), P("ckpt", None, "wall", "mode"), P("mode"))
    return jax.shard_map(
        on_device,
        mesh=mesh,
        in_specs=placed,
        out_specs=P(None, None, ("wall", "ckpt"), "mode"),
        check_vma=False,
    )
```

profile of v0, /device:TPU:0, one launch (start us, length us, event | category | flops | bytes accessed | tf_op | source)
XLA Modules:
  0.0 946.5 jit_solution(16211169976453454492)
XLA Ops:
  6.5 9.0 copy.107
  21.6 96.7 %all-gather.2 = s32[8,1,512]{2,1,0:T(1,128)S(1)} all-gather(s32[1,1,512]{2,1,0:T(1,128)S(1)} %bitcast.288), channel_id=1, replica_groups=mesh['mode'=8,'wall'=2,'ckpt'=2] {'mode'}, dimensions={0}, use_global_device_ids=true | all-gather | bytes 18432 | tf_op jit(solution)/shard_map/all_gather | solution.py:161
  128.9 6.4 copy.194
  140.5 20.3 %fusion.69 = f32[64,5,32,64]{3,0,2,1:T(8,128)} fusion(f32[5,32,64,64]{3,2,1,0:T(8,128)} %reshape_squeeze.20), kind=kOutput, calls=%fused_computation.136 | convolution fusion | flops 503373824 | bytes 5242880 | tf_op jit(solution)/shard_map/...k,kz->...z/dot_general | solution.py:70
  160.8 17.4 %fusion.81 = f32[64,5,32,64]{3,0,2,1:T(8,128)} fusion(f32[5,32,64,64]{3,2,1,0:T(8,128)S(1)} %copy-done), kind=kOutput, calls=%fused_computation.148 | convolution fusion | flops 503373824 | bytes 5242880 | tf_op jit(solution)/shard_map/...k,kz->...z/dot_general | solution.py:71
  178.2 8.8 copy.109
  187.0 6.8 all_to_all.42
  203.6 19.6 %convolution_subtract_fusion.5 = f32[64,5,32,64]{3,0,2,1:T(8,128)S(1)} fusion(f32[64,5,32,64]{3,0,2,1:T(8,128)} %fusion.69, f32[5,32,64,64]{3,2,1,0:T(8,128)} %reshape_squeeze.21), kind=kOutput, calls=%fused_computation.72 | convolution fusion | flops 504029184 | bytes 7864320 | tf_op jit(solution)/shard_map/...k,kz->...z/dot_general | solution.py:73
  223.2 15.6 %convolution_add_fusion.5 = f32[64,5,32,64]{3,0,2,1:T(8,128)S(1)} fusion(f32[64,5,32,64]{3,0,2,1:T(8,128)S(1)} %bitcast.282, f32[5,32,64,64]{3,2,1,0:T(8,128)S(1)} %copy-done.5), kind=kOutput, calls=%fused_computation.71 | convolution fusion | flops 504029184 | bytes 7864320 | tf_op jit(solution)/shard_map/...k,kz->...z/dot_general | solution.py:72
  238.8 6.5 fusion.160
  245.3 7.7 convolution_add_fusion
  257.3 7.5 fusion.153
  266.4 5.5 collective-permute-done.1
  316.5 5.5 mul.451
  328.8 5.5 mul.447
  334.4 11.8 %multiply_subtract_fusion.1 = (f32[64,10240]{1,0:T(8,128)S(1)}, f32[64,10240]{1,0:T(8,128)S(1)}) fusion(f32[64,10240]{1,0:T(8,128)} %mul.451, f32[64,10240]{1,0:T(8,128)} %mul.447, f32[64,10240]{1,0:T(8,128)} %convolution_add_fusion, f32[64,10240]{1,0:T(8,128)} %fusion.153, f32[64,10240]{0,1:T(8,128)} %bitcast.277, s32[64]{0:T(128)S(1)} %copy-done.26), kind=kOutput, calls=%fused_computation.65 | convolution fusion | flops 507961344 | bytes 18350336 | tf_op jit(solution)/shard_map/dot_general | solution.py:82
  362.7 11.6 %fusion.17 = f32[5,32,64,64]{3,2,1,0:T(8,128)} fusion(f32[64,5,32,64]{3,2,1,0:T(8,128)} %reshape.103), kind=kOutput, calls=%fused_computation.41 | convolution fusion | flops 503373824 | bytes 5242880 | tf_op jit(solution)/shard_map/...k,kz->...z/dot_general | solution.py:72
  374.4 8.4 fusion.19
  392.3 12.0 %fusion.36 = f32[5,32,64,64]{3,2,1,0:T(8,128)} fusion(f32[5,32,64,64]{3,2,1,0:T(8,128)} %fusion.17, f32[64,5,32,64]{3,2,1,0:T(8,128)} %reshape.102), kind=kOutput, calls=%fused_computation.68 | convolution fusion | flops 504033280 | bytes 7864320 | tf_op jit(solution)/shard_map/...k,kz->...z/dot_general | solution.py:71
  408.3 12.0 %fusion.33 = f32[5,32,64,64]{3,2,1,0:T(8,128)} fusion(f32[5,32,64,64]{3,2,1,0:T(8,128)} %fusion.19, f32[64,5,32,64]{3,2,1,0:T(8,128)} %reshape.102), kind=kOutput, calls=%fused_computation.67 | convolution fusion | flops 504029184 | bytes 7864320 | tf_op jit(solution)/shard_map/...k,kz->...z/dot_general | solution.py:70
  425.7 7.7 fusion.7
  441.7 9.7 %all-gather = f32[16,1,4096]{2,1,0:T(1,128)S(1)} all-gather(f32[2,1,4096]{2,1,0:T(1,128)S(1)} %get-tuple-element.468), channel_id=2, replica_groups=mesh['mode'=8,'wall'=2,'ckpt'=2] {'mode'}, dimensions={0}, use_global_device_ids=true | all-gather | bytes 294912 | tf_op jit(solution)/shard_map/all_gather | solution.py:35
  454.3 24.3 %psum.14 = f32[1,2,4096]{2,0,1:T(1,128)S(1)} all-reduce(f32[1,2,4096]{2,0,1:T(1,128)} %get-tuple-element.467), channel_id=1, replica_groups=mesh['mode'=8,'wall'=2,'ckpt'=2] {'mode'}, use_global_device_ids=true, to_apply=%region_3.4 | all-reduce | flops 8192 | bytes 65536 | tf_op jit(solution)/shard_map/psum | solution.py:145
  478.6 13.6 %all_gather.28 = f32[4,2,4096]{2,1,0:T(2,128)S(1)} all-gather(f32[1,2,4096]{2,1,0:T(2,128)S(1)} %copy.122), channel_id=1, replica_groups=mesh['mode'=8,'wall'=2,'ckpt'=2] {'wall','ckpt'}, dimensions={0}, use_global_device_ids=true | all-gather | bytes 163840 | tf_op jit(solution)/shard_map/all_gather | solution.py:35
  498.7 5.4 reshape_squeeze.22
  504.1 8.1 fusion.74
  512.2 6.2 fusion.84
  522.1 9.4 subtract_bitcast_fusion
  531.5 5.4 copy.123
  552.1 5.5 mul.476
  560.6 5.6 mul.472
  566.2 9.3 add_bitcast_fusion
  575.4 5.4 copy.124
  612.6 11.3 %fusion.9 = f32[5,32,64,64]{3,2,1,0:T(8,128)} fusion(f32[64,5,32,64]{3,2,1,0:T(8,128)} %reshape.107), kind=kOutput, calls=%fused_computation.33 | convolution fusion | flops 503373824 | bytes 5242880 | tf_op jit(solution)/shard_map/...k,kz->...z/dot_general | solution.py:72
  633.6 12.6 %fusion.42 = f32[5,32,64,64]{3,2,1,0:T(8,128)} fusion(f32[5,32,64,64]{3,2,1,0:T(8,128)} %fusion.9, f32[64,5,32,64]{3,2,1,0:T(8,128)} %reshape.106), kind=kOutput, calls=%fused_computation.70 | convolution fusion | flops 504033280 | bytes 7864320 | tf_op jit(solution)/shard_map/...k,kz->...z/dot_general | solution.py:71
  646.2 8.0 fusion.11
  659.0 8.5 fusion.39
  672.9 5.6 stack_reshape.14
  687.0 6.2 copy_subtract_fusion
  698.5 8.4 all-gather.1
  709.7 23.6 %psum.15 = f32[1,2,4096]{2,0,1:T(1,128)S(1)} all-reduce(f32[1,2,4096]{2,0,1:T(1,128)S(1)} %get-tuple-element.465), channel_id=1, replica_groups=mesh['mode'=8,'wall'=2,'ckpt'=2] {'mode'}, use_global_device_ids=true, to_apply=%region_9.10 | all-reduce | flops 8192 | bytes 65536 | tf_op jit(solution)/shard_map/psum | solution.py:145
  733.4 13.4 %all_gather.31 = f32[4,2,4096]{2,1,0:T(2,128)S(1)} all-gather(f32[1,2,4096]{2,1,0:T(2,128)S(1)} %copy.132), channel_id=1, replica_groups=mesh['mode'=8,'wall'=2,'ckpt'=2] {'wall','ckpt'}, dimensions={0}, use_global_device_ids=true | all-gather | bytes 163840 | tf_op jit(solution)/shard_map/all_gather | solution.py:35
  752.5 23.7 %copy.134 = f32[2,5,32,4096]{2,0,1,3:T(2,128)} copy(f32[2,5,32,4096]{3,2,1,0:T(8,128)} %pad_maximum_fusion.9) | data formatting | bytes 10485760 | tf_op jit(solution)/shard_map/concatenate | solution.py:124
  776.2 23.0 %reshape.127 = f32[8,1,163840]{2,1,0:T(1,128)} reshape(f32[4096,5,2,32]{3,2,1,0:T(2,128)} %bitcast.272) | data formatting | bytes 10485760
  799.1 64.8 %all_to_all.54 = f32[8,1,163840]{2,1,0:T(1,128)} all-to-all(f32[8,1,163840]{2,1,0:T(1,128)} %reshape.127), channel_id=1, replica_groups=mesh['mode'=8,'wall'=2,'ckpt'=2] {'mode'}, dimensions={0} | all-to-all | bytes 10485760 | tf_op jit(solution)/shard_map/all_to_all | solution.py:152
  864.5 16.8 %reduce.7 = f32[8,163840]{1,0:T(8,128)} reduce(f32[8,1,163840]{2,1,0:T(1,128)} %all_to_all.54, f32[]{:T(128)} %broadcast.435), dimensions={1}, to_apply=%all_to_all.47.reduce_sub_computation | reduce | bytes 10485764 | tf_op jit(solution)/shard_map/all_to_all | solution.py:152
  881.3 34.2 %reshape.128 = f32[4096,5,2,32]{3,2,1,0:T(2,128)} reshape(f32[8,163840]{1,0:T(8,128)} %reduce.7) | data formatting | bytes 10485760
  915.5 23.7 %copy.135 = f32[2,5,8,32,512]{4,3,2,1,0:T(8,128)} copy(f32[2,5,8,32,512]{3,0,1,4,2:T(2,128)} %bitcast.273) | data formatting | bytes 10485760 | tf_op jit(solution)/shard_map/all_to_all | solution.py:152
  (215 shorter events, 238.9 us)
Async XLA Ops:
  15.5 6.1 copy-start.30
  15.5 109.0 %all-to-all-start = ((f32[2,5,256,512]{3,1,0,2:T(8,128)}), f32[2,5,256,512]{3,1,0,2:T(8,128)}, u32[]{:S(2)}, u32[]{:S(2)}) async-start(f32[2,5,256,512]{3,1,0,2:T(8,128)} %copy.107), calls=%async_computation | async-start | bytes 16777216 | tf_op jit(solution)/shard_map/all_to_all | solution.py:165
  20.8 99.0 %all-gather.5.cloned.1.call-start = ((), (), s32[]{:S(2)}) async-start(), calls=%async_computation.3 | async-start | bytes 6291456 | tf_op jit(solution)/shard_map/all_gather | solution.py:158
  119.1 138.1 %copy-start.25 = (s32[64]{0:T(128)}, s32[64]{0:T(128)S(1)}, u32[]{:S(2)}) copy-start(s32[64]{0:T(128)S(1)} %and_select_fusion) | copy-start | bytes 772
  124.5 147.6 %all-to-all-start.1 = ((f32[2,2,256,512]{3,1,0,2:T(2,128)}), f32[2,2,256,512]{3,1,0,2:T(2,128)}, u32[]{:S(2)}, u32[]{:S(2)}) async-start(f32[2,2,256,512]{3,1,0,2:T(2,128)} %copy.110), calls=%async_computation.1 | async-start | bytes 4194304 | tf_op jit(solution)/shard_map/all_to_all | solution.py:166
  140.5 20.3 %copy-start = (f32[5,32,64,64]{3,2,1,0:T(8,128)S(1)}, f32[5,32,64,64]{3,2,1,0:T(8,128)}, u32[]{:S(2)}) copy-start(f32[5,32,64,64]{3,2,1,0:T(8,128)} %reshape_squeeze.20) | copy-start | bytes 7864324
  195.8 57.3 %collective-permute-start.2 = (f32[2,5,1,4096]{3,2,0,1:T(1,128)S(1)}, f32[2,5,1,4096]{3,2,0,1:T(1,128)S(1)}, u32[]{:S(2)}, u32[]{:S(2)}) collective-permute-start(f32[2,5,1,4096]{3,2,0,1:T(1,128)S(1)} %get-tuple-element.458), channel_id=1, source_target_pairs={{0,4},{4,8},{8,12},{12,16},{16,20},{20,24},{24,28},{28,0},{1,5},{5... | collective-permute-start | bytes 491528 | tf_op jit(solution)/shard_map/ppermute | solution.py:25
  196.2 68.6 %collective-permute-start = (f32[2,5,1,4096]{3,2,0,1:T(1,128)S(1)}, f32[2,5,1,4096]{3,2,0,1:T(1,128)S(1)}, u32[]{:S(2)}, u32[]{:S(2)}) collective-permute-start(f32[2,5,1,4096]{3,2,0,1:T(1,128)S(1)} %get-tuple-element.457), channel_id=1, source_target_pairs={{4,0},{8,4},{12,8},{16,12},{20,16},{24,20},{28,24},{0,28},{5,1},{9... | collective-permute-start | bytes 491528 | tf_op jit(solution)/shard_map/ppermute | solution.py:28
  198.5 24.7 %slice-start.4 = ((s8[5242880]{0:T(1024)(128)(4,1)}), s8[1048576]{0:T(1024)(128)(4,1)S(1)}, s32[]{:S(2)}) async-start(s8[5242880]{0:T(1024)(128)(4,1)} %bitcast.281), calls=%async_computation.8 | async-start | bytes 2097152
  203.6 19.6 %copy-start.5 = (f32[5,32,64,64]{3,2,1,0:T(8,128)S(1)}, f32[5,32,64,64]{3,2,1,0:T(8,128)}, u32[]{:S(2)}) copy-start(f32[5,32,64,64]{3,2,1,0:T(8,128)} %reshape_squeeze.21) | copy-start | bytes 7864324
  203.6 19.6 %slice-start.5 = ((s8[5242880]{0:T(1024)(128)(4,1)}), s8[4194304]{0:T(1024)(128)(4,1)S(1)}, s32[]{:S(2)}) async-start(s8[5242880]{0:T(1024)(128)(4,1)} %bitcast.281), calls=%async_computation.9 | async-start | bytes 8388608
  238.8 14.2 %copy-start.3 = (f32[64,5,32,64]{3,0,2,1:T(8,128)}, f32[64,5,32,64]{3,0,2,1:T(8,128)S(1)}, u32[]{:S(2)}) copy-start(f32[64,5,32,64]{3,0,2,1:T(8,128)S(1)} %convolution_add_fusion.5) | copy-start | bytes 7864324
  253.0 13.2 %collective-permute-start.3 = (f32[2,5,1,4096]{3,2,0,1:T(1,128)S(1)}, f32[2,5,1,4096]{3,2,0,1:T(1,128)S(1)}, u32[]{:S(2)}, u32[]{:S(2)}) collective-permute-start(f32[2,5,1,4096]{3,2,0,1:T(1,128)S(1)} %collective-permute-done.2), channel_id=1, source_target_pairs={{0,1},{1,2},{2,3},{4,5},{5,6},{6,7},{8,9},{9,10},{10,11},{12,13},{... | collective-permute-start | bytes 491528 | tf_op jit(solution)/shard_map/ppermute | solution.py:25
  264.8 7.2 collective-permute-start.1
  297.2 5.8 copy-start.18
  316.5 5.5 copy-start.19
  328.8 5.5 copy-start.26
  334.4 11.8 %copy-start.28 = (s32[64]{0:T(128)S(1)}, s32[64]{0:T(128)}, u32[]{:S(2)}) copy-start(s32[64]{0:T(128)} %get-tuple-element.409) | copy-start | bytes 772
  362.7 11.6 %copy-start.1 = (f32[64,5,32,64]{3,2,1,0:T(8,128)S(1)}, f32[64,5,32,64]{3,2,1,0:T(8,128)}, u32[]{:S(2)}) copy-start(f32[64,5,32,64]{3,2,1,0:T(8,128)} %reshape.103) | copy-start | bytes 7864324
  374.4 8.4 copy-start.12
  433.4 2.7 copy-start.7
  433.4 2.7 copy-start.24
  433.8 61.8 %copy-start.8 = (f32[2,3,32,4096]{3,2,0,1:T(8,128)}, f32[2,3,32,4096]{3,2,0,1:T(8,128)S(1)}, u32[]{:S(2)}) copy-start(f32[2,3,32,4096]{3,2,0,1:T(8,128)S(1)} %slice.164) | copy-start | bytes 9437188
  492.7 2.9 copy-start.16
  495.6 1.0 copy-start.17
  504.1 8.1 copy-start.2
  536.9 3.9 copy-start.27
  540.9 8.2 copy-start.20
  552.1 5.5 copy-start.21
  585.2 1.5 copy-start.10
  586.7 4.6 copy-start.13
  586.7 4.6 copy-start.14
  586.7 4.6 copy-start.15
  591.2 5.1 copy-start.29
  603.1 53.7 %collective-permute-start.6 = (f32[2,5,1,4096]{3,2,0,1:T(1,128)S(1)}, f32[2,5,1,4096]{3,2,0,1:T(1,128)S(1)}, u32[]{:S(2)}, u32[]{:S(2)}) collective-permute-start(f32[2,5,1,4096]{3,2,0,1:T(1,128)S(1)} %get-tuple-element.452), channel_id=1, source_target_pairs={{0,4},{4,8},{8,12},{12,16},{16,20},{20,24},{24,28},{28,0},{1,5},{5... | collective-permute-start | bytes 491528 | tf_op jit(solution)/shard_map/ppermute | solution.py:25
  612.6 11.3 %copy-start.11 = (f32[64,10240]{1,0:T(8,128)S(1)}, f32[64,10240]{1,0:T(8,128)}, u32[]{:S(2)}) copy-start(f32[64,10240]{1,0:T(8,128)} %fusion.172) | copy-start | bytes 7864324
  628.2 17.9 %slice-start = ((s8[5242880]{0:T(1024)(128)(4,1)}), s8[1048576]{0:T(1024)(128)(4,1)S(1)}, s32[]{:S(2)}) async-start(s8[5242880]{0:T(1024)(128)(4,1)} %bitcast.274), calls=%async_computation.4 | async-start | bytes 2097152
  633.6 12.6 %slice-start.1 = ((s8[5242880]{0:T(1024)(128)(4,1)}), s8[4194304]{0:T(1024)(128)(4,1)S(1)}, s32[]{:S(2)}) async-start(s8[5242880]{0:T(1024)(128)(4,1)} %bitcast.274), calls=%async_computation.5 | async-start | bytes 8388608
  646.2 12.9 %copy-start.4 = (f32[64,5,32,64]{3,2,1,0:T(8,128)S(1)}, f32[64,5,32,64]{3,2,1,0:T(8,128)}, u32[]{:S(2)}) copy-start(f32[64,5,32,64]{3,2,1,0:T(8,128)} %reshape.106) | copy-start | bytes 7864324
  654.1 24.3 %collective-permute-start.4 = (f32[2,5,1,4096]{3,2,0,1:T(1,128)S(1)}, f32[2,5,1,4096]{3,2,0,1:T(1,128)}, u32[]{:S(2)}, u32[]{:S(2)}) collective-permute-start(f32[2,5,1,4096]{3,2,0,1:T(1,128)S(1)} %get-tuple-element.451), channel_id=1, source_target_pairs={{4,0},{8,4},{12,8},{16,12},{20,16},{24,20},{28,24},{0,28},{5,1},{9... | collective-permute-start | bytes 491528 | tf_op jit(solution)/shard_map/ppermute | solution.py:28
  656.8 22.9 %collective-permute-start.7 = (f32[2,5,1,4096]{3,2,0,1:T(1,128)S(1)}, f32[2,5,1,4096]{3,2,0,1:T(1,128)}, u32[]{:S(2)}, u32[]{:S(2)}) collective-permute-start(f32[2,5,1,4096]{3,2,0,1:T(1,128)S(1)} %collective-permute-done.6), channel_id=1, source_target_pairs={{0,1},{1,2},{2,3},{4,5},{5,6},{6,7},{8,9},{9,10},{10,11},{12,13},{... | collective-permute-start | bytes 491528 | tf_op jit(solution)/shard_map/ppermute | solution.py:25
  672.9 14.1 %copy-start.9 = (f32[2,3,32,4096]{3,2,0,1:T(8,128)S(1)}, f32[2,3,32,4096]{3,2,0,1:T(8,128)}, u32[]{:S(2)}) copy-start(f32[2,3,32,4096]{3,2,0,1:T(8,128)} %copy-done.8) | copy-start | bytes 9437188
  678.5 7.4 collective-permute-start.5
  693.2 2.4 copy-start.6
  693.2 16.1 %copy-start.23 = (f32[2,4096]{1,0:T(2,128)S(1)}, f32[2,4096]{1,0:T(2,128)}, u32[]{:S(2)}) copy-start(f32[2,4096]{1,0:T(2,128)} %custom-call.2) | copy-start | bytes 98308
  693.2 53.5 %copy-start.22 = (f32[2,4096]{1,0:T(2,128)S(1)}, f32[2,4096]{1,0:T(2,128)}, u32[]{:S(2)}) copy-start(f32[2,4096]{1,0:T(2,128)} %custom-call.3) | copy-start | bytes 98308
  697.3 52.4 %slice-start.2 = ((f32[2,5,32,4096]{3,2,1,0:T(8,128)}), f32[2,3,32,4096]{3,2,1,0:T(8,128)S(1)}, s32[]{:S(2)}) async-start(f32[2,5,32,4096]{3,2,1,0:T(8,128)} %copy-done.6), calls=%async_computation.6 | async-start | bytes 6291456 | tf_op jit(solution)/shard_map/slice | solution.py:124
  746.9 2.8 slice-start.3
Sparse Core Ops, SparseCore 0:
  23.2 59.6 all-gather.4
where the time goes:
time: 958 us; the launch traced here: 946 us
  matrix products  295 us (31%)
  local copies, waits for them, and re-layouts  293 us (31%)
  blocking collectives  254 us (27%)
  other arithmetic  52.8 us (6%)
  starting transfers between devices  24.4 us (3%)
  between operations  14.6 us (2%)
  waiting for transfers between devices  11.3 us (1%)
    all_gather x1, blocking collectives, on_device(): full_map = lax.all_gather(mode_map, 'mode', axis=0, tiled=True)  96.7 us
    unnamed x73, local copies, waits for them, and re-layouts  71.3 us
    all_to_all x1, blocking collectives, to_modes(): lax.all_to_all(values, 'mode', split_axis=3, concat_axis=2, tiled=True)  64.8 us
    dot_general x5, matrix products, span_dft(): real_cos = jnp.einsum('...k,kz->...z', real_part, cosine, precision=HIGHEST)  52.1 us
    dot_general x5, matrix products, span_dft(): jnp.einsum('...k,kz->...z', real_part, sine_part, precision=HIGHEST)  51.5 us
    dot_general x5, matrix products, span_dft(): imag_cos = jnp.einsum('...k,kz->...z', imag_part, cosine, precision=HIGHEST)  49.8 us
    dot_general x5, matrix products, span_dft(): jnp.einsum('...k,kz->...z', imag_part, sine_part, precision=HIGHEST)  49 us
    psum x2, blocking collectives, wall_step_spectral(): block_sum = lax.psum(totals, 'mode')  47.9 us
  transfers between devices with their start and end apart: 11, of which 2 were waited for; matrix products, arithmetic and copies ran while one was open for 21% of the time, Pallas kernels for 0%

commit v1 on v0

v1 whole, which is shorter than its diff:
```python
import functools
import math

import jax
import jax.numpy as jnp
import numpy as np
from jax import lax
from jax.experimental import pallas as pl
from jax.experimental.pallas import tpu as pltpu
from jax.sharding import PartitionSpec as P

NF = 64
NK = 64
LANES = 2 * NK
KAPPA = 0.2
COUPLING = 0.5
HIGHEST = lax.Precision.HIGHEST
ROW_BLOCKS = ("wall", "ckpt")
ALL_AXES = ("mode", "wall", "ckpt")
VMEM = pltpu.CompilerParams(vmem_limit_bytes=56 * 1024 * 1024)
F32 = jnp.float32


def complex_lanes(matrix):
    twice = np.kron(np.eye(2), matrix)
    return np.block([[twice.real, twice.imag], [-twice.imag, twice.real]]).astype(np.float32)


def span_matrix(direction):
    ids = np.arange(NK)
    return np.exp(2j * math.pi * direction * (np.outer(ids, ids) % NK) / NK)


def beta_matrix():
    ids = np.arange(NK)
    signed = (ids + NK // 2) % NK - NK // 2
    return span_matrix(-1) @ np.diag(2.0 / NK * signed) @ span_matrix(1) / NK


def low_half(shape):
    return lax.broadcasted_iota(jnp.int32, shape, len(shape) - 1) < NK


def swap(value):
    return pltpu.roll(value, NK, value.ndim - 1)


def dft4(x, sign):
    (ar, ai), (br, bi), (cr, ci), (dr, di) = x
    pr, pi, mr, mi = ar + cr, ai + ci, ar - cr, ai - ci
    qr, qi, nr, ni = br + dr, bi + di, br - dr, bi - di
    if sign > 0:
        nr, ni = -ni, nr
    else:
        nr, ni = ni, -nr
    return [(pr + qr, pi + qi), (mr + nr, mi + ni), (pr - qr, pi - qi), (mr - nr, mi - ni)]


def dft8(x, sign):
    even = dft4(x[0::2], sign)
    odd = dft4(x[1::2], sign)
    half = math.sqrt(0.5)
    (r1, i1), (r2, i2), (r3, i3) = odd[1], odd[2], odd[3]
    if sign > 0:
        odd[1] = (half * (r1 - i1), half * (i1 + r1))
        odd[2] = (-i2, r2)
        odd[3] = (-half * (r3 + i3), half * (r3 - i3))
    else:
        odd[1] = (half * (r1 + i1), half * (i1 - r1))
        odd[2] = (i2, -r2)
        odd[3] = (half * (i3 - r3), -half * (i3 + r3))
    first = [(a + c, b + d) for (a, b), (c, d) in zip(even, odd)]
    second = [(a - c, b - d) for (a, b), (c, d) in zip(even, odd)]
    return first + second


def turned(pair, power, sign):
    power %= NF
    if power == 0:
        return pair
    angle = 2.0 * math.pi * power / NF
    c, s = math.cos(angle), sign * math.sin(angle)
    re, im = pair
    return (c * re - s * im, c * im + s * re)


class Sizes:
    def __init__(self, rows, slots):
        self.group = lax.axis_size("mode")
        self.block_rows = rows
        self.slots = slots
        self.lane_groups = slots // LANES
        self.blocks = slots // NK
        self.rows = rows // self.group
        self.half = self.rows // 2
        self.tile = min(8, self.half)
        self.tiles = self.half // self.tile
        self.padded = (self.half + 7) // 8 * 8 + 16
        self.body = 2 * self.blocks * self.half
        self.rims = 2 * self.blocks


def cut_pieces(sz, with_rims, me, planes, out_at, k):
    row = pl.multiple_of((me ^ k) * sz.rows, sz.rows)
    for g in range(sz.lane_groups):
        whole = planes[g, pl.ds(row, sz.rows), :]
        for c in range(2):
            part = whole[:, c * LANES : (c + 1) * LANES]
            top, bottom = part[: sz.half], part[sz.half :]
            low = low_half(top.shape)
            for odd, value in (
                (0, jnp.where(low, top, swap(bottom))),
                (1, jnp.where(low, swap(top), bottom)),
            ):
                place = (c * sz.blocks + 2 * g + odd) * sz.half
                out_at(place, sz.half, value)
    if not with_rims:
        return
    dest = me ^ k
    before = jnp.where(dest == 0, sz.block_rows, dest * sz.rows - 1)
    after = jnp.where(dest == sz.group - 1, sz.block_rows + 1, (dest + 1) * sz.rows)
    for g in range(sz.lane_groups):
        down = planes[g, pl.ds(before, 1), :]
        up = planes[g, pl.ds(after, 1), :]
        for c in range(2):
            top = down[:, c * LANES : (c + 1) * LANES]
            bottom = up[:, c * LANES : (c + 1) * LANES]
            low = low_half(top.shape)
            place = sz.body + c * sz.blocks + 2 * g
            out_at(place, 1, jnp.where(low, top, swap(bottom)))
            out_at(place + 1, 1, jnp.where(low, swap(top), bottom))


def adjoint_prep_kernel(sz, me_ref, x_ref, rim_ref, w_ref, *rest):
    outs, planes = rest[: sz.group], rest[sz.group]
    w = w_ref[...]
    for g in range(sz.lane_groups):
        at = pl.ds(g * LANES, LANES)
        x = jnp.concatenate([x_ref[0, 0, :, at], x_ref[1, 0, :, at]], axis=1)
        planes[g, : sz.block_rows, :] = jnp.dot(x, w, precision=HIGHEST, preferred_element_type=F32)
        rim = jnp.concatenate([rim_ref[0, 0, :, at], rim_ref[1, 0, :, at]], axis=1)
        planes[g, sz.block_rows :, :] = jnp.dot(rim, w, precision=HIGHEST, preferred_element_type=F32)
    me = me_ref[0]
    for k in range(sz.group):

        def out_at(place, count, value, out=outs[k]):
            out[0, place : place + count, :] = value

        cut_pieces(sz, True, me, planes, out_at, k)


def adjoint_prep(sz, me, adjoint, rims, fields):
    count = len(fields)
    stride = fields[1] - fields[0] if count > 1 else 1
    first = fields[0]
    length = sz.body + sz.rims
    return pl.pallas_call(
        functools.partial(adjoint_prep_kernel, sz),
        grid_spec=pltpu.PrefetchScalarGridSpec(
            num_scalar_prefetch=1,
            grid=(count,),
            in_specs=[
                pl.BlockSpec(
                    (2, 1, sz.block_rows, sz.slots), lambda i, me: (0, first + stride * i, 0, 0)
                ),
                pl.BlockSpec((2, 1, 8, sz.slots), lambda i, me: (0, first + stride * i, 0, 0)),
                pl.BlockSpec((2 * LANES, 2 * LANES), lambda i, me: (0, 0)),
            ],
            out_specs=[pl.BlockSpec((1, length, LANES), lambda i, me: (i, 0, 0))] * sz.group,
            scratch_shapes=[pltpu.VMEM((sz.lane_groups, sz.block_rows + 8, 2 * LANES), F32)],
        ),
        out_shape=[jax.ShapeDtypeStruct((count, length, LANES), F32)] * sz.group,
        compiler_params=VMEM,
        name="adjoint_prep",
    )(me, adjoint, rims, jnp.asarray(complex_lanes(span_matrix(1))))


def forward_prep_kernel(sz, me_ref, x_ref, w_ref, *rest):
    outs, planes = rest[: sz.group], rest[sz.group]
    w = w_ref[...]
    for g in range(sz.lane_groups):
        at = pl.ds(g * LANES, LANES)
        x = jnp.concatenate([x_ref[0, 0, :, at], x_ref[0, 1, :, at]], axis=1)
        planes[g, :, :] = jnp.dot(x, w, precision=HIGHEST, preferred_element_type=F32)
    me = me_ref[0]
    for k in range(sz.group):

        def out_at(place, count, value, out=outs[k]):
            out[0, place : place + count, :] = value

        cut_pieces(sz, False, me, planes, out_at, k)


def forward_prep(sz, me, both):
    stations = both.shape[0]
    return pl.pallas_call(
        functools.partial(forward_prep_kernel, sz),
        grid_spec=pltpu.PrefetchScalarGridSpec(
            num_scalar_prefetch=1,
            grid=(stations,),
            in_specs=[
                pl.BlockSpec((1, 2, sz.block_rows, sz.slots), lambda i, me: (i, 0, 0, 0)),
                pl.BlockSpec((2 * LANES, 2 * LANES), lambda i, me: (0, 0)),
            ],
            out_specs=[pl.BlockSpec((1, sz.body, LANES), lambda i, me: (i, 0, 0))] * sz.group,
            scratch_shapes=[pltpu.VMEM((sz.lane_groups, sz.block_rows, 2 * LANES), F32)],
        ),
        out_shape=[jax.ShapeDtypeStruct((stations, sz.body, LANES), F32)] * sz.group,
        compiler_params=VMEM,
        name="forward_prep",
    )(me, both, jnp.asarray(complex_lanes(span_matrix(1))))


def gather_pieces(sz, table_ref, pieces, state, lead, rims=None):
    for k, piece in enumerate(pieces):
        for j in range(sz.blocks):
            freq = table_ref[k * sz.blocks + j]
            for c in range(2):
                at = (c * sz.blocks + j) * sz.half
                state[c, freq, lead : lead + sz.half, :] = piece[0, at : at + sz.half, :]
                if rims is not None:
                    rim = sz.body + c * sz.blocks + j
                    rims[c, pl.ds(freq, 1), :] = piece[0, rim : rim + 1, :]


def lead_first(sz, state, lead, work, s):
    rows = pl.ds(lead + s * sz.tile, sz.tile)
    out_rows = pl.ds(s * sz.tile, sz.tile)
    for a in range(8):
        x = [(state[0, a + 8 * b, rows, :], state[1, a + 8 * b, rows, :]) for b in range(8)]
        for t, pair in enumerate(dft8(x, 1)):
            re, im = turned(pair, a * t, 1)
            work[0, 8 * t + a, out_rows, :] = re
            work[1, 8 * t + a, out_rows, :] = im


def lead_second(sz, work, t, s):
    rows = pl.ds(s * sz.tile, sz.tile)
    x = [(work[0, 8 * t + a, rows, :], work[1, 8 * t + a, rows, :]) for a in range(8)]
    return dft8(x, 1)


def forward_kernel(sz, table_ref, *rest):
    pieces, out, state, work = rest[: sz.group], rest[sz.group], rest[-2], rest[-1]
    gather_pieces(sz, table_ref, pieces, state, 0)

    @pl.loop(0, sz.tiles)
    def _(s):
        rows = pl.ds(s * sz.tile, sz.tile)
        lead_first(sz, state, 0, work, s)
        for t in range(8):
            for u, (re, im) in enumerate(lead_second(sz, work, t, s)):
                out[0, 0, 8 * t + u, rows, :] = re
                out[0, 1, 8 * t + u, rows, :] = im


def forward_physical(sz, table, pieces):
    stations = pieces[0].shape[0]
    full = (2, NF, sz.half, LANES)
    return pl.pallas_call(
        functools.partial(forward_kernel, sz),
        grid_spec=pltpu.PrefetchScalarGridSpec(
            num_scalar_prefetch=1,
            grid=(stations,),
            in_specs=[pl.BlockSpec((1, sz.body, LANES), lambda i, t: (i, 0, 0))] * sz.group,
            out_specs=pl.BlockSpec((1,) + full, lambda i, t: (i, 0, 0, 0, 0)),
            scratch_shapes=[pltpu.VMEM(full, F32), pltpu.VMEM(full, F32)],
        ),
        out_shape=jax.ShapeDtypeStruct((stations,) + full, F32),
        compiler_params=VMEM,
        name="forward_physical",
    )(table, *pieces)


def place_edges(sz, state, rims):
    padded = sz.padded
    rows = state.reshape(2 * NF * padded, LANES)
    first = rows[pl.ds(8, 2 * NF, stride=padded), :]
    last = rows[pl.ds(8 + sz.half - 1, 2 * NF, stride=padded), :]
    low = low_half(first.shape)
    rows[pl.ds(7, 2 * NF, stride=padded), :] = jnp.where(low, rims, swap(last))
    rows[pl.ds(8 + sz.half, 2 * NF, stride=padded), :] = jnp.where(low, swap(first), rims)


def advance(sz, state, work, phys, store, s):
    rows = pl.ds(s * sz.tile, sz.tile)
    lead_first(sz, state, 8, work, s)
    for t in range(8):
        here = lead_second(sz, work, t, s)
        product = []
        for u, (re, im) in enumerate(here):
            wr, wi = phys[0, 0, 8 * t + u, rows, :], phys[0, 1, 8 * t + u, rows, :]
            product.append((wr * re + wi * im, wr * im - wi * re))
        for a, pair in enumerate(dft8(product, -1)):
            re, im = turned(pair, a * t, -1)
            work[0, 8 * t + a, rows, :] = re
            work[1, 8 * t + a, rows, :] = im
    for a in range(8):
        x = [(work[0, 8 * t + a, rows, :], work[1, 8 * t + a, rows, :]) for t in range(8)]
        for b, pair in enumerate(dft8(x, -1)):
            f = a + 8 * b
            for c in range(2):
                mid = state[c, f, pl.ds(8 + s * sz.tile, sz.tile), :]
                up = state[c, f, pl.ds(9 + s * sz.tile, sz.tile), :]
                down = state[c, f, pl.ds(7 + s * sz.tile, sz.tile), :]
                stepped = (1.0 - 2.0 * KAPPA) * mid + KAPPA * (up + down)
                store(c, f, s, stepped - (COUPLING / NF) * pair[c])


def ends_of(sz, stepped, first_ref, last_ref):
    if sz.half % 8:
        first = stepped[:, :, 0, :].reshape(2 * NF, LANES)
        last = stepped[:, :, sz.half - 1, :].reshape(2 * NF, LANES)
    else:
        rows = stepped.reshape(2 * NF * sz.half, LANES)
        first = rows[pl.ds(0, 2 * NF, stride=sz.half), :]
        last = rows[pl.ds(sz.half - 1, 2 * NF, stride=sz.half), :]
    low = low_half((NF, LANES))
    first_ref[0] = jnp.where(low, first[:NF], swap(first[NF:]))
    last_ref[0] = jnp.where(low, swap(last[:NF]), last[NF:])


def station_one_kernel(sz, table_ref, *rest):
    pieces = rest[: sz.group]
    phys, out, first_ref, last_ref, total_ref, state, work, rims = rest[sz.group :]
    gather_pieces(sz, table_ref, pieces, state, 8, rims)
    place_edges(sz, state, rims.reshape(2 * NF, LANES)[...])

    @pl.loop(0, sz.tiles)
    def _(s):
        def store(c, f, s, value):
            out[0, c, f, pl.ds(s * sz.tile, sz.tile), :] = value

        advance(sz, state, work, phys, store, s)

    ends_of(sz, out.at[0], first_ref, last_ref)
    sums = jnp.sum(out[0], axis=2)
    sums = sums + swap(sums)
    total_ref[0] = jnp.where(low_half((NF, LANES)), sums[0], sums[1])


def station_one(sz, table, pieces, phys, station):
    count = pieces[0].shape[0]
    full = (2, NF, sz.half, LANES)
    flat = pl.BlockSpec((1, NF, LANES), lambda i, t: (i, 0, 0))
    flat_shape = jax.ShapeDtypeStruct((count, NF, LANES), F32)
    return pl.pallas_call(
        functools.partial(station_one_kernel, sz),
        grid_spec=pltpu.PrefetchScalarGridSpec(
            num_scalar_prefetch=1,
            grid=(count,),
            in_specs=[pl.BlockSpec((1, sz.body + sz.rims, LANES), lambda i, t: (i, 0, 0))] * sz.group
            + [pl.BlockSpec((1,) + full, lambda i, t: (station, 0, 0, 0, 0))],
            out_specs=[pl.BlockSpec((1,) + full, lambda i, t: (i, 0, 0, 0, 0)), flat, flat, flat],
            scratch_shapes=[
                pltpu.VMEM((2, NF, sz.padded, LANES), F32),
                pltpu.VMEM(full, F32),
                pltpu.VMEM((2, NF, LANES), F32),
            ],
        ),
        out_shape=[jax.ShapeDtypeStruct((count,) + full, F32), flat_shape, flat_shape, flat_shape],
        compiler_params=VMEM,
        name="station_one",
    )(table, *pieces, phys)


def running_rows(sz, value, start):
    row = lax.broadcasted_iota(jnp.int32, value.shape, 0)
    reach = 1
    while reach < sz.half:
        value = value + jnp.where(row >= reach, pltpu.roll(value, reach, 0), 0.0)
        reach *= 2
    bottom = jnp.where(low_half((1, LANES)), 0.0, swap(value[sz.half - 1 :]))
    return value + (bottom + start)


def add_running_kernel(sz, row_scale, stepped, zero, two, alpha_ref, start, w_ref, out, first, last):
    both = jnp.concatenate([two[0, 0], two[0, 1]], axis=2).reshape(NF * sz.half, 2 * LANES)
    turned_two = jnp.dot(both, w_ref[...], precision=HIGHEST, preferred_element_type=F32)
    for f in range(NF):
        at = f * sz.half
        alpha = 2.0 / NF * ((f + NF // 2) % NF - NF // 2)
        spread = start[pl.ds(f, 1), :]
        low = low_half((1, LANES))
        starts = (jnp.where(low, spread, swap(spread)), jnp.where(low, swap(spread), spread))
        run = []
        for c in range(2):
            source = turned_two[at : at + sz.half, c * LANES : (c + 1) * LANES]
            source = source + alpha * zero[0, c, f]
            run.append(running_rows(sz, source, starts[c]))
        out[0, 0, f] = stepped[0, 0, f] + row_scale * run[1]
        out[0, 1, f] = stepped[0, 1, f] - row_scale * run[0]
    ends_of(sz, out.at[0], first, last)


def add_running(sz, row_scale, stepped, pair, start):
    full = (1, 2, NF, sz.half, LANES)
    flat = pl.BlockSpec((1, NF, LANES), lambda i: (0, 0, 0))
    flat_shape = jax.ShapeDtypeStruct((1, NF, LANES), F32)
    return pl.pallas_call(
        functools.partial(add_running_kernel, sz, row_scale),
        grid=(1,),
        in_specs=[
            pl.BlockSpec(full, lambda i: (0, 0, 0, 0, 0)),
            pl.BlockSpec(full, lambda i: (0, 0, 0, 0, 0)),
            pl.BlockSpec(full, lambda i: (1, 0, 0, 0, 0)),
            pl.BlockSpec((8, LANES), lambda i: (0, 0)),
            pl.BlockSpec((NF, LANES), lambda i: (0, 0)),
            pl.BlockSpec((2 * LANES, 2 * LANES), lambda i: (0, 0)),
        ],
        out_specs=[pl.BlockSpec(full, lambda i: (0, 0, 0, 0, 0)), flat, flat],
        out_shape=[jax.ShapeDtypeStruct(full, F32), flat_shape, flat_shape],
        compiler_params=VMEM,
        name="add_running",
    )(
        stepped,
        pair,
        pair,
        jnp.zeros((8, LANES), F32),
        start,
        jnp.asarray(complex_lanes(beta_matrix())),
    )


def station_zero_kernel(sz, table_ref, current, before, after, phys, *rest):
    outs, (state, work, stepped) = rest[: sz.group], rest[sz.group :]
    state[:, :, 8 : 8 + sz.half, :] = current[0]
    low = low_half((NF, LANES))
    rims = jnp.concatenate(
        [jnp.where(low, before[0], swap(after[0])), jnp.where(low, swap(before[0]), after[0])], 0
    )
    place_edges(sz, state, rims)

    @pl.loop(0, sz.tiles)
    def _(s):
        def store(c, f, s, value):
            stepped[c, f, pl.ds(s * sz.tile, sz.tile), :] = value

        advance(sz, state, work, phys, store, s)

    for k in range(sz.group):
        for j in range(sz.blocks):
            freq = table_ref[k * sz.blocks + j]
            for c in range(2):
                at = (c * sz.blocks + j) * sz.half
                outs[k][0, at : at + sz.half, :] = stepped[c, freq]


def station_zero(sz, table, current, before, after, phys, station):
    count = current.shape[0]
    full = (2, NF, sz.half, LANES)
    flat = pl.BlockSpec((1, NF, LANES), lambda i, t: (i, 0, 0))
    return pl.pallas_call(
        functools.partial(station_zero_kernel, sz),
        grid_spec=pltpu.PrefetchScalarGridSpec(
            num_scalar_prefetch=1,
            grid=(count,),
            in_specs=[
                pl.BlockSpec((1,) + full, lambda i, t: (i, 0, 0, 0, 0)),
                flat,
                flat,
                pl.BlockSpec((1,) + full, lambda i, t: (station, 0, 0, 0, 0)),
            ],
            out_specs=[pl.BlockSpec((1, sz.body, LANES), lambda i, t: (i, 0, 0))] * sz.group,
            scratch_shapes=[
                pltpu.VMEM((2, NF, sz.padded, LANES), F32),
                pltpu.VMEM(full, F32),
                pltpu.VMEM(full, F32),
            ],
        ),
        out_shape=[jax.ShapeDtypeStruct((count, sz.body, LANES), F32)] * sz.group,
        compiler_params=VMEM,
        name="station_zero",
    )(table, current, before, after, phys)


def join_pieces(sz, me, pieces, planes):
    for k, piece in enumerate(pieces):
        row = pl.multiple_of((me ^ k) * sz.rows, sz.rows)
        for g in range(sz.lane_groups):
            halves = []
            for c in range(2):
                at = (c * sz.blocks + 2 * g) * sz.half
                even = piece[0, at : at + sz.half, :]
                odd = piece[0, at + sz.half : at + 2 * sz.half, :]
                low = low_half(even.shape)
                top = jnp.where(low, even, swap(odd))
                bottom = jnp.where(low, swap(even), odd)
                halves.append(jnp.concatenate([top, bottom], axis=0))
            planes[g, pl.ds(row, sz.rows), :] = jnp.concatenate(halves, axis=1)


def post_kernel(sz, running, row_scale, me_ref, *rest):
    pieces, rest = rest[: sz.group], rest[sz.group :]
    w_ref, rest = rest[0], rest[1:]
    if running == "add":
        sums_ref, start_ref, rest = rest[0], rest[1], rest[2:]
    elif running == "make":
        alpha_ref, beta_ref, tri_ref, rest = rest[0], rest[1], rest[2], rest[3:]
    planes = rest[-1]
    outs = rest[:-1]
    if running != "make":
        outs = outs[1:]
    out = outs[0]
    join_pieces(sz, me_ref[0], pieces, planes)
    w = w_ref[...]
    for g in range(sz.lane_groups):
        at = pl.ds(g * LANES, LANES)
        back = jnp.dot(planes[g], w, precision=HIGHEST, preferred_element_type=F32)
        halves = [back[:, :LANES], back[:, LANES:]]
        if running == "add":
            sums = [sums_ref[c, :, at] + start_ref[pl.ds(c, 1), at] for c in range(2)]
            halves = [halves[0] + row_scale * sums[1], halves[1] - row_scale * sums[0]]
        for c in range(2):
            out[c, 0, :, at] = halves[c]
        if running == "make":
            rate = jnp.where(pl.program_id(0) == 0, alpha_ref[:, at], beta_ref[:, at])
            part = jnp.concatenate([halves[0] * rate, halves[1] * rate], axis=1)
            total = jnp.dot(tri_ref[...], part, precision=HIGHEST, preferred_element_type=F32)

            @pl.when(pl.program_id(0) == 0)
            def _():
                for c in range(2):
                    outs[1][c, :, at] = total[:, c * LANES : (c + 1) * LANES]

            @pl.when(pl.program_id(0) != 0)
            def _():
                for c in range(2):
                    outs[1][c, :, at] += total[:, c * LANES : (c + 1) * LANES]


def post(sz, row_scale, me, pieces, fields, held, running=None, extra=()):
    count = len(fields)
    stride = fields[1] - fields[0] if count > 1 else 1
    first = fields[0]
    w = jnp.asarray(complex_lanes(span_matrix(-1) / NK))
    w_spec = pl.BlockSpec((2 * LANES, 2 * LANES), lambda i, me: (0, 0))
    in_specs = [pl.BlockSpec((1, sz.body, LANES), lambda i, me: (i, 0, 0))] * sz.group + [w_spec]
    row_spec = pl.BlockSpec((1, sz.slots), lambda i, me: (0, 0))
    sums_spec = pl.BlockSpec((2, sz.block_rows, sz.slots), lambda i, me: (0, 0, 0))
    if running == "add":
        in_specs += [sums_spec, pl.BlockSpec((2, sz.slots), lambda i, me: (0, 0))]
    elif running == "make":
        square = pl.BlockSpec((sz.block_rows, sz.block_rows), lambda i, me: (0, 0))
        in_specs += [row_spec, row_spec, square]
    out_specs = [
        pl.BlockSpec((2, 1, sz.block_rows, sz.slots), lambda i, me: (0, first + stride * i, 0, 0))
    ]
    out_shape = [jax.ShapeDtypeStruct((2, 5, sz.block_rows, sz.slots), F32)]
    aliases = {}
    operands = [me, *pieces, w, *extra]
    if running == "make":
        out_specs.append(sums_spec)
        out_shape.append(jax.ShapeDtypeStruct((2, sz.block_rows, sz.slots), F32))
    else:
        in_specs.append(pl.BlockSpec(memory_space=pl.ANY))
        operands.append(held)
        aliases = {len(operands) - 1: 0}
    return pl.pallas_call(
        functools.partial(post_kernel, sz, running, row_scale),
        grid_spec=pltpu.PrefetchScalarGridSpec(
            num_scalar_prefetch=1,
            grid=(count,),
            in_specs=in_specs,
            out_specs=out_specs,
            scratch_shapes=[pltpu.VMEM((sz.lane_groups, sz.block_rows, 2 * LANES), F32)],
        ),
        out_shape=out_shape,
        input_output_aliases=aliases,
        compiler_params=VMEM,
        name="post",
    )(*operands)


def exchange(pieces):
    group = lax.axis_size("mode")
    return [pieces[0]] + [
        lax.ppermute(pieces[k], "mode", [(i, i ^ k) for i in range(group)])
        for k in range(1, group)
    ]


def device_of(position):
    group, blocks = lax.axis_size("mode"), lax.axis_size(ROW_BLOCKS)
    return position % group * blocks + position // group


def chain(value, step):
    count = lax.axis_size(ALL_AXES)
    pairs = [
        (device_of(i), device_of(i + step)) for i in range(count) if 0 <= i + step < count
    ]
    return lax.ppermute(value, ALL_AXES, pairs)


def on_device(adjoint, forward, mode_map):
    sz = Sizes(adjoint.shape[2], adjoint.shape[3])
    stations = lax.axis_size("ckpt")
    row_scale = 1.0 / math.sqrt(sz.block_rows * lax.axis_size("wall") * stations)
    me = lax.axis_index("mode").astype(jnp.int32)
    me_arg = me.reshape(1)

    freq_index = lax.div(mode_map, jnp.int32(NK))
    span_index = lax.rem(mode_map, jnp.int32(NK))
    alpha = 2.0 / NF * ((freq_index + NF // 2) % NF - NF // 2).astype(F32)
    beta = 2.0 / NK * ((span_index + NK // 2) % NK - NK // 2).astype(F32)
    freqs = lax.all_gather(freq_index.reshape(sz.blocks, NK)[:, 0], "mode", axis=0)
    table = freqs[jnp.arange(sz.group, dtype=jnp.int32) ^ me].reshape(-1)

    blocks = lax.axis_size(ROW_BLOCKS)
    low = lax.ppermute(adjoint[:, :, -1:], ROW_BLOCKS, [(i, i + 1) for i in range(blocks - 1)])
    high = lax.ppermute(adjoint[:, :, :1], ROW_BLOCKS, [(i + 1, i) for i in range(blocks - 1)])
    rims = jnp.concatenate([low, high, jnp.zeros_like(adjoint[:, :, :6])], 2)

    here = lax.axis_index("ckpt")
    parts = forward.reshape(2, stations, sz.block_rows, sz.slots)
    both = lax.all_to_all(parts, "ckpt", split_axis=1, concat_axis=1, tiled=True)
    both = jnp.moveaxis(both, 1, 0)

    chunks = [(0, 2), (3, 4), (1,)]
    adjoint_pieces = [exchange(adjoint_prep(sz, me_arg, adjoint, rims, c)) for c in chunks]
    phys = forward_physical(sz, table, exchange(forward_prep(sz, me_arg, both)))

    current = []
    for index, fields in enumerate(chunks):
        stepped, first, last, total = station_one(sz, table, adjoint_pieces[index], phys, 1)
        if index == 0:
            pair = stepped
            freq_ids = np.arange(NF)
            rate = (2.0 / NF * ((freq_ids + NF // 2) % NF - NF // 2)).astype(np.float32)
            bmat = beta_matrix()
            mixed = np.block([[bmat.real, bmat.imag], [-bmat.imag, bmat.real]]).astype(np.float32)
            mine = jnp.asarray(rate)[:, None] * total[0] + jnp.dot(
                total[1], jnp.asarray(mixed), precision=HIGHEST
            )
            everyone = lax.all_gather(mine, ALL_AXES, axis=0)
            order = np.argsort([device_of(i) for i in range(lax.axis_size(ALL_AXES))])
            place = lax.axis_index(ROW_BLOCKS) * sz.group + me
            earlier = jnp.asarray(order, jnp.int32)[:, None, None] < place
            start = jnp.sum(jnp.where(earlier, everyone, 0.0), axis=0)
        if fields == (1,):
            stepped, first, last = add_running(sz, row_scale, stepped, pair, start)
        current.append((stepped, chain(last, 1), chain(first, -1)))

    back = [exchange(station_zero(sz, table, *c, phys, 0)) for c in current]

    tri = jnp.asarray(np.tril(np.ones((sz.block_rows, sz.block_rows), np.float32)))
    out, sums = post(
        sz, row_scale, me_arg, back[0], chunks[0], None, "make", (alpha[None], beta[None], tri)
    )
    totals = lax.all_gather(sums[:, -1], ROW_BLOCKS, axis=0)
    earlier = lax.broadcasted_iota(jnp.int32, totals.shape, 0) < lax.axis_index(ROW_BLOCKS)
    start = jnp.sum(jnp.where(earlier, totals, 0.0), axis=0)
    (out,) = post(sz, row_scale, me_arg, back[1], chunks[1], out)
    (out,) = post(sz, row_scale, me_arg, back[2], chunks[2], out, "add", (sums, start))
    return out


def solution(mesh):
    placed = (P(None, None, ROW_BLOCKS, "mode"), P("ckpt", None, "wall", "mode"), P("mode"))
    return jax.shard_map(
        on_device,
        mesh=mesh,
        in_specs=placed,
        out_specs=P(None, None, ROW_BLOCKS, "mode"),
        check_vma=False,
    )
```

time: 958 us -> 319 us (0.33); the launches traced: 946 us -> 318 us
  matrix products: 295 us -> 1.58 us
  local copies, waits for them, and re-layouts: 293 us -> 14.7 us
  blocking collectives: 254 us -> 32.5 us
  Pallas kernels: 0 us -> 87.5 us
  waiting for transfers between devices: 11.3 us -> 80.5 us
  starting transfers between devices: 24.4 us -> 82 us
  other arithmetic: 52.8 us -> 4.09 us
    dot_general x40 -> x1, matrix products: 295 us -> 1.58 us  [on_device(): jnp.dot(total[1], jnp.asarray(mixed), precision=HIGHEST)]
    all_gather x5 -> x1, blocking collectives: 142 us -> 15 us  [on_device(): totals = lax.all_gather(sums[:, -1], ROW_BLOCKS, axis=0)]
    pallas_call x0 -> x15, Pallas kernels: none -> 87.5 us  [the longest x3 21.6 us: post(): pl.pallas_call(functools.partial(post_kernel, sz, running, row_scale), gr...]
    ppermute x8 -> x57, waiting for transfers between devices: 10.6 us -> 80.5 us  [the longest x49 61.1 us: exchange(): lax.ppermute(pieces[k], 'mode', [(i, i ^ k) for i in range(group)])]
    all_to_all x1 -> x0, blocking collectives: 64.8 us -> none  [to_modes(): lax.all_to_all(values, 'mode', split_axis=3, concat_axis=2, tiled=True)]
    unnamed x73 -> x151, local copies, waits for them, and re-layouts: 71.3 us -> 7.66 us
    ppermute x8 -> x57, starting transfers between devices: 14.7 us -> 77.7 us  [the longest x49 61.2 us: exchange(): lax.ppermute(pieces[k], 'mode', [(i, i ^ k) for i in range(group)])]
    all_to_all x7 -> x0, local copies, waits for them, and re-layouts: 52.1 us -> none  [the longest x2 24.3 us: to_modes(): lax.all_to_all(values, 'mode', split_axis=3, concat_axis=2, tiled=True)]
  transfers between devices with their start and end apart: 11 -> 59, of which waited for: 2 -> 13; matrix products, arithmetic and copies ran while one was open for 21% -> 3% of each run, Pallas kernels for 0% -> 24%
where the time goes in v1:
time: 319 us; the launch traced here: 318 us
  Pallas kernels  87.5 us (27%)
  starting transfers between devices  82 us (26%)
  waiting for transfers between devices  80.5 us (25%)
  blocking collectives  32.5 us (10%)
  between operations  14.8 us (5%)
  local copies, waits for them, and re-layouts  14.7 us (5%)
  other arithmetic  4.09 us (1%)
    ppermute x49, starting transfers between devices, exchange(): lax.ppermute(pieces[k], 'mode', [(i, i ^ k) for i in range(group)])  61.2 us
    ppermute x49, waiting for transfers between devices, exchange(): lax.ppermute(pieces[k], 'mode', [(i, i ^ k) for i in range(group)])  61.1 us
    pallas_call x3, Pallas kernels, post(): pl.pallas_call(functools.partial(post_kernel, sz, running, row_scale), gr...  21.6 us
    pallas_call x3, Pallas kernels, station_one(): pl.pallas_call(functools.partial(station_one_kernel, sz), grid_spec=pltpu...  18.4 us
    pallas_call x3, Pallas kernels, station_zero(): pl.pallas_call(functools.partial(station_zero_kernel, sz), grid_spec=pltp...  18 us
    unnamed x1, blocking collectives  17.5 us
    ppermute x1, waiting for transfers between devices, on_device(): lax.ppermute(adjoint[:, :, -1:], ROW_BLOCKS, [(i, i + 1) for i in range(b...  16.6 us
    pallas_call x3, Pallas kernels, adjoint_prep(): pl.pallas_call(functools.partial(adjoint_prep_kernel, sz), grid_spec=pltp...  16.2 us
  transfers between devices with their start and end apart: 59, of which 13 were waited for; matrix products, arithmetic and copies ran while one was open for 3% of the time, Pallas kernels for 24%

profile of v1, /device:TPU:0, one launch (start us, length us, event | category | flops | bytes accessed | tf_op | source)
XLA Modules:
  0.0 317.6 jit_solution(7722233364478109056)
XLA Ops:
  6.5 3.1 copy.20
  9.6 4.3 %all-to-all-start = ((f32[2,2,256,512]{3,2,0,1:T(8,128)}), f32[2,2,256,512]{3,2,0,1:T(8,128)S(1)}, u32[]{:S(2)}, u32[]{:S(2)}) async-start(f32[2,2,256,512]{3,2,0,1:T(8,128)} %copy.20), calls=%async_computation | async-start | bytes 4194304 | tf_op jit(solution)/shard_map/all_to_all | solution.py:617
  14.9 4.5 %collective-permute-start = (f32[2,5,1,512]{3,2,1,0:T(1,128)S(1)}, f32[2,5,1,512]{3,2,1,0:T(1,128)S(1)}, u32[]{:S(2)}, u32[]{:S(2)}) collective-permute-start(f32[2,5,1,512]{3,2,1,0:T(1,128)S(1)} %get-tuple-element.143), channel_id=1, source_target_pairs={{0,1},{1,2},{2,3},{4,5},{5,6},{6,7},{8,9},{9,10},{10,11},{12,13},{... | collective-permute-start | bytes 61448 | tf_op jit(solution)/shard_map/ppermute | solution.py:611
  20.8 16.6 %collective-permute-done = f32[2,5,1,512]{3,2,1,0:T(1,128)S(1)} collective-permute-done((f32[2,5,1,512]{3,2,1,0:T(1,128)S(1)}, f32[2,5,1,512]{3,2,1,0:T(1,128)S(1)}, u32[]{:S(2)}, u32[]{:S(2)}) %collective-permute-start) | collective-permute-done | bytes 20512 | tf_op jit(solution)/shard_map/ppermute | solution.py:611
  37.3 2.9 collective-permute-done.1
  41.0 6.0 %adjoint_prep.4 = (f32[2,272,128]{2,1,0:T(8,128)}, f32[2,272,128]{2,1,0:T(8,128)}, f32[2,272,128]{2,1,0:T(8,128)}, f32[2,272,128]{2,1,0:T(8,128)}, f32[2,272,128...) custom-call(s32[1]{0:T(128)} %bitcast.me_ref, f32[2,5,256,512]{3,2,1,0:T(8,128)} %x_ref.5, ...), custom_call_target="tpu_custom_call" | custom-call | tf_op jit(solution)/shard_map/adjoint_prep/pallas_call | solution.py:157
  47.1 1.7 collective-permute-start.17
  50.1 5.0 %forward_prep.1 = (f32[2,256,128]{2,1,0:T(8,128)}, f32[2,256,128]{2,1,0:T(8,128)}, f32[2,256,128]{2,1,0:T(8,128)}, f32[2,256,128]{2,1,0:T(8,128)}, f32[2,256,128...) custom-call(s32[1]{0:T(128)} %bitcast.me_ref, ...), custom_call_target="tpu_custom_call" | custom-call | tf_op jit(solution)/shard_map/forward_prep/pallas_call | solution.py:196
  60.3 4.3 %collective-permute-done.10.rest_2_ = f32[2,256,128]{2,1,0:T(8,128)S(1)} collective-permute-done((f32[2,256,128]{2,1,0:T(8,128)}, f32[2,256,128]{2,1,0:T(8,128)S(1)}, u32[]{:S(2)}, u32[]{:S(2)}) %collective-permute-start.10) | collective-permute-done | bytes 262176 | tf_op jit(solution)/shard_map/ppermute | solution.py:578
  64.8 4.3 %collective-permute-done.11.rest_3_ = f32[2,256,128]{2,1,0:T(8,128)S(1)} collective-permute-done((f32[2,256,128]{2,1,0:T(8,128)}, f32[2,256,128]{2,1,0:T(8,128)S(1)}, u32[]{:S(2)}, u32[]{:S(2)}) %collective-permute-start.11) | collective-permute-done | bytes 262176 | tf_op jit(solution)/shard_map/ppermute | solution.py:578
  70.4 1.7 collective-permute-start.19
  72.1 10.3 %collective-permute-done.13.rest_5_ = f32[2,256,128]{2,1,0:T(8,128)S(1)} collective-permute-done((f32[2,256,128]{2,1,0:T(8,128)}, f32[2,256,128]{2,1,0:T(8,128)S(1)}, u32[]{:S(2)}, u32[]{:S(2)}) %collective-permute-start.13) | collective-permute-done | bytes 262176 | tf_op jit(solution)/shard_map/ppermute | solution.py:578
  82.4 2.1 collective-permute-start.20
  89.2 17.5 %all-reduce = s32[64]{0:T(128)S(1)} all-reduce(s32[64]{0:T(128)S(1)} %dynamic-update-slice), channel_id=2, replica_groups=mesh['mode'=8,'wall'=2,'ckpt'=2] {'mode'}, use_global_device_ids=true, to_apply=%add | all-reduce | flops 64 | bytes 512
  108.0 3.9 %forward_physical.1.rest_8_.phys = f32[2,2,64,16,128]{4,3,2,1,0:T(8,128)} custom-call(s32[64]{0:T(128)} %reshape.33.table_ref, f32[2,256,128]{2,1,0:T(8,128)} %get-tuple-element.82.rest_0_, f32[2,256,128]{2,1,0:T(8,128)} %copy-done.26, f32[2,256,128]{2,1,0:T(8,128)} %copy-done.27, f32[2,256,128]{2,1,0:T(8,128)} %copy-done.28, f32[2,256,128]{2,1,0:T(8,128)} %copy-done.29, ...), custom_call_target="tpu_custom_call" | custom-call | tf_op jit(solution)/shard_map/forward_physical/pallas_call | solution.py:260
  113.0 6.8 %station_one.4 = (f32[2,2,64,16,128]{4,3,2,1,0:T(8,128)}, f32[2,64,128]{2,1,0:T(8,128)}, f32[2,64,128]{2,1,0:T(8,128)}, f32[2,64,128]{2,1,0:T(8,128)}) custom-call(s32[64]{0:T(128)} %reshape.33.table_ref, f32[2,272,128]{2,1,0:T(8,128)} %get-tuple-element.91.rest_0_, f32[2,272,128]{2,1,0:T(8,128)} %copy-done.1, f32[2,272,128]{2,1,0:T(8,128)} %copy-done.2, ...), custom_call_target="tpu_custom_call" | custom-call | tf_op jit(solution)/shard_map/station_one/pallas_call | solution.py:347
  119.8 1.6 fusion.2
  121.4 6.0 %adjoint_prep.5 = (f32[2,272,128]{2,1,0:T(8,128)}, f32[2,272,128]{2,1,0:T(8,128)}, f32[2,272,128]{2,1,0:T(8,128)}, f32[2,272,128]{2,1,0:T(8,128)}, f32[2,272,128...) custom-call(s32[1]{0:T(128)} %bitcast.me_ref, f32[2,5,256,512]{3,2,1,0:T(8,128)} %x_ref.5, ...), custom_call_target="tpu_custom_call" | custom-call | tf_op jit(solution)/shard_map/adjoint_prep/pallas_call | solution.py:157
  132.6 4.9 %collective-permute-done.42.rest_2_ = f32[2,272,128]{2,1,0:T(8,128)S(1)} collective-permute-done((f32[2,272,128]{2,1,0:T(8,128)}, f32[2,272,128]{2,1,0:T(8,128)S(1)}, u32[]{:S(2)}, u32[]{:S(2)}) %collective-permute-start.42) | collective-permute-done | bytes 278560 | tf_op jit(solution)/shard_map/ppermute | solution.py:578
  137.8 4.1 %adjoint_prep.3 = (f32[1,272,128]{2,1,0:T(8,128)}, f32[1,272,128]{2,1,0:T(8,128)}, f32[1,272,128]{2,1,0:T(8,128)}, f32[1,272,128]{2,1,0:T(8,128)}, f32[1,272,128...) custom-call(s32[1]{0:T(128)} %bitcast.me_ref, f32[2,5,256,512]{3,2,1,0:T(8,128)} %x_ref.5, ...), custom_call_target="tpu_custom_call" | custom-call | tf_op jit(solution)/shard_map/adjoint_prep/pallas_call | solution.py:157
  143.6 12.5 %collective-permute-done.45.rest_5_ = f32[2,272,128]{2,1,0:T(8,128)S(1)} collective-permute-done((f32[2,272,128]{2,1,0:T(8,128)}, f32[2,272,128]{2,1,0:T(8,128)S(1)}, u32[]{:S(2)}, u32[]{:S(2)}) %collective-permute-start.45) | collective-permute-done | bytes 278560 | tf_op jit(solution)/shard_map/ppermute | solution.py:578
  157.2 6.8 %station_one.5 = (f32[2,2,64,16,128]{4,3,2,1,0:T(8,128)}, f32[2,64,128]{2,1,0:T(8,128)}, f32[2,64,128]{2,1,0:T(8,128)}, f32[2,64,128]{2,1,0:T(8,128)}) custom-call(s32[64]{0:T(128)} %reshape.33.table_ref, f32[2,272,128]{2,1,0:T(8,128)} %get-tuple-element.123.rest_0_, f32[2,272,128]{2,1,0:T(8,128)} %copy-done.8, f32[2,272,128]{2,1,0:T(8,128)} %copy-done.9, ...), custom_call_target="tpu_custom_call" | custom-call | tf_op jit(solution)/shard_map/station_one/pallas_call | solution.py:347
  164.0 3.0 collective-permute-start.48
  168.3 2.3 collective-permute-start.3
  171.6 6.7 %station_zero.5 = (f32[2,256,128]{2,1,0:T(8,128)}, f32[2,256,128]{2,1,0:T(8,128)}, f32[2,256,128]{2,1,0:T(8,128)}, f32[2,256,128]{2,1,0:T(8,128)}, f32[2,256,128...) custom-call(s32[64]{0:T(128)} %reshape.33.table_ref, ...), custom_call_target="tpu_custom_call" | custom-call | tf_op jit(solution)/shard_map/station_zero/pallas_call | solution.py:453
  178.3 3.0 collective-permute-start.50
  182.8 2.8 collective-permute-start.7
  186.0 7.8 %collective-permute-done.5.rest_4_ = f32[1,272,128]{2,1,0:T(8,128)S(1)} collective-permute-done((f32[1,272,128]{2,1,0:T(8,128)S(1)}, f32[1,272,128]{2,1,0:T(8,128)S(1)}, u32[]{:S(2)}, u32[]{:S(2)}) %collective-permute-start.5) | collective-permute-done | bytes 139296 | tf_op jit(solution)/shard_map/ppermute | solution.py:578
  196.7 5.0 %collective-permute-start.51 = (f32[2,256,128]{2,1,0:T(8,128)}, f32[2,256,128]{2,1,0:T(8,128)S(1)}, u32[]{:S(2)}, u32[]{:S(2)}) collective-permute-start(f32[2,256,128]{2,1,0:T(8,128)} %get-tuple-element.136), channel_id=1, source_target_pairs={{0,8},{4,12},{8,0},{12,4},{16,24},{20,28},{24,16},{28,20},{1,9},{5... | collective-permute-start | bytes 786440 | tf_op jit(solution)/shard_map/ppermute | solution.py:578
  205.1 1.6 collective-permute-start.55
  206.7 6.7 %station_zero.4 = (f32[2,256,128]{2,1,0:T(8,128)}, f32[2,256,128]{2,1,0:T(8,128)}, f32[2,256,128]{2,1,0:T(8,128)}, f32[2,256,128]{2,1,0:T(8,128)}, f32[2,256,128...) custom-call(s32[64]{0:T(128)} %reshape.33.table_ref, ...), custom_call_target="tpu_custom_call" | custom-call | tf_op jit(solution)/shard_map/station_zero/pallas_call | solution.py:453
  216.9 10.5 %collective-permute-done.54.rest_5_ = f32[2,256,128]{2,1,0:T(8,128)S(1)} collective-permute-done((f32[2,256,128]{2,1,0:T(8,128)}, f32[2,256,128]{2,1,0:T(8,128)S(1)}, u32[]{:S(2)}, u32[]{:S(2)}) %collective-permute-start.54) | collective-permute-done | bytes 262176 | tf_op jit(solution)/shard_map/ppermute | solution.py:578
  228.0 2.0 collective-permute-start.37
  230.0 4.8 %station_one.3 = (f32[1,2,64,16,128]{4,3,2,1,0:T(8,128)}, f32[1,64,128]{2,1,0:T(8,128)}, f32[1,64,128]{2,1,0:T(8,128)}, f32[1,64,128]{2,1,0:T(8,128)}) custom-call(s32[64]{0:T(128)} %reshape.33.table_ref, f32[1,272,128]{2,1,0:T(8,128)} %get-tuple-element.74.rest_0_, f32[1,272,128]{2,1,0:T(8,128)} %copy-done.36, f32[1,272,128]{2,1,0:T(8,128)} %copy-done.37, ...), custom_call_target="tpu_custom_call" | custom-call | tf_op jit(solution)/shard_map/station_one/pallas_call | solution.py:347
  234.8 2.0 select_reduce_fusion.start
  237.4 4.4 %add_running.1 = (f32[1,2,64,16,128]{4,3,2,1,0:T(8,128)}, f32[1,64,128]{2,1,0:T(8,128)}, f32[1,64,128]{2,1,0:T(8,128)}) custom-call(f32[1,2,64,16,128]{4,3,2,1,0:T(8,128)} %get-tuple-element.90.stepped, f32[2,2,64,16,128]{4,3,2,1,0:T(8,128)} %get-tuple-element.99.zero.two.current, f32[2,2,64,16,128]{4,3,2,1,0:T(8,128)} %get-tuple-element.99.zero.two.current, ...), custom_call_target="tpu_custom_call" | custom-call | tf_op jit(solution)/shard_map/add_running/pallas_call | solution.py:400
  241.9 2.4 collective-permute-start.23
  245.6 1.7 collective-permute-start.38
  247.3 1.7 collective-permute-start.39
  249.0 5.5 %collective-permute-start.40 = (f32[2,256,128]{2,1,0:T(8,128)S(1)}, f32[2,256,128]{2,1,0:T(8,128)S(1)}, u32[]{:S(2)}, u32[]{:S(2)}) collective-permute-start(f32[2,256,128]{2,1,0:T(8,128)S(1)} %copy-done.61), channel_id=1, source_target_pairs={{0,28},{4,24},{8,20},{12,16},{16,12},{20,8},{24,4},{28,0},{1,29},{... | collective-permute-start | bytes 786440 | tf_op jit(solution)/shard_map/ppermute | solution.py:578
  254.5 4.7 %station_zero.3 = (f32[1,256,128]{2,1,0:T(8,128)}, f32[1,256,128]{2,1,0:T(8,128)}, f32[1,256,128]{2,1,0:T(8,128)}, f32[1,256,128]{2,1,0:T(8,128)}, f32[1,256,128...) custom-call(s32[64]{0:T(128)} %reshape.33.table_ref, ...), custom_call_target="tpu_custom_call" | custom-call | tf_op jit(solution)/shard_map/station_zero/pallas_call | solution.py:453
  260.0 4.7 %collective-permute-done.38.rest_5_ = f32[2,256,128]{2,1,0:T(8,128)S(1)} collective-permute-done((f32[2,256,128]{2,1,0:T(8,128)S(1)}, f32[2,256,128]{2,1,0:T(8,128)S(1)}, u32[]{:S(2)}, u32[]{:S(2)}) %collective-permute-start.38) | collective-permute-done | bytes 262176 | tf_op jit(solution)/shard_map/ppermute | solution.py:578
  264.7 2.5 collective-permute-start.27
  267.3 1.7 collective-permute-start.28
  271.7 12.4 %post.3 = (f32[2,5,256,512]{3,2,1,0:T(8,128)}, f32[2,256,512]{2,1,0:T(8,128)}) custom-call(s32[1]{0:T(128)} %bitcast.me_ref, f32[2,256,128]{2,1,0:T(8,128)} %get-tuple-element.114.rest_0_, f32[2,256,128]{2,1,0:T(8,128)} %copy-done.22, f32[2,256,128]{2,1,0:T(8,128)} %copy-done.23, f32[2,256,128]{2,1,0:T(8,128)} %copy-done.24, f32[2,256,128]{2,1,0:T(8,128)} %copy-done.25, ...), custom_call_target="tpu_custom_call" | custom-call | tf_op jit(solution)/shard_map/post/pallas_call | solution.py:559
  284.9 15.0 %all-gather.2 = f32[8,1,512]{2,1,0:T(1,128)S(1)} all-gather(f32[2,1,512]{2,1,0:T(1,128)S(1)} %slice.23), channel_id=4, replica_groups=mesh['mode'=8,'wall'=2,'ckpt'=2] {'wall','ckpt'}, dimensions={0}, use_global_device_ids=true | all-gather | bytes 20480 | tf_op jit(solution)/shard_map/all_gather | solution.py:651
  300.0 5.2 %post.4.rest_11_ = f32[2,5,256,512]{3,2,1,0:T(8,128)} custom-call(s32[1]{0:T(128)} %bitcast.me_ref, f32[2,256,128]{2,1,0:T(8,128)} %get-tuple-element.134.rest_0_, f32[2,256,128]{2,1,0:T(8,128)} %copy-done.15, f32[2,256,128]{2,1,0:T(8,128)} %copy-done.16, f32[2,256,128]{2,1,0:T(8,128)} %copy-done.17, ...), custom_call_target="tpu_custom_call", output_to_operand_aliasing={{}: (10, {})} | custom-call | tf_op jit(solution)/shard_map/post/pallas_call | solution.py:559
  306.8 4.0 %post.5 = f32[2,5,256,512]{3,2,1,0:T(8,128)} custom-call(s32[1]{0:T(128)} %bitcast.me_ref, f32[1,256,128]{2,1,0:T(8,128)} %get-tuple-element.104.rest_0_, f32[1,256,128]{2,1,0:T(8,128)} %copy-done.43, f32[1,256,128]{2,1,0:T(8,128)} %copy-done.44, f32[1,256,128]{2,1,0:T(8,128)} %copy-done.45, ...), custom_call_target="tpu_custom_call", output_to_operand_aliasing={{}: (12, {})} | custom-call | tf_op jit(solution)/shard_map/post/pallas_call | solution.py:559
  (262 shorter events, 48.0 us)
Async XLA Ops:
  9.6 39.2 %all-to-all-start = ((f32[2,2,256,512]{3,2,0,1:T(8,128)}), f32[2,2,256,512]{3,2,0,1:T(8,128)S(1)}, u32[]{:S(2)}, u32[]{:S(2)}) async-start(f32[2,2,256,512]{3,2,0,1:T(8,128)} %copy.20), calls=%async_computation | async-start | bytes 4194304 | tf_op jit(solution)/shard_map/all_to_all | solution.py:617
  13.9 220.9 %all-gather.5.cloned.1.call-start = ((), (), s32[]{:S(2)}) async-start(), calls=%async_computation.1 | async-start | bytes 1081344 | tf_op jit(solution)/shard_map/all_gather | solution.py:636
  14.9 22.4 %collective-permute-start = (f32[2,5,1,512]{3,2,1,0:T(1,128)S(1)}, f32[2,5,1,512]{3,2,1,0:T(1,128)S(1)}, u32[]{:S(2)}, u32[]{:S(2)}) collective-permute-start(f32[2,5,1,512]{3,2,1,0:T(1,128)S(1)} %get-tuple-element.143), channel_id=1, source_target_pairs={{0,1},{1,2},{2,3},{4,5},{5,6},{6,7},{8,9},{9,10},{10,11},{12,13},{... | collective-permute-start | bytes 61448 | tf_op jit(solution)/shard_map/ppermute | solution.py:611
  19.4 20.8 %collective-permute-start.1 = (f32[2,5,1,512]{3,2,1,0:T(1,128)S(1)}, f32[2,5,1,512]{3,2,1,0:T(1,128)S(1)}, u32[]{:S(2)}, u32[]{:S(2)}) collective-permute-start(f32[2,5,1,512]{3,2,1,0:T(1,128)S(1)} %get-tuple-element.144), channel_id=1, source_target_pairs={{1,0},{2,1},{3,2},{5,4},{6,5},{7,6},{9,8},{10,9},{11,10},{13,12},{... | collective-permute-start | bytes 61448 | tf_op jit(solution)/shard_map/ppermute | solution.py:612
  47.1 11.4 %collective-permute-start.17 = (f32[2,272,128]{2,1,0:T(8,128)}, f32[2,272,128]{2,1,0:T(8,128)S(1)}, u32[]{:S(2)}, u32[]{:S(2)}) collective-permute-start(f32[2,272,128]{2,1,0:T(8,128)} %get-tuple-element.93), channel_id=1, source_target_pairs={{0,8},{4,12},{8,0},{12,4},{16,24},{20,28},{24,16},{28,20},{1,9},{5... | collective-permute-start | bytes 835592 | tf_op jit(solution)/shard_map/ppermute | solution.py:578
  55.7 13.4 %collective-permute-start.11 = (f32[2,256,128]{2,1,0:T(8,128)}, f32[2,256,128]{2,1,0:T(8,128)S(1)}, u32[]{:S(2)}, u32[]{:S(2)}) collective-permute-start(f32[2,256,128]{2,1,0:T(8,128)} %get-tuple-element.85), channel_id=1, source_target_pairs={{0,12},{4,8},{8,4},{12,0},{16,28},{20,24},{24,20},{28,16},{1,13},{... | collective-permute-start | bytes 786440 | tf_op jit(solution)/shard_map/ppermute | solution.py:578
  57.0 13.3 %collective-permute-start.12 = (f32[2,256,128]{2,1,0:T(8,128)}, f32[2,256,128]{2,1,0:T(8,128)S(1)}, u32[]{:S(2)}, u32[]{:S(2)}) collective-permute-start(f32[2,256,128]{2,1,0:T(8,128)} %get-tuple-element.86), channel_id=1, source_target_pairs={{0,16},{4,20},{8,24},{12,28},{16,0},{20,4},{24,8},{28,12},{1,17},{... | collective-permute-start | bytes 786440 | tf_op jit(solution)/shard_map/ppermute | solution.py:578
  58.6 23.8 %collective-permute-start.13 = (f32[2,256,128]{2,1,0:T(8,128)}, f32[2,256,128]{2,1,0:T(8,128)S(1)}, u32[]{:S(2)}, u32[]{:S(2)}) collective-permute-start(f32[2,256,128]{2,1,0:T(8,128)} %get-tuple-element.87), channel_id=1, source_target_pairs={{0,20},{4,16},{8,28},{12,24},{16,4},{20,0},{24,12},{28,8},{1,21},{... | collective-permute-start | bytes 786440 | tf_op jit(solution)/shard_map/ppermute | solution.py:578
  58.8 25.6 %collective-permute-start.14 = (f32[2,256,128]{2,1,0:T(8,128)}, f32[2,256,128]{2,1,0:T(8,128)S(1)}, u32[]{:S(2)}, u32[]{:S(2)}) collective-permute-start(f32[2,256,128]{2,1,0:T(8,128)} %get-tuple-element.88), channel_id=1, source_target_pairs={{0,24},{4,28},{8,16},{12,20},{16,8},{20,12},{24,0},{28,4},{1,25},{... | collective-permute-start | bytes 786440 | tf_op jit(solution)/shard_map/ppermute | solution.py:578
  64.7 20.9 %collective-permute-start.15 = (f32[2,256,128]{2,1,0:T(8,128)}, f32[2,256,128]{2,1,0:T(8,128)S(1)}, u32[]{:S(2)}, u32[]{:S(2)}) collective-permute-start(f32[2,256,128]{2,1,0:T(8,128)} %get-tuple-element.89), channel_id=1, source_target_pairs={{0,28},{4,24},{8,20},{12,16},{16,12},{20,8},{24,4},{28,0},{1,29},{... | collective-permute-start | bytes 786440 | tf_op jit(solution)/shard_map/ppermute | solution.py:578
  69.1 42.7 %collective-permute-start.18 = (f32[2,272,128]{2,1,0:T(8,128)}, f32[2,272,128]{2,1,0:T(8,128)S(1)}, u32[]{:S(2)}, u32[]{:S(2)}) collective-permute-start(f32[2,272,128]{2,1,0:T(8,128)} %get-tuple-element.94), channel_id=1, source_target_pairs={{0,12},{4,8},{8,4},{12,0},{16,28},{20,24},{24,20},{28,16},{1,13},{... | collective-permute-start | bytes 835592 | tf_op jit(solution)/shard_map/ppermute | solution.py:578
  70.4 41.5 %collective-permute-start.19 = (f32[2,272,128]{2,1,0:T(8,128)}, f32[2,272,128]{2,1,0:T(8,128)S(1)}, u32[]{:S(2)}, u32[]{:S(2)}) collective-permute-start(f32[2,272,128]{2,1,0:T(8,128)} %get-tuple-element.95), channel_id=1, source_target_pairs={{0,16},{4,20},{8,24},{12,28},{16,0},{20,4},{24,8},{28,12},{1,17},{... | collective-permute-start | bytes 835592 | tf_op jit(solution)/shard_map/ppermute | solution.py:578
  82.4 29.6 %collective-permute-start.20 = (f32[2,272,128]{2,1,0:T(8,128)}, f32[2,272,128]{2,1,0:T(8,128)S(1)}, u32[]{:S(2)}, u32[]{:S(2)}) collective-permute-start(f32[2,272,128]{2,1,0:T(8,128)} %get-tuple-element.96), channel_id=1, source_target_pairs={{0,20},{4,16},{8,28},{12,24},{16,4},{20,0},{24,12},{28,8},{1,21},{... | collective-permute-start | bytes 835592 | tf_op jit(solution)/shard_map/ppermute | solution.py:578
  85.2 26.8 %collective-permute-start.21 = (f32[2,272,128]{2,1,0:T(8,128)}, f32[2,272,128]{2,1,0:T(8,128)S(1)}, u32[]{:S(2)}, u32[]{:S(2)}) collective-permute-start(f32[2,272,128]{2,1,0:T(8,128)} %get-tuple-element.97), channel_id=1, source_target_pairs={{0,24},{4,28},{8,16},{12,20},{16,8},{20,12},{24,0},{28,4},{1,25},{... | collective-permute-start | bytes 835592 | tf_op jit(solution)/shard_map/ppermute | solution.py:578
  86.2 25.7 %collective-permute-start.22 = (f32[2,272,128]{2,1,0:T(8,128)S(1)}, f32[2,272,128]{2,1,0:T(8,128)S(1)}, u32[]{:S(2)}, u32[]{:S(2)}) collective-permute-start(f32[2,272,128]{2,1,0:T(8,128)S(1)} %copy-done.59), channel_id=1, source_target_pairs={{0,28},{4,24},{8,20},{12,16},{16,12},{20,8},{24,4},{28,0},{1,29},{... | collective-permute-start | bytes 835592 | tf_op jit(solution)/shard_map/ppermute | solution.py:578
  128.0 14.6 %collective-permute-start.43 = (f32[2,272,128]{2,1,0:T(8,128)}, f32[2,272,128]{2,1,0:T(8,128)S(1)}, u32[]{:S(2)}, u32[]{:S(2)}) collective-permute-start(f32[2,272,128]{2,1,0:T(8,128)} %get-tuple-element.126), channel_id=1, source_target_pairs={{0,12},{4,8},{8,4},{12,0},{16,28},{20,24},{24,20},{28,16},{1,13},{... | collective-permute-start | bytes 835592 | tf_op jit(solution)/shard_map/ppermute | solution.py:578
  129.4 14.2 %collective-permute-start.44 = (f32[2,272,128]{2,1,0:T(8,128)}, f32[2,272,128]{2,1,0:T(8,128)S(1)}, u32[]{:S(2)}, u32[]{:S(2)}) collective-permute-start(f32[2,272,128]{2,1,0:T(8,128)} %get-tuple-element.127), channel_id=1, source_target_pairs={{0,16},{4,20},{8,24},{12,28},{16,0},{20,4},{24,8},{28,12},{1,17},{... | collective-permute-start | bytes 835592 | tf_op jit(solution)/shard_map/ppermute | solution.py:578
  131.0 25.1 %collective-permute-start.45 = (f32[2,272,128]{2,1,0:T(8,128)}, f32[2,272,128]{2,1,0:T(8,128)S(1)}, u32[]{:S(2)}, u32[]{:S(2)}) collective-permute-start(f32[2,272,128]{2,1,0:T(8,128)} %get-tuple-element.128), channel_id=1, source_target_pairs={{0,20},{4,16},{8,28},{12,24},{16,4},{20,0},{24,12},{28,8},{1,21},{... | collective-permute-start | bytes 835592 | tf_op jit(solution)/shard_map/ppermute | solution.py:578
  131.1 25.0 %collective-permute-start.46 = (f32[2,272,128]{2,1,0:T(8,128)}, f32[2,272,128]{2,1,0:T(8,128)S(1)}, u32[]{:S(2)}, u32[]{:S(2)}) collective-permute-start(f32[2,272,128]{2,1,0:T(8,128)} %get-tuple-element.129), channel_id=1, source_target_pairs={{0,24},{4,28},{8,16},{12,20},{16,8},{20,12},{24,0},{28,4},{1,25},{... | collective-permute-start | bytes 835592 | tf_op jit(solution)/shard_map/ppermute | solution.py:578
  137.5 18.9 %collective-permute-start.47 = (f32[2,272,128]{2,1,0:T(8,128)}, f32[2,272,128]{2,1,0:T(8,128)S(1)}, u32[]{:S(2)}, u32[]{:S(2)}) collective-permute-start(f32[2,272,128]{2,1,0:T(8,128)} %get-tuple-element.130), channel_id=1, source_target_pairs={{0,28},{4,24},{8,20},{12,16},{16,12},{20,8},{24,4},{28,0},{1,29},{... | collective-permute-start | bytes 835592 | tf_op jit(solution)/shard_map/ppermute | solution.py:578
  142.6 39.7 %collective-permute-start.2 = (f32[1,272,128]{2,1,0:T(8,128)}, f32[1,272,128]{2,1,0:T(8,128)S(1)}, u32[]{:S(2)}, u32[]{:S(2)}) collective-permute-start(f32[1,272,128]{2,1,0:T(8,128)} %get-tuple-element.75), channel_id=1, source_target_pairs={{0,4},{4,0},{8,12},{12,8},{16,20},{20,16},{24,28},{28,24},{1,5},{5... | collective-permute-start | bytes 417800 | tf_op jit(solution)/shard_map/ppermute | solution.py:578
  168.3 14.5 %collective-permute-start.3 = (f32[1,272,128]{2,1,0:T(8,128)S(1)}, f32[1,272,128]{2,1,0:T(8,128)S(1)}, u32[]{:S(2)}, u32[]{:S(2)}) collective-permute-start(f32[1,272,128]{2,1,0:T(8,128)S(1)} %copy-done.69), channel_id=1, source_target_pairs={{0,8},{4,12},{8,0},{12,4},{16,24},{20,28},{24,16},{28,20},{1,9},{5... | collective-permute-start | bytes 417800 | tf_op jit(solution)/shard_map/ppermute | solution.py:578
  170.7 15.0 %collective-permute-start.4 = (f32[1,272,128]{2,1,0:T(8,128)S(1)}, f32[1,272,128]{2,1,0:T(8,128)S(1)}, u32[]{:S(2)}, u32[]{:S(2)}) collective-permute-start(f32[1,272,128]{2,1,0:T(8,128)S(1)} %copy-done.68), channel_id=1, source_target_pairs={{0,12},{4,8},{8,4},{12,0},{16,28},{20,24},{24,20},{28,16},{1,13},{... | collective-permute-start | bytes 417800 | tf_op jit(solution)/shard_map/ppermute | solution.py:578
  178.3 26.8 %collective-permute-start.50 = (f32[2,256,128]{2,1,0:T(8,128)}, f32[2,256,128]{2,1,0:T(8,128)S(1)}, u32[]{:S(2)}, u32[]{:S(2)}) collective-permute-start(f32[2,256,128]{2,1,0:T(8,128)} %get-tuple-element.135), channel_id=1, source_target_pairs={{0,4},{4,0},{8,12},{12,8},{16,20},{20,16},{24,28},{28,24},{1,5},{5... | collective-permute-start | bytes 786440 | tf_op jit(solution)/shard_map/ppermute | solution.py:578
  181.3 12.5 %collective-permute-start.5 = (f32[1,272,128]{2,1,0:T(8,128)S(1)}, f32[1,272,128]{2,1,0:T(8,128)S(1)}, u32[]{:S(2)}, u32[]{:S(2)}) collective-permute-start(f32[1,272,128]{2,1,0:T(8,128)S(1)} %copy-done.67), channel_id=1, source_target_pairs={{0,16},{4,20},{8,24},{12,28},{16,0},{20,4},{24,8},{28,12},{1,17},{... | collective-permute-start | bytes 417800 | tf_op jit(solution)/shard_map/ppermute | solution.py:578
  182.3 12.8 %collective-permute-start.6 = (f32[1,272,128]{2,1,0:T(8,128)S(1)}, f32[1,272,128]{2,1,0:T(8,128)S(1)}, u32[]{:S(2)}, u32[]{:S(2)}) collective-permute-start(f32[1,272,128]{2,1,0:T(8,128)S(1)} %copy-done.66), channel_id=1, source_target_pairs={{0,20},{4,16},{8,28},{12,24},{16,4},{20,0},{24,12},{28,8},{1,21},{... | collective-permute-start | bytes 417800 | tf_op jit(solution)/shard_map/ppermute | solution.py:578
  182.8 13.8 %collective-permute-start.7 = (f32[1,272,128]{2,1,0:T(8,128)S(1)}, f32[1,272,128]{2,1,0:T(8,128)S(1)}, u32[]{:S(2)}, u32[]{:S(2)}) collective-permute-start(f32[1,272,128]{2,1,0:T(8,128)S(1)} %copy-done.65), channel_id=1, source_target_pairs={{0,24},{4,28},{8,16},{12,20},{16,8},{20,12},{24,0},{28,4},{1,25},{... | collective-permute-start | bytes 417800 | tf_op jit(solution)/shard_map/ppermute | solution.py:578
  185.6 16.1 %collective-permute-start.8 = (f32[1,272,128]{2,1,0:T(8,128)S(1)}, f32[1,272,128]{2,1,0:T(8,128)S(1)}, u32[]{:S(2)}, u32[]{:S(2)}) collective-permute-start(f32[1,272,128]{2,1,0:T(8,128)S(1)} %copy-done.64), channel_id=1, source_target_pairs={{0,28},{4,24},{8,20},{12,16},{16,12},{20,8},{24,4},{28,0},{1,29},{... | collective-permute-start | bytes 417800 | tf_op jit(solution)/shard_map/ppermute | solution.py:578
  196.7 16.7 %collective-permute-start.51 = (f32[2,256,128]{2,1,0:T(8,128)}, f32[2,256,128]{2,1,0:T(8,128)S(1)}, u32[]{:S(2)}, u32[]{:S(2)}) collective-permute-start(f32[2,256,128]{2,1,0:T(8,128)} %get-tuple-element.136), channel_id=1, source_target_pairs={{0,8},{4,12},{8,0},{12,4},{16,24},{20,28},{24,16},{28,20},{1,9},{5... | collective-permute-start | bytes 786440 | tf_op jit(solution)/shard_map/ppermute | solution.py:578
  202.4 12.0 %collective-permute-start.52 = (f32[2,256,128]{2,1,0:T(8,128)}, f32[2,256,128]{2,1,0:T(8,128)S(1)}, u32[]{:S(2)}, u32[]{:S(2)}) collective-permute-start(f32[2,256,128]{2,1,0:T(8,128)} %get-tuple-element.137), channel_id=1, source_target_pairs={{0,12},{4,8},{8,4},{12,0},{16,28},{20,24},{24,20},{28,16},{1,13},{... | collective-permute-start | bytes 786440 | tf_op jit(solution)/shard_map/ppermute | solution.py:578
  202.4 13.3 %collective-permute-start.53 = (f32[2,256,128]{2,1,0:T(8,128)}, f32[2,256,128]{2,1,0:T(8,128)S(1)}, u32[]{:S(2)}, u32[]{:S(2)}) collective-permute-start(f32[2,256,128]{2,1,0:T(8,128)} %get-tuple-element.138), channel_id=1, source_target_pairs={{0,16},{4,20},{8,24},{12,28},{16,0},{20,4},{24,8},{28,12},{1,17},{... | collective-permute-start | bytes 786440 | tf_op jit(solution)/shard_map/ppermute | solution.py:578
  203.8 23.6 %collective-permute-start.54 = (f32[2,256,128]{2,1,0:T(8,128)}, f32[2,256,128]{2,1,0:T(8,128)S(1)}, u32[]{:S(2)}, u32[]{:S(2)}) collective-permute-start(f32[2,256,128]{2,1,0:T(8,128)} %get-tuple-element.139), channel_id=1, source_target_pairs={{0,20},{4,16},{8,28},{12,24},{16,4},{20,0},{24,12},{28,8},{1,21},{... | collective-permute-start | bytes 786440 | tf_op jit(solution)/shard_map/ppermute | solution.py:578
  205.1 22.9 %collective-permute-start.55 = (f32[2,256,128]{2,1,0:T(8,128)}, f32[2,256,128]{2,1,0:T(8,128)S(1)}, u32[]{:S(2)}, u32[]{:S(2)}) collective-permute-start(f32[2,256,128]{2,1,0:T(8,128)} %get-tuple-element.140), channel_id=1, source_target_pairs={{0,24},{4,28},{8,16},{12,20},{16,8},{20,12},{24,0},{28,4},{1,25},{... | collective-permute-start | bytes 786440 | tf_op jit(solution)/shard_map/ppermute | solution.py:578
  213.4 28.5 %collective-permute-start.56 = (f32[2,256,128]{2,1,0:T(8,128)S(1)}, f32[2,256,128]{2,1,0:T(8,128)S(1)}, u32[]{:S(2)}, u32[]{:S(2)}) collective-permute-start(f32[2,256,128]{2,1,0:T(8,128)S(1)} %copy-done.60), channel_id=1, source_target_pairs={{0,28},{4,24},{8,20},{12,16},{16,12},{20,8},{24,4},{28,0},{1,29},{... | collective-permute-start | bytes 786440 | tf_op jit(solution)/shard_map/ppermute | solution.py:578
  214.4 29.9 %collective-permute-start.34 = (f32[2,256,128]{2,1,0:T(8,128)}, f32[2,256,128]{2,1,0:T(8,128)S(1)}, u32[]{:S(2)}, u32[]{:S(2)}) collective-permute-start(f32[2,256,128]{2,1,0:T(8,128)} %get-tuple-element.115), channel_id=1, source_target_pairs={{0,4},{4,0},{8,12},{12,8},{16,20},{20,16},{24,28},{28,24},{1,5},{5... | collective-permute-start | bytes 786440 | tf_op jit(solution)/shard_map/ppermute | solution.py:578
  215.7 29.9 %collective-permute-start.35 = (f32[2,256,128]{2,1,0:T(8,128)}, f32[2,256,128]{2,1,0:T(8,128)S(1)}, u32[]{:S(2)}, u32[]{:S(2)}) collective-permute-start(f32[2,256,128]{2,1,0:T(8,128)} %get-tuple-element.116), channel_id=1, source_target_pairs={{0,8},{4,12},{8,0},{12,4},{16,24},{20,28},{24,16},{28,20},{1,9},{5... | collective-permute-start | bytes 786440 | tf_op jit(solution)/shard_map/ppermute | solution.py:578
  227.4 31.8 %collective-permute-start.36 = (f32[2,256,128]{2,1,0:T(8,128)}, f32[2,256,128]{2,1,0:T(8,128)S(1)}, u32[]{:S(2)}, u32[]{:S(2)}) collective-permute-start(f32[2,256,128]{2,1,0:T(8,128)} %get-tuple-element.117), channel_id=1, source_target_pairs={{0,12},{4,8},{8,4},{12,0},{16,28},{20,24},{24,20},{28,16},{1,13},{... | collective-permute-start | bytes 786440 | tf_op jit(solution)/shard_map/ppermute | solution.py:578
  228.0 31.3 %collective-permute-start.37 = (f32[2,256,128]{2,1,0:T(8,128)}, f32[2,256,128]{2,1,0:T(8,128)S(1)}, u32[]{:S(2)}, u32[]{:S(2)}) collective-permute-start(f32[2,256,128]{2,1,0:T(8,128)} %get-tuple-element.118), channel_id=1, source_target_pairs={{0,16},{4,20},{8,24},{12,28},{16,0},{20,4},{24,8},{28,12},{1,17},{... | collective-permute-start | bytes 786440 | tf_op jit(solution)/shard_map/ppermute | solution.py:578
  245.6 19.1 %collective-permute-start.38 = (f32[2,256,128]{2,1,0:T(8,128)S(1)}, f32[2,256,128]{2,1,0:T(8,128)S(1)}, u32[]{:S(2)}, u32[]{:S(2)}) collective-permute-start(f32[2,256,128]{2,1,0:T(8,128)S(1)} %copy-done.63), channel_id=1, source_target_pairs={{0,20},{4,16},{8,28},{12,24},{16,4},{20,0},{24,12},{28,8},{1,21},{... | collective-permute-start | bytes 786440 | tf_op jit(solution)/shard_map/ppermute | solution.py:578
  247.3 19.9 %collective-permute-start.39 = (f32[2,256,128]{2,1,0:T(8,128)S(1)}, f32[2,256,128]{2,1,0:T(8,128)S(1)}, u32[]{:S(2)}, u32[]{:S(2)}) collective-permute-start(f32[2,256,128]{2,1,0:T(8,128)S(1)} %copy-done.62), channel_id=1, source_target_pairs={{0,24},{4,28},{8,16},{12,20},{16,8},{20,12},{24,0},{28,4},{1,25},{... | collective-permute-start | bytes 786440 | tf_op jit(solution)/shard_map/ppermute | solution.py:578
  249.0 20.0 %collective-permute-start.40 = (f32[2,256,128]{2,1,0:T(8,128)S(1)}, f32[2,256,128]{2,1,0:T(8,128)S(1)}, u32[]{:S(2)}, u32[]{:S(2)}) collective-permute-start(f32[2,256,128]{2,1,0:T(8,128)S(1)} %copy-done.61), channel_id=1, source_target_pairs={{0,28},{4,24},{8,20},{12,16},{16,12},{20,8},{24,4},{28,0},{1,29},{... | collective-permute-start | bytes 786440 | tf_op jit(solution)/shard_map/ppermute | solution.py:578
  259.2 10.5 %collective-permute-start.25 = (f32[1,256,128]{2,1,0:T(8,128)}, f32[1,256,128]{2,1,0:T(8,128)S(1)}, u32[]{:S(2)}, u32[]{:S(2)}) collective-permute-start(f32[1,256,128]{2,1,0:T(8,128)} %get-tuple-element.105), channel_id=1, source_target_pairs={{0,4},{4,0},{8,12},{12,8},{16,20},{20,16},{24,28},{28,24},{1,5},{5... | collective-permute-start | bytes 393224 | tf_op jit(solution)/shard_map/ppermute | solution.py:578
  259.3 11.4 %collective-permute-start.26 = (f32[1,256,128]{2,1,0:T(8,128)}, f32[1,256,128]{2,1,0:T(8,128)S(1)}, u32[]{:S(2)}, u32[]{:S(2)}) collective-permute-start(f32[1,256,128]{2,1,0:T(8,128)} %get-tuple-element.106), channel_id=1, source_target_pairs={{0,8},{4,12},{8,0},{12,4},{16,24},{20,28},{24,16},{28,20},{1,9},{5... | collective-permute-start | bytes 393224 | tf_op jit(solution)/shard_map/ppermute | solution.py:578
  264.7 41.2 %collective-permute-start.27 = (f32[1,256,128]{2,1,0:T(8,128)}, f32[1,256,128]{2,1,0:T(8,128)S(1)}, u32[]{:S(2)}, u32[]{:S(2)}) collective-permute-start(f32[1,256,128]{2,1,0:T(8,128)} %get-tuple-element.107), channel_id=1, source_target_pairs={{0,12},{4,8},{8,4},{12,0},{16,28},{20,24},{24,20},{28,16},{1,13},{... | collective-permute-start | bytes 393224 | tf_op jit(solution)/shard_map/ppermute | solution.py:578
  267.3 38.6 %collective-permute-start.28 = (f32[1,256,128]{2,1,0:T(8,128)}, f32[1,256,128]{2,1,0:T(8,128)S(1)}, u32[]{:S(2)}, u32[]{:S(2)}) collective-permute-start(f32[1,256,128]{2,1,0:T(8,128)} %get-tuple-element.108), channel_id=1, source_target_pairs={{0,16},{4,20},{8,24},{12,28},{16,0},{20,4},{24,8},{28,12},{1,17},{... | collective-permute-start | bytes 393224 | tf_op jit(solution)/shard_map/ppermute | solution.py:578
  269.0 36.9 %collective-permute-start.29 = (f32[1,256,128]{2,1,0:T(8,128)}, f32[1,256,128]{2,1,0:T(8,128)S(1)}, u32[]{:S(2)}, u32[]{:S(2)}) collective-permute-start(f32[1,256,128]{2,1,0:T(8,128)} %get-tuple-element.109), channel_id=1, source_target_pairs={{0,20},{4,16},{8,28},{12,24},{16,4},{20,0},{24,12},{28,8},{1,21},{... | collective-permute-start | bytes 393224 | tf_op jit(solution)/shard_map/ppermute | solution.py:578
  269.7 36.2 %collective-permute-start.30 = (f32[1,256,128]{2,1,0:T(8,128)}, f32[1,256,128]{2,1,0:T(8,128)S(1)}, u32[]{:S(2)}, u32[]{:S(2)}) collective-permute-start(f32[1,256,128]{2,1,0:T(8,128)} %get-tuple-element.110), channel_id=1, source_target_pairs={{0,24},{4,28},{8,16},{12,20},{16,8},{20,12},{24,0},{28,4},{1,25},{... | collective-permute-start | bytes 393224 | tf_op jit(solution)/shard_map/ppermute | solution.py:578
  270.7 35.2 %collective-permute-start.31 = (f32[1,256,128]{2,1,0:T(8,128)}, f32[1,256,128]{2,1,0:T(8,128)S(1)}, u32[]{:S(2)}, u32[]{:S(2)}) collective-permute-start(f32[1,256,128]{2,1,0:T(8,128)} %get-tuple-element.111), channel_id=1, source_target_pairs={{0,28},{4,24},{8,20},{12,16},{16,12},{20,8},{24,4},{28,0},{1,29},{... | collective-permute-start | bytes 393224 | tf_op jit(solution)/shard_map/ppermute | solution.py:578
  (85 other events, 1184.0 us)
Sparse Core Ops, SparseCore 0:
  121.6 60.5 all-gather.4

commit v2 on v1

v2 whole, which is shorter than its diff:
```python
import functools
import math

import jax
import jax.numpy as jnp
import numpy as np
from jax import lax
from jax.experimental import pallas as pl
from jax.experimental.pallas import tpu as pltpu
from jax.sharding import PartitionSpec as P

NF = 64
NK = 64
LANES = 2 * NK
KAPPA = 0.2
COUPLING = 0.5
HIGHEST = lax.Precision.HIGHEST
ROW_BLOCKS = ("wall", "ckpt")
VMEM = pltpu.CompilerParams(vmem_limit_bytes=56 * 1024 * 1024)
F32 = jnp.float32
CHUNKS = ((0, 2), (3, 4, 1))
INWARD = (True, True)
STORED = True
OUTWARD = (True, True)


def complex_lanes(matrix):
    twice = np.kron(np.eye(2), matrix)
    return np.block([[twice.real, twice.imag], [-twice.imag, twice.real]]).astype(np.float32)


def span_matrix(direction):
    ids = np.arange(NK)
    return np.exp(2j * math.pi * direction * (np.outer(ids, ids) % NK) / NK)


def beta_matrix():
    ids = np.arange(NK)
    signed = (ids + NK // 2) % NK - NK // 2
    return span_matrix(-1) @ np.diag(2.0 / NK * signed) @ span_matrix(1) / NK


def split(value):
    high = value.astype(jnp.bfloat16)
    return high, (value - high.astype(F32)).astype(jnp.bfloat16)


def halves_of(matrix):
    high, low = split(jnp.asarray(matrix))
    return jnp.stack([high, low])


def dot3(x, w_ref):
    high, low = split(x)
    dot = functools.partial(jnp.dot, preferred_element_type=F32)
    return (dot(low, w_ref[0]) + dot(high, w_ref[1])) + dot(high, w_ref[0])


def low_half(shape):
    return lax.broadcasted_iota(jnp.int32, shape, len(shape) - 1) < NK


def swap(value):
    return pltpu.roll(value, NK, value.ndim - 1)


def dft4(x, sign):
    (ar, ai), (br, bi), (cr, ci), (dr, di) = x
    pr, pi, mr, mi = ar + cr, ai + ci, ar - cr, ai - ci
    qr, qi, nr, ni = br + dr, bi + di, br - dr, bi - di
    if sign > 0:
        nr, ni = -ni, nr
    else:
        nr, ni = ni, -nr
    return [(pr + qr, pi + qi), (mr + nr, mi + ni), (pr - qr, pi - qi), (mr - nr, mi - ni)]


def dft8(x, sign):
    even = dft4(x[0::2], sign)
    odd = dft4(x[1::2], sign)
    half = math.sqrt(0.5)
    (r1, i1), (r2, i2), (r3, i3) = odd[1], odd[2], odd[3]
    if sign > 0:
        odd[1] = (half * (r1 - i1), half * (i1 + r1))
        odd[2] = (-i2, r2)
        odd[3] = (-half * (r3 + i3), half * (r3 - i3))
    else:
        odd[1] = (half * (r1 + i1), half * (i1 - r1))
        odd[2] = (i2, -r2)
        odd[3] = (half * (i3 - r3), -half * (i3 + r3))
    first = [(a + c, b + d) for (a, b), (c, d) in zip(even, odd)]
    second = [(a - c, b - d) for (a, b), (c, d) in zip(even, odd)]
    return first + second


def turned(pair, power, sign):
    power %= NF
    if power == 0:
        return pair
    angle = 2.0 * math.pi * power / NF
    c, s = math.cos(angle), sign * math.sin(angle)
    re, im = pair
    return (c * re - s * im, c * im + s * re)


class Sizes:
    def __init__(self, rows, slots):
        self.group = lax.axis_size("mode")
        self.block_rows = rows
        self.slots = slots
        self.lane_groups = slots // LANES
        self.blocks = slots // NK
        self.rows = rows // self.group
        self.half = self.rows // 2
        self.tile = min(8, self.half)
        self.tiles = self.half // self.tile
        self.padded = (self.half + 7) // 8 * 8 + 16
        self.body = 2 * self.blocks * self.half
        self.rims = 2 * self.blocks


class Pieces:
    def __init__(self, whole, arrays):
        self.whole, self.arrays = whole, arrays

    def specs(self, group):
        if self.whole:
            length = self.arrays[0].shape[2]
            return [pl.BlockSpec((group, 1, length, LANES), lambda i, *_: (0, i, 0, 0))]
        length = self.arrays[0].shape[1]
        return [pl.BlockSpec((1, length, LANES), lambda i, *_: (i, 0, 0))] * group

    @staticmethod
    def shapes(whole, group, count, length):
        if whole:
            return [jax.ShapeDtypeStruct((group, count, length, LANES), F32)]
        return [jax.ShapeDtypeStruct((count, length, LANES), F32)] * group

    def exchange(self):
        if self.whole:
            return Pieces(True, [lax.all_to_all(self.arrays[0], "mode", 0, 0, tiled=True)])
        group = len(self.arrays)
        moved = [
            lax.ppermute(self.arrays[k], "mode", [(i, i ^ k) for i in range(group)])
            for k in range(1, group)
        ]
        return Pieces(False, [self.arrays[0]] + moved)


def field_at(fields):
    return lambda i: sum(jnp.where(i == n, f, 0) for n, f in enumerate(fields))


def piece_refs(refs, whole, group):
    if whole:
        return [refs[0].at[k, 0] for k in range(group)], refs[1:]
    return [ref.at[0] for ref in refs[:group]], refs[group:]


def partner(whole, me, k):
    return k if whole else me ^ k


def pair_rows(top, bottom):
    low = low_half(top.shape)
    return jnp.where(low, top, swap(bottom)), jnp.where(low, swap(top), bottom)


def cut_pieces(sz, dest, planes, out, base=0):
    row = pl.multiple_of(8 + dest * sz.rows, 8)
    for g in range(sz.lane_groups):
        whole = planes[g, pl.ds(row, sz.rows), :]
        for c in range(2):
            part = whole[:, c * LANES : (c + 1) * LANES]
            for odd, value in enumerate(pair_rows(part[: sz.half], part[sz.half :])):
                place = base + (c * sz.blocks + 2 * g + odd) * sz.half
                out[place : place + sz.half, :] = value


def join(x_ref, at):
    return jnp.concatenate([x_ref[c, ..., at].reshape(-1, LANES) for c in range(2)], axis=1)


def join_rows(x_ref, rows, step, at):
    parts = [
        jnp.concatenate([x_ref[pl.ds(r + c * step, 1), :] for r in rows], axis=0) for c in range(2)
    ]
    at = slice(at.start, at.start + at.size)
    return jnp.concatenate([part[:, at] for part in parts], axis=1)


def put_rows(sz, out, place, rows):
    for c in range(2):
        at = slice(c * LANES, (c + 1) * LANES)
        for g, (down, up) in enumerate(rows):
            for odd, value in enumerate(pair_rows(down[:, at], up[:, at])):
                row = place + c * sz.blocks + 2 * g + odd
                out[row : row + 1, :] = value


def cut_rims(sz, dest, planes, out, place, depths):
    for depth in range(depths):
        down = pl.ds(8 - 1 - depth + dest * sz.rows, 1)
        up = pl.ds(8 + depth + (dest + 1) * sz.rows, 1)
        rows = [(planes[g, down, :], planes[g, up, :]) for g in range(sz.lane_groups)]
        put_rows(sz, out, place + depth * sz.rims, rows)


def adjoint_prep_kernel(sz, whole, with_rims, field, me_ref, x_ref, w_ref, *rest):
    _, *rest = rest
    if with_rims:
        low, high, *rest = rest
        outs, (planes,) = piece_refs(rest, whole, sz.group)
    else:
        outs, (ends, planes) = piece_refs(rest, whole, sz.group)
    body = slice(8, 8 + sz.block_rows)
    row = 2 * field(pl.program_id(0))
    for g in range(sz.lane_groups):
        at = pl.ds(g * LANES, LANES)
        planes[g, body, :] = dot3(
            jnp.concatenate([x_ref[0, 0, :, at], x_ref[1, 0, :, at]], axis=1), w_ref
        )
        if with_rims:
            step = low.shape[0] // 2 - 1
            planes[g, 6:8, :] = dot3(join_rows(low, (row, row + 1), step, at), w_ref)
            planes[g, 8 + sz.block_rows : 10 + sz.block_rows, :] = dot3(
                join_rows(high, (row, row + 1), step, at), w_ref
            )
    for k in range(sz.group):
        dest = partner(whole, me_ref[0], k)
        cut_pieces(sz, dest, planes, outs[k])
        if with_rims:
            cut_rims(sz, dest, planes, outs[k], sz.body, 2)
        else:
            for g in range(sz.lane_groups):
                for n, row in enumerate((0, 1, sz.rows - 1, sz.rows - 2)):
                    row = 8 + k * sz.rows + row
                    ends[0, n, g, k : k + 1, :] = planes[g, row : row + 1, :]


def adjoint_prep(sz, whole, me, adjoint, w, fields, after, edges=None):
    count = len(fields)
    field = field_at(fields)
    with_rims = edges is not None
    shapes = Pieces.shapes(whole, sz.group, count, sz.body + (2 * sz.rims if with_rims else 0))
    in_specs = [
        pl.BlockSpec((2, 1, sz.block_rows, sz.slots), lambda i, me: (0, field(i), 0, 0)),
        pl.BlockSpec(w.shape, lambda i, me: (0, 0, 0)),
        pl.BlockSpec(memory_space=pl.ANY),
    ]
    operands = [me, adjoint, w, after]
    out_specs, out_shape = Pieces(whole, shapes).specs(sz.group), list(shapes)
    if with_rims:
        in_specs += [pl.BlockSpec(x.shape, lambda i, me: (0, 0)) for x in edges]
        operands += edges
    else:
        ends = (4, sz.lane_groups, sz.group, 2 * LANES)
        out_specs.append(pl.BlockSpec((1,) + ends, lambda i, me: (i, 0, 0, 0, 0)))
        out_shape.append(jax.ShapeDtypeStruct((count,) + ends, F32))
    arrays = pl.pallas_call(
        functools.partial(adjoint_prep_kernel, sz, whole, with_rims, field),
        grid_spec=pltpu.PrefetchScalarGridSpec(
            num_scalar_prefetch=1,
            grid=(count,),
            in_specs=in_specs,
            out_specs=out_specs,
            scratch_shapes=[pltpu.VMEM((sz.lane_groups, sz.block_rows + 16, 2 * LANES), F32)],
        ),
        out_shape=out_shape,
        compiler_params=VMEM,
        name="adjoint_prep",
    )(*operands)
    return Pieces(whole, arrays[: len(shapes)]), arrays[len(shapes) :]


def forward_prep_kernel(
    sz, whole, chunk, me_ref, own, other, before, low, high, past, ends, freq, w_ref, *rest
):
    outs, (planes, rims) = piece_refs(rest, whole, sz.group)
    here = me_ref[1]
    body = slice(8, 8 + sz.block_rows)
    for g in range(sz.lane_groups):
        at = pl.ds(g * LANES, LANES)
        for x_ref, station in ((own, here), (other, 1 - here)):
            planes[station, g, body, :] = dot3(join(x_ref.at[0], at), w_ref)
        count = low.shape[0] - 2
        step = count // 2
        inner = here == 0
        row = [before[0, c, 7:8, at] for c in range(2)]
        row = jnp.concatenate(row, axis=1)
        row = jnp.where(inner, join_rows(low, (count,), 1, at), row)
        planes[1, g, 7:8, :] = dot3(row, w_ref)
        row = jnp.where(inner, join_rows(high, (count,), 1, at), join_rows(past, (0,), 1, at))
        planes[1, g, 8 + sz.block_rows : 9 + sz.block_rows, :] = dot3(row, w_ref)
        far_low, far_high = (
            dot3(jnp.concatenate([x_ref[c * step : (c + 1) * step, at] for c in range(2)], 1), w_ref)
            for x_ref in (low, high)
        )
        for i, field in enumerate(chunk):
            for depth in range(2):
                row = 2 * field + 1 - depth
                rims[i, depth, 0, g] = jnp.concatenate(
                    [far_low[row : row + 1], ends[i, 2 + depth, g][:-1]], 0
                )
                row = 2 * field + depth
                rims[i, depth, 1, g] = jnp.concatenate(
                    [ends[i, depth, g][1:], far_high[row : row + 1]], 0
                )
    for k in range(sz.group):
        dest = partner(whole, me_ref[0], k)
        outs[k][:8, :] = freq[...]
        for station in range(2):
            cut_pieces(sz, dest, planes.at[station], outs[k], 8 + station * sz.body)
        place = 8 + 2 * sz.body
        cut_rims(sz, dest, planes.at[1], outs[k], place, 1)
        row = pl.ds(dest, 1)
        for i in range(len(chunk)):
            for depth in range(2):
                place += sz.rims
                rows = [
                    (rims[i, depth, 0, g, row, :], rims[i, depth, 1, g, row, :])
                    for g in range(sz.lane_groups)
                ]
                put_rows(sz, outs[k], place, rows)


def forward_prep(sz, whole, me, forward, other, edges, ends, freq, w, chunk):
    length = (8 + 2 * sz.body + (1 + 2 * len(chunk)) * sz.rims + 7) // 8 * 8
    shapes = Pieces.shapes(whole, sz.group, 1, length)
    rows = (1, 2, sz.block_rows, sz.slots)
    rest = [*edges, ends, freq, w]
    before = sz.block_rows // 8 - 1
    arrays = pl.pallas_call(
        functools.partial(forward_prep_kernel, sz, whole, chunk),
        grid_spec=pltpu.PrefetchScalarGridSpec(
            num_scalar_prefetch=1,
            grid=(1,),
            in_specs=[
                pl.BlockSpec(rows, lambda i, me: (0, 0, me[1], 0)),
                pl.BlockSpec(rows, lambda i, me: (0, 0, 0, 0)),
                pl.BlockSpec((1, 2, 8, sz.slots), lambda i, me: (0, 0, before, 0)),
            ]
            + [pl.BlockSpec(x.shape, lambda i, me, zeros=(0,) * x.ndim: zeros) for x in rest],
            out_specs=Pieces(whole, shapes).specs(sz.group),
            scratch_shapes=[
                pltpu.VMEM((2, sz.lane_groups, sz.block_rows + 16, 2 * LANES), F32),
                pltpu.VMEM((len(chunk), 2, 2, sz.lane_groups, sz.group, 2 * LANES), F32),
            ],
        ),
        out_shape=shapes,
        compiler_params=VMEM,
        name="forward_prep",
    )(me, forward, other, forward, *rest)
    return Pieces(whole, arrays)


def frequency(sz, table_ref, whole, k, j):
    place = k ^ table_ref[sz.group * sz.blocks] if whole else k
    return table_ref[place * sz.blocks + j]


def gather_pieces(sz, table_ref, whole, pieces, state, lead, base=0):
    for k, piece in enumerate(pieces):
        for j in range(sz.blocks):
            freq = frequency(sz, table_ref, whole, k, j)
            for c in range(2):
                at = base + (c * sz.blocks + j) * sz.half
                state[c, freq, lead : lead + sz.half, :] = piece[at : at + sz.half, :]


def lead_first(sz, state, rows, work, out_rows):
    for a in range(8):
        x = [(state[0, a + 8 * b, rows, :], state[1, a + 8 * b, rows, :]) for b in range(8)]
        for t, pair in enumerate(dft8(x, 1)):
            re, im = turned(pair, a * t, 1)
            work[0, 8 * t + a, out_rows, :] = re
            work[1, 8 * t + a, out_rows, :] = im


def lead_second(work, t, rows):
    x = [(work[0, 8 * t + a, rows, :], work[1, 8 * t + a, rows, :]) for a in range(8)]
    return dft8(x, 1)


def couple(sz, state, rows, work, work_rows, phys, phys_rows, store):
    lead_first(sz, state, rows, work, work_rows)
    for t in range(8):
        product = []
        for u, (re, im) in enumerate(lead_second(work, t, work_rows)):
            wr, wi = phys[0, 8 * t + u, phys_rows, :], phys[1, 8 * t + u, phys_rows, :]
            product.append((wr * re + wi * im, wr * im - wi * re))
        for a, pair in enumerate(dft8(product, -1)):
            re, im = turned(pair, a * t, -1)
            work[0, 8 * t + a, work_rows, :] = re
            work[1, 8 * t + a, work_rows, :] = im
    for a in range(8):
        x = [
            (work[0, 8 * t + a, work_rows, :], work[1, 8 * t + a, work_rows, :]) for t in range(8)
        ]
        for b, pair in enumerate(dft8(x, -1)):
            store(a + 8 * b, pair)


def gather_rims(sz, table_ref, whole, pieces, rims, base):
    for k, piece in enumerate(pieces):
        for j in range(sz.blocks):
            freq = frequency(sz, table_ref, whole, k, j)
            for c in range(2):
                at = base + c * sz.blocks + j
                rims[c, pl.ds(freq, 1), :] = piece[at : at + 1, :]


def forward_kernel(sz, whole, chunk, me_ref, *rest):
    pieces, rest = piece_refs(rest, whole, sz.group)
    heads, rest = piece_refs(rest, whole, sz.group)
    out, next_out, rims, table_ref, state, work, next_state, next_work = rest
    count = sz.group * sz.blocks
    for k in range(sz.group):
        place = k ^ me_ref[0] if whole else k
        for j in range(sz.blocks):
            table_ref[place * sz.blocks + j] = heads[k][j, 0].astype(jnp.int32)
    for n in range(4):
        table_ref[count + n] = me_ref[n]
    for station in range(2):
        gather_pieces(sz, table_ref, whole, pieces, state, 0, 8 + station * sz.body)

        @pl.loop(0, sz.tiles)
        def _(s):
            rows = pl.ds(s * sz.tile, sz.tile)
            lead_first(sz, state, rows, work, rows)
            for t in range(8):
                for u, (re, im) in enumerate(lead_second(work, t, rows)):
                    out[station, 0, 8 * t + u, rows, :] = re
                    out[station, 1, 8 * t + u, rows, :] = im

    base = 8 + 2 * sz.body
    gather_rims(sz, table_ref, whole, pieces, rims.at[0, 0], base)
    spread_rims(rims[0, 0].reshape(2 * NF, LANES), next_state, 0)
    rows = slice(0, 8)
    lead_first(sz, next_state, rows, next_work, rows)
    for t in range(8):
        for u, (re, im) in enumerate(lead_second(next_work, t, rows)):
            next_out[0, 8 * t + u] = re[:1]
            next_out[1, 8 * t + u] = im[:1]
    for i in range(chunk):
        for depth in range(2):
            base += sz.rims
            gather_rims(sz, table_ref, whole, pieces, rims.at[i, depth], base)


def forward_physical(sz, me, pieces, chunk):
    full = (2, NF, sz.half, LANES)
    rims = (chunk, 2, 2, NF, LANES)
    if pieces.whole:
        heads = [
            pl.BlockSpec((sz.group, 1, 8, LANES), lambda i, t: (0, 0, 0, 0), memory_space=pltpu.SMEM)
        ]
    else:
        head = pl.BlockSpec((1, 8, LANES), lambda i, t: (0, 0, 0), memory_space=pltpu.SMEM)
        heads = [head] * sz.group
    return pl.pallas_call(
        functools.partial(forward_kernel, sz, pieces.whole, chunk),
        grid_spec=pltpu.PrefetchScalarGridSpec(
            num_scalar_prefetch=1,
            grid=(1,),
            in_specs=pieces.specs(sz.group) + heads,
            out_specs=[
                pl.BlockSpec((2,) + full, lambda i, t: (0, 0, 0, 0, 0)),
                pl.BlockSpec((2, NF, 1, LANES), lambda i, t: (0, 0, 0, 0)),
                pl.BlockSpec(rims, lambda i, t: (0, 0, 0, 0, 0)),
                pl.BlockSpec(memory_space=pltpu.SMEM),
            ],
            scratch_shapes=[
                pltpu.VMEM(full, F32),
                pltpu.VMEM(full, F32),
                pltpu.VMEM((2, NF, 8, LANES), F32),
                pltpu.VMEM((2, NF, 8, LANES), F32),
            ],
        ),
        out_shape=[
            jax.ShapeDtypeStruct((2,) + full, F32),
            jax.ShapeDtypeStruct((2, NF, 1, LANES), F32),
            jax.ShapeDtypeStruct(rims, F32),
            jax.ShapeDtypeStruct((sz.group * sz.blocks + 4,), jnp.int32),
        ],
        compiler_params=VMEM,
        name="forward_physical",
    )(me, *pieces.arrays, *pieces.arrays)


def spread_rims(rims, state, n):
    state.reshape(2 * NF * 8, LANES)[pl.ds(n, 2 * NF, stride=8), :] = rims


def place_edges(sz, state, rims):
    padded = sz.padded
    rows = state.reshape(2 * NF * padded, LANES)
    first = rows[pl.ds(8, 2 * NF, stride=padded), :]
    last = rows[pl.ds(8 + sz.half - 1, 2 * NF, stride=padded), :]
    low = low_half(first.shape)
    rows[pl.ds(7, 2 * NF, stride=padded), :] = jnp.where(low, rims, swap(last))
    rows[pl.ds(8 + sz.half, 2 * NF, stride=padded), :] = jnp.where(low, swap(first), rims)


def advance(sz, state, work, phys, out, lead):
    @pl.loop(0, sz.tiles)
    def _(s):
        rows = pl.ds(8 + s * sz.tile, sz.tile)
        at = pl.ds(s * sz.tile, sz.tile)

        def store(f, pair):
            for c in range(2):
                mid = state[c, f, rows, :]
                up = state[c, f, pl.ds(9 + s * sz.tile, sz.tile), :]
                down = state[c, f, pl.ds(7 + s * sz.tile, sz.tile), :]
                stepped = (1.0 - 2.0 * KAPPA) * mid + KAPPA * (up + down)
                out[c, f, pl.ds(lead + s * sz.tile, sz.tile), :] = (
                    stepped - (COUPLING / NF) * pair[c]
                )

        couple(sz, state, rows, work, at, phys, at, store)


def march_kernel(sz, whole_in, whole_out, row_scale, fields, table_ref, *rest):
    pieces, rest = piece_refs(rest, whole_in, sz.group)
    phys, next_phys, *rest = rest
    running = row_scale is not None
    if running:
        all_rims, rest = rim_refs(rest, whole_in, sz.group)
        pair, pair_rims, start, w_ref, *rest = rest
    else:
        rims_in, w_ref, *rest = rest
    outs, rest = piece_refs(rest, whole_out, sz.group)
    if not running:
        pair_out, pair_rims_out, total_out, *rest = rest
    state, work, middle, stepped, rims, next_state, next_work, next_coupling, sums = rest
    step = pl.program_id(0)
    count = sz.group * sz.blocks

    @pl.when(step == 0)
    def _():
        next_state[...] = jnp.zeros_like(next_state)
        for i in range(fields):
            for depth in range(2):
                if running:
                    views = [ref.at[i] for ref in all_rims]
                    gather_rims(sz, table_ref, whole_in, views, rims.at[i, depth], depth * sz.rims)
                else:
                    rims[i, depth] = rims_in[i, depth]
            spread_rims(rims[i, 0].reshape(2 * NF, LANES), next_state, i)
        rows = slice(0, 8)

        def store(f, pair):
            for c in range(2):
                next_coupling[c, f] = (COUPLING / NF) * pair[c]

        couple(sz, next_state, rows, next_work, rows, next_phys, slice(0, 1), store)

    gather_pieces(sz, table_ref, whole_in, pieces, state, 8)
    near = rims[step, 0].reshape(2 * NF, LANES)
    place_edges(sz, state, near)
    advance(sz, state, work, phys.at[1], middle, 8)

    low = low_half((2 * NF, LANES))
    flat = state.reshape(2 * NF * sz.padded, LANES)
    inner = jnp.where(
        low,
        flat[pl.ds(8, 2 * NF, stride=sz.padded), :],
        flat[pl.ds(8 + sz.half - 1, 2 * NF, stride=sz.padded), :],
    )
    far = rims[step, 1].reshape(2 * NF, LANES)
    coupled = next_coupling.reshape(2 * NF * 8, LANES)[pl.ds(step, 2 * NF, stride=8), :]
    near = (1.0 - 2.0 * KAPPA) * near + KAPPA * (inner + far) - coupled
    rims[step, 0] = near.reshape(2, NF, LANES)
    if running:

        @pl.when(step == fields - 1)
        def _():
            add_running(
                sz, row_scale, middle, rims.at[step, 0], pair, pair_rims, start, w_ref, next_work
            )

    first = table_ref[count + 2].astype(F32)
    last = table_ref[count + 3].astype(F32)
    near = rims[step, 0].reshape(2 * NF, LANES) * jnp.where(low, 1.0 - first, 1.0 - last)
    if not running:
        pair_rims_out[0] = near.reshape(2, NF, LANES)
        body = middle[:, :, 8 : 8 + sz.half, :]
        pair_out[0] = body
        value = jnp.sum(body, axis=2)
        value = value + swap(value)

        @pl.when(step == 0)
        def _():
            freq = lax.broadcasted_iota(jnp.int32, value.shape, 1)
            rate = 2.0 / NF * ((freq + NF // 2) % NF - NF // 2).astype(F32)
            sums[...] = rate * value

        @pl.when(step != 0)
        def _():
            turned = dot3(jnp.concatenate([value[0], value[1]], axis=1), w_ref)
            re, im = sums[0] + turned[:, :LANES], sums[1] + turned[:, LANES:]
            total = jnp.where(low_half((NF, LANES)), re, im)
            total_out[...] = total

    place_edges(sz, middle, near)
    advance(sz, middle, work, phys.at[0], stepped, 0)
    for k in range(sz.group):
        for j in range(sz.blocks):
            freq = frequency(sz, table_ref, whole_out, k, j)
            for c in range(2):
                at = (c * sz.blocks + j) * sz.half
                outs[k][at : at + sz.half, :] = stepped[c, freq]


def rim_refs(refs, whole, group):
    if whole:
        return [refs[0].at[k] for k in range(group)], refs[1:]
    return list(refs[:group]), refs[group:]


def march(sz, whole_out, table, pieces, phys, next_phys, fields, rims=None, row_scale=None, running=()):
    full = (2, NF, sz.half, LANES)
    shapes = Pieces.shapes(whole_out, sz.group, fields, sz.body)

    def constant(x):
        return pl.BlockSpec(x.shape, lambda i, t, zeros=(0,) * len(x.shape): zeros)

    def by_field(shape):
        return pl.BlockSpec((1,) + shape, lambda i, t, zeros=(0,) * len(shape): (i,) + zeros)

    body = Pieces(pieces.whole, Pieces.shapes(pieces.whole, sz.group, fields, sz.body))
    in_specs = body.specs(sz.group) + [constant(phys), constant(next_phys)]
    operands = [table, *pieces.arrays, phys, next_phys]
    out_specs, out_shape = Pieces(whole_out, shapes).specs(sz.group), list(shapes)
    if running:
        place = sz.body // (2 * sz.rims)
        if pieces.whole:
            block = (sz.group, fields, 2 * sz.rims, LANES)
            in_specs.append(pl.BlockSpec(block, lambda i, t: (0, 0, place, 0)))
        else:
            block = (fields, 2 * sz.rims, LANES)
            in_specs += [pl.BlockSpec(block, lambda i, t: (0, place, 0))] * sz.group
        in_specs += [constant(x) for x in running]
        operands += [*pieces.arrays, *running]
    else:
        in_specs += [constant(x) for x in rims]
        operands += rims
        for shape in (full, (2, NF, LANES)):
            out_specs.append(by_field(shape))
            out_shape.append(jax.ShapeDtypeStruct((fields,) + shape, F32))
        out_shape.append(jax.ShapeDtypeStruct((NF, LANES), F32))
        out_specs.append(constant(out_shape[-1]))
    padded = pltpu.VMEM((2, NF, sz.padded, LANES), F32)
    small = pltpu.VMEM((2, NF, 8, LANES), F32)
    arrays = pl.pallas_call(
        functools.partial(march_kernel, sz, pieces.whole, whole_out, row_scale, fields),
        grid_spec=pltpu.PrefetchScalarGridSpec(
            num_scalar_prefetch=1,
            grid=(fields,),
            in_specs=in_specs,
            out_specs=out_specs,
            scratch_shapes=[
                padded,
                pltpu.VMEM(full, F32),
                padded,
                pltpu.VMEM(full, F32),
                pltpu.VMEM((fields, 2, 2, NF, LANES), F32),
                small,
                small,
                small,
                pltpu.VMEM((2, NF, LANES), F32),
            ],
        ),
        out_shape=out_shape,
        compiler_params=VMEM,
        name="march",
    )(*operands)
    return Pieces(whole_out, arrays[: len(shapes)]), arrays[len(shapes) :]


def running_rows(sz, value, start):
    row = lax.broadcasted_iota(jnp.int32, value.shape, 0)
    reach = 1
    while reach < sz.half:
        value = value + jnp.where(row >= reach, pltpu.roll(value, reach, 0), 0.0)
        reach *= 2
    bottom = jnp.where(low_half((1, LANES)), 0.0, swap(value[sz.half - 1 :]))
    return value + (bottom + start)


def add_running(sz, row_scale, middle, near, pair, pair_rims, start, w_ref, work):
    both = jnp.concatenate([pair[1, 0], pair[1, 1]], axis=2).reshape(NF * sz.half, 2 * LANES)
    turned_two = dot3(both, w_ref)
    turned_rims = dot3(jnp.concatenate([pair_rims[1, 0], pair_rims[1, 1]], axis=1), w_ref)
    low = low_half((1, LANES))
    for f in range(NF):
        at = f * sz.half
        alpha = 2.0 / NF * ((f + NF // 2) % NF - NF // 2)
        spread = start[pl.ds(f, 1), :]
        starts = (jnp.where(low, spread, swap(spread)), jnp.where(low, swap(spread), spread))
        run = []
        for c in range(2):
            lanes = slice(c * LANES, (c + 1) * LANES)
            source = turned_two[at : at + sz.half, lanes] + alpha * pair[0, c, f]
            run.append(running_rows(sz, source, starts[c]))
            past = turned_rims[f : f + 1, lanes] + alpha * pair_rims[0, c, f : f + 1, :]
            work[c, f, 0:1, :] = jnp.where(low, starts[c], run[c][sz.half - 1 :] + past)
        rows = slice(8, 8 + sz.half)
        middle[0, f, rows, :] += row_scale * run[1]
        middle[1, f, rows, :] -= row_scale * run[0]
        near[0, f : f + 1, :] += row_scale * work[1, f, 0:1, :]
        near[1, f : f + 1, :] -= row_scale * work[0, f, 0:1, :]


def join_pieces(sz, whole, me, pieces, planes):
    for k, piece in enumerate(pieces):
        row = pl.multiple_of(partner(whole, me, k) * sz.rows, sz.rows)
        for g in range(sz.lane_groups):
            halves = []
            for c in range(2):
                at = (c * sz.blocks + 2 * g) * sz.half
                even = piece[at : at + sz.half, :]
                odd = piece[at + sz.half : at + 2 * sz.half, :]
                low = low_half(even.shape)
                top = jnp.where(low, even, swap(odd))
                bottom = jnp.where(low, swap(even), odd)
                halves.append(jnp.concatenate([top, bottom], axis=0))
            planes[g, pl.ds(row, sz.rows), :] = jnp.concatenate(halves, axis=1)


def post_kernel(sz, whole, running, row_scale, me_ref, *rest):
    pieces, rest = piece_refs(rest, whole, sz.group)
    w_ref, rest = rest[0], rest[1:]
    if running == "add":
        sums_ref, start_ref, rest = rest[0], rest[1], rest[2:]
    elif running == "make":
        alpha_ref, beta_ref, tri_ref, rest = rest[0], rest[1], rest[2], rest[3:]
        rest, source = rest[:-1], rest[-1]
    planes = rest[-1]
    outs = rest[:-1]
    if running != "make":
        outs = outs[1:]
    out = outs[0]
    join_pieces(sz, whole, me_ref[0], pieces, planes)
    for g in range(sz.lane_groups):
        at = pl.ds(g * LANES, LANES)
        back = dot3(planes[g], w_ref)
        halves = [back[:, :LANES], back[:, LANES:]]
        for c in range(2):
            out[c, 0, :, at] = halves[c]
        if running == "add":

            @pl.when(pl.program_id(0) == pl.num_programs(0) - 1)
            def _():
                sums = [sums_ref[c, :, at] + start_ref[pl.ds(c, 1), at] for c in range(2)]
                out[0, 0, :, at] += row_scale * sums[1]
                out[1, 0, :, at] -= row_scale * sums[0]

        if running == "make":

            @pl.when(pl.program_id(0) == 0)
            def _():
                for c in range(2):
                    source[g, :, c * LANES : (c + 1) * LANES] = halves[c] * alpha_ref[:, at]

            @pl.when(pl.program_id(0) != 0)
            def _():
                both = [
                    source[g, :, c * LANES : (c + 1) * LANES] + halves[c] * beta_ref[:, at]
                    for c in range(2)
                ]
                high, low = split(jnp.concatenate(both, axis=1))
                tri = tri_ref[...]
                total = jnp.dot(tri, low, preferred_element_type=F32)
                total = total + jnp.dot(tri, high, preferred_element_type=F32)
                for c in range(2):
                    outs[1][c, :, at] = total[:, c * LANES : (c + 1) * LANES]
                    outs[2][c : c + 1, at] = total[-1:, c * LANES : (c + 1) * LANES]


def post(sz, row_scale, me, pieces, fields, held, running=None, extra=()):
    count = len(fields)
    field = field_at(fields)
    w = halves_of(complex_lanes(span_matrix(-1) / NK))
    w_spec = pl.BlockSpec((2, 2 * LANES, 2 * LANES), lambda i, me: (0, 0, 0))
    in_specs = pieces.specs(sz.group) + [w_spec]
    row_spec = pl.BlockSpec((1, sz.slots), lambda i, me: (0, 0))
    sums_spec = pl.BlockSpec((2, sz.block_rows, sz.slots), lambda i, me: (0, 0, 0))
    if running == "add":
        in_specs += [sums_spec, pl.BlockSpec((2, sz.slots), lambda i, me: (0, 0))]
    elif running == "make":
        square = pl.BlockSpec((sz.block_rows, sz.block_rows), lambda i, me: (0, 0))
        in_specs += [row_spec, row_spec, square]
    out_specs = [
        pl.BlockSpec((2, 1, sz.block_rows, sz.slots), lambda i, me: (0, field(i), 0, 0))
    ]
    out_shape = [jax.ShapeDtypeStruct((2, 5, sz.block_rows, sz.slots), F32)]
    aliases = {}
    operands = [me, *pieces.arrays, w, *extra]
    plane = pltpu.VMEM((sz.lane_groups, sz.block_rows, 2 * LANES), F32)
    if running == "make":
        out_specs.append(sums_spec)
        out_shape.append(jax.ShapeDtypeStruct((2, sz.block_rows, sz.slots), F32))
        out_specs.append(pl.BlockSpec((2, sz.slots), lambda i, me: (0, 0)))
        out_shape.append(jax.ShapeDtypeStruct((2, sz.slots), F32))
    else:
        in_specs.append(pl.BlockSpec(memory_space=pl.ANY))
        operands.append(held)
        aliases = {len(operands) - 1: 0}
    return pl.pallas_call(
        functools.partial(post_kernel, sz, pieces.whole, running, row_scale),
        grid_spec=pltpu.PrefetchScalarGridSpec(
            num_scalar_prefetch=1,
            grid=(count,),
            in_specs=in_specs,
            out_specs=out_specs,
            scratch_shapes=[plane] * (2 if running == "make" else 1),
        ),
        out_shape=out_shape,
        input_output_aliases=aliases,
        compiler_params=VMEM,
        name="post",
    )(*operands)


def follow(pieces, earlier):
    def kernel(*refs):
        pass

    count = len(pieces.arrays)
    in_place = pl.BlockSpec(memory_space=pl.ANY)
    arrays = pl.pallas_call(
        kernel,
        in_specs=[in_place] * (count + len(earlier)),
        out_specs=[in_place] * count,
        out_shape=[jax.ShapeDtypeStruct(x.shape, x.dtype) for x in pieces.arrays],
        input_output_aliases={n: n for n in range(count)},
        name="follow",
    )(*pieces.arrays, *earlier)
    return Pieces(pieces.whole, arrays)


def edge_kernel(first_ref, last_ref, before, middle, after, token, low, high, past):
    rows = first_ref.shape[1] * 2
    for c in range(2):
        for field in range(first_ref.shape[1]):
            at = c * rows + 2 * field
            low[at : at + 2, :] = last_ref[c, field, 6:8, :]
            high[at : at + 2, :] = first_ref[c, field, 0:2, :]
        at = 2 * rows + c
        low[at : at + 1, :] = after[0, c, 7:8, :]
        high[at : at + 1, :] = middle[0, c, 0:1, :]
        past[c : c + 1, :] = before[0, c, 0:1, :]


def edge_rows(sz, adjoint, forward, after):
    parts, fields = adjoint.shape[:2]
    rows = (parts, fields, 8, sz.slots)
    stored = (1, parts, 8, sz.slots)
    tiles = sz.block_rows // 8
    last = forward.shape[2] // 8 - 1
    count = parts * fields * 2 + parts
    return pl.pallas_call(
        edge_kernel,
        grid=(1,),
        in_specs=[
            pl.BlockSpec(rows, lambda i: (0, 0, 0, 0)),
            pl.BlockSpec(rows, lambda i: (0, 0, tiles - 1, 0)),
            pl.BlockSpec(stored, lambda i: (0, 0, 0, 0)),
            pl.BlockSpec(stored, lambda i: (0, 0, tiles, 0)),
            pl.BlockSpec(stored, lambda i: (0, 0, last, 0)),
            pl.BlockSpec(memory_space=pl.ANY),
        ],
        out_specs=[pl.BlockSpec((n, sz.slots), lambda i: (0, 0)) for n in (count, count, parts)],
        out_shape=[jax.ShapeDtypeStruct((n, sz.slots), F32) for n in (count, count, parts)],
        name="edge_rows",
    )(adjoint, adjoint, forward, forward, forward, after)


def shifted(value, axes, step, count):
    return lax.ppermute(value, axes, [(i, i + step) for i in range(count) if 0 <= i + step < count])


def nearer_sum_by_pairs(value, axis):
    count, mine = lax.axis_size(axis), lax.axis_index(axis)
    other = lax.ppermute(value, axis, [(i, i ^ 1) for i in range(count)])
    before = jnp.where(mine & 1 != 0, other, 0.0)
    both = total = value + other
    for k in range(2, count, 2):
        other = lax.ppermute(both, axis, [(i, i ^ k) for i in range(count)])
        before = before + jnp.where(mine ^ k < mine, other, 0.0)
        total = total + other
    return before, total


def nearer_sum(value):
    blocks = lax.axis_size(ROW_BLOCKS)
    return sum(shifted(value, ROW_BLOCKS, step, blocks) for step in range(1, blocks))


def on_device(adjoint, forward, mode_map):
    sz = Sizes(adjoint.shape[2], adjoint.shape[3])
    stations = lax.axis_size("ckpt")
    row_scale = 1.0 / math.sqrt(sz.block_rows * lax.axis_size("wall") * stations)
    me = lax.axis_index("mode").astype(jnp.int32)
    here = lax.axis_index("ckpt").astype(jnp.int32)
    block, blocks = lax.axis_index(ROW_BLOCKS), lax.axis_size(ROW_BLOCKS)
    is_first = (block == 0) & (me == 0)
    is_last = (block == blocks - 1) & (me == sz.group - 1)
    place = jnp.stack([me, here, is_first.astype(jnp.int32), is_last.astype(jnp.int32)])
    spread = halves_of(complex_lanes(span_matrix(1)))
    chunks = CHUNKS

    other = lax.dynamic_slice_in_dim(forward, (1 - here) * sz.block_rows, sz.block_rows, 2)
    moved = lax.ppermute(other, "ckpt", [(i, stations - 1 - i) for i in range(stations)])

    pieces, (ends,) = adjoint_prep(sz, INWARD[0], place, adjoint, spread, chunks[0], other)
    inward = [pieces.exchange()]

    low, high, past = edge_rows(sz, adjoint, forward, ends)
    low = shifted(low, ROW_BLOCKS, 1, blocks)
    high = shifted(high, ROW_BLOCKS, -1, blocks)
    past = shifted(past, ROW_BLOCKS, -stations, blocks)

    freq_index = lax.div(mode_map, jnp.int32(NK))
    span_index = lax.rem(mode_map, jnp.int32(NK))
    alpha = 2.0 / NF * ((freq_index + NF // 2) % NF - NF // 2).astype(F32)
    beta = 2.0 / NK * ((span_index + NK // 2) % NK - NK // 2).astype(F32)
    freq = freq_index.reshape(sz.blocks, NK)[:, :1].astype(F32)
    freq = jnp.pad(jnp.broadcast_to(freq, (sz.blocks, LANES)), ((0, 8 - sz.blocks), (0, 0)))

    stored = forward_prep(
        sz, STORED, place, forward, moved, (low, high, past), ends, freq, spread, chunks[0]
    )
    pieces, _ = adjoint_prep(
        sz, INWARD[1], place, adjoint, spread, chunks[1], stored.arrays[0], (low, high)
    )
    stored = follow(stored, inward[0].arrays).exchange()
    inward.append(follow(pieces, stored.arrays).exchange())

    phys, next_phys, rims, table = forward_physical(sz, place, stored, len(chunks[0]))
    turn = halves_of(complex_lanes(beta_matrix()))
    out, (pair, pair_rims, total) = march(
        sz, OUTWARD[0], table, inward[0], phys, next_phys, len(chunks[0]), (rims, turn)
    )
    start, whole = nearer_sum_by_pairs(total, "mode")
    start = start + nearer_sum(whole)
    running = (pair, pair_rims, start, turn)
    back = [follow(out, [start, inward[1].arrays[0]]).exchange()]
    out, _ = march(
        sz,
        OUTWARD[1],
        table,
        inward[1],
        phys,
        next_phys,
        len(chunks[1]),
        row_scale=row_scale,
        running=running,
    )
    back.append(out.exchange())

    tri = jnp.asarray(np.tril(np.ones((sz.block_rows, sz.block_rows))), jnp.bfloat16)
    out, sums, total = post(
        sz, row_scale, place, back[0], chunks[0], None, "make", (alpha[None], beta[None], tri)
    )
    start = nearer_sum(total)
    (out,) = post(sz, row_scale, place, back[1], chunks[1], out, "add", (sums, start))
    return out


def solution(mesh):
    placed = (P(None, None, ROW_BLOCKS, "mode"), P("ckpt", None, "wall", "mode"), P("mode"))
    return jax.shard_map(
        on_device,
        mesh=mesh,
        in_specs=placed,
        out_specs=P(None, None, ROW_BLOCKS, "mode"),
        check_vma=False,
    )
```

time: 319 us -> 233 us (0.73)
  starting transfers between devices: 82 us -> 47.6 us
  blocking collectives: 32.5 us -> 0 us
  Pallas kernels: 87.5 us -> 66.2 us
  waiting for transfers between devices: 80.5 us -> 99.2 us
  between operations: 14.8 us -> 0.17 us
    all_to_all x1 -> x5, waiting for transfers between devices: 0.01 us -> 56.4 us  [exchange(): lax.all_to_all(self.arrays[0], 'mode', 0, 0, tiled=True)]
    ppermute x57 -> x14, starting transfers between devices: 77.7 us -> 27.4 us  [the longest x9 21.8 us: shifted(): lax.ppermute(value, axes, [(i, i + step) for i in range(count) if 0 <= i...]
    ppermute x57 -> x14, waiting for transfers between devices: 80.5 us -> 42.9 us  [the longest x9 21 us: shifted(): lax.ppermute(value, axes, [(i, i + step) for i in range(count) if 0 <= i...]
    pallas_call x15 -> x12, Pallas kernels: 87.5 us -> 66.2 us  [the longest x2 26.7 us: march(): pl.pallas_call(functools.partial(march_kernel, sz, pieces.whole, whole_ou...]
    unnamed x1 -> x0, blocking collectives: 17.5 us -> none
    all_to_all x1 -> x5, starting transfers between devices: 4.29 us -> 20.2 us  [exchange(): lax.all_to_all(self.arrays[0], 'mode', 0, 0, tiled=True)]
    all_gather x1 -> x0, blocking collectives: 15 us -> none  [on_device(): totals = lax.all_gather(sums[:, -1], ROW_BLOCKS, axis=0)]
    reshape x3 -> x1, local copies, waits for them, and re-layouts: 3.77 us -> 0.08 us  [on_device(): freq = freq_index.reshape(sz.blocks, NK)[:, :1].astype(F32)]
  transfers between devices with their start and end apart: 59 -> 19, of which waited for: 13 -> 10; matrix products, arithmetic and copies ran while one was open for 3% -> 4% of each run, Pallas kernels for 24% -> 23%
where the time goes in v2:
time: 233 us; the launch traced here: 232 us
  waiting for transfers between devices  99.2 us (43%)
  Pallas kernels  66.2 us (28%)
  starting transfers between devices  47.6 us (20%)
  local copies, waits for them, and re-layouts  14 us (6%)
  other arithmetic  4.77 us (2%)
    all_to_all x5, waiting for transfers between devices, exchange(): lax.all_to_all(self.arrays[0], 'mode', 0, 0, tiled=True)  56.4 us
    pallas_call x2, Pallas kernels, march(): pl.pallas_call(functools.partial(march_kernel, sz, pieces.whole, whole_ou...  26.7 us
    ppermute x9, starting transfers between devices, shifted(): lax.ppermute(value, axes, [(i, i + step) for i in range(count) if 0 <= i...  21.8 us
    ppermute x9, waiting for transfers between devices, shifted(): lax.ppermute(value, axes, [(i, i + step) for i in range(count) if 0 <= i...  21 us
    ppermute x3, waiting for transfers between devices, nearer_sum_by_pairs(): other = lax.ppermute(both, axis, [(i, i ^ k) for i in range(count)])  20.8 us
    all_to_all x5, starting transfers between devices, exchange(): lax.all_to_all(self.arrays[0], 'mode', 0, 0, tiled=True)  20.2 us
    pallas_call x2, Pallas kernels, post(): pl.pallas_call(functools.partial(post_kernel, sz, pieces.whole, running,...  14.7 us
    pallas_call x2, Pallas kernels, adjoint_prep(): pl.pallas_call(functools.partial(adjoint_prep_kernel, sz, whole, with_rim...  11.4 us
  transfers between devices with their start and end apart: 19, of which 10 were waited for; matrix products, arithmetic and copies ran while one was open for 4% of the time, Pallas kernels for 23%

profile of v2, /device:TPU:0, one launch (start us, length us, event | category | flops | bytes accessed | tf_op | source)
XLA Modules:
  0.0 231.9 jit_solution(16918152618634885883)
XLA Ops:
  0.0 2.3 constant_dynamic-slice_fusion.rest_0_
  2.3 0.6 pad_add_fusion.me_ref
  2.9 4.5 %adjoint_prep.2 = (f32[8,2,256,128]{3,2,1,0:T(8,128)}, f32[2,4,4,8,256]{4,3,2,1,0:T(8,128)}) custom-call(s32[4]{0:T(128)} %pad_add_fusion.me_ref, f32[2,5,256,512]{3,2,1,0:T(8,128)} %x_ref.3, bf16[2,256,256]{2,1,0:T(8,128)(2,1)} %constant.82.w_ref, f32[1,2,256,512]{3,2,1,0:T(8,128)} %constant_dynamic-slice_fusion.rest_0_), custom_call_target="tpu_custom_call" | custom-call | tf_op jit(solution)/shard_map/adjoint_prep/pallas_call | solution.py:260
  7.4 5.3 %all-to-all-start = ((f32[8,2,256,128]{3,2,1,0:T(8,128)}), f32[8,2,256,128]{3,2,1,0:T(8,128)S(1)}, u32[]{:S(2)}, u32[]{:S(2)}) async-start(f32[8,2,256,128]{3,2,1,0:T(8,128)} %get-tuple-element.25), calls=%async_computation | async-start | bytes 4194304 | tf_op jit(solution)/shard_map/all_to_all | solution.py:141
  12.7 1.6 collective-permute-start
  14.4 1.7 edge_rows.1
  16.1 1.3 collective-permute-start.3
  17.4 2.4 %collective-permute-start.1 = (f32[22,512]{1,0:T(8,128)}, f32[22,512]{1,0:T(8,128)S(1)}, u32[]{:S(2)}, u32[]{:S(2)}) collective-permute-start(f32[22,512]{1,0:T(8,128)} %get-tuple-element.22), channel_id=1, source_target_pairs={{0,1},{1,2},{2,3},{4,5},{5,6},{6,7},{8,9},{9,10},{10,11},{12,13},{... | collective-permute-start | bytes 135176 | tf_op jit(solution)/shard_map/ppermute | solution.py:882
  19.7 1.3 collective-permute-start.2
  21.3 1.5 collective-permute-done.3.past
  22.8 15.8 %collective-permute-done.1.low.rest_1_ = f32[22,512]{1,0:T(8,128)S(1)} collective-permute-done((f32[22,512]{1,0:T(8,128)}, f32[22,512]{1,0:T(8,128)S(1)}, u32[]{:S(2)}, u32[]{:S(2)}) %collective-permute-start.1) | collective-permute-done | bytes 45088 | tf_op jit(solution)/shard_map/ppermute | solution.py:882
  38.6 0.9 collective-permute-done.2.high.rest_2_
  39.5 0.7 broadcast_in_dim.21.freq
  40.1 6.4 %forward_prep.1.rest_0_ = f32[8,1,600,128]{3,2,1,0:T(8,128)} custom-call(s32[4]{0:T(128)} %pad_add_fusion.me_ref, f32[1,2,512,512]{3,2,1,0:T(8,128)} %before.3, f32[1,2,256,512]{3,2,1,0:T(8,128)} %collective-permute-done.other, f32[1,2,512,512]{3,2,1,0:T(8,128)} %before.3, f32[22,512]{1,0:T(8,128)} %copy-done.6, f32[22,512]{1,0:T(8,128)} %copy-done.7, ...), custom_call_target="tpu_custom_call" | custom-call | tf_op jit(solution)/shard_map/forward_prep/pallas_call | solution.py:333
  46.5 3.3 %copy.13.refs_0_ = f32[8,1,600,128]{3,2,1,0:T(8,128)} copy(f32[8,1,600,128]{3,2,1,0:T(8,128)} %forward_prep.1.rest_0_) | data formatting | bytes 4915200
  49.9 1.4 copy-done.2
  51.3 3.8 %all-to-all-start.1 = ((f32[8,1,600,128]{3,2,1,0:T(8,128)}), f32[8,1,600,128]{3,2,1,0:T(8,128)S(1)}, u32[]{:S(2)}, u32[]{:S(2)}) async-start(f32[8,1,600,128]{3,2,1,0:T(8,128)} %follow.3), calls=%async_computation.1 | async-start | bytes 4915200 | tf_op jit(solution)/shard_map/all_to_all | solution.py:141
  55.1 6.9 %adjoint_prep.3.refs_0_ = f32[8,3,288,128]{3,2,1,0:T(8,128)} custom-call(s32[4]{0:T(128)} %pad_add_fusion.me_ref, f32[2,5,256,512]{3,2,1,0:T(8,128)} %x_ref.3, bf16[2,256,256]{2,1,0:T(8,128)(2,1)} %constant.82.w_ref, f32[8,1,600,128]{3,2,1,0:T(8,128)} %forward_prep.1.rest_0_, f32[22,512]{1,0:T(8,128)} %copy-done.6, f32[22,512]{1,0:T(8,128)} %copy-done.7), custom_call_target="tpu_custom_call" | custom-call | tf_op jit(solution)/shard_map/adjoint_prep/pallas_call | solution.py:260
  62.0 23.6 %all-to-all-done.1.rest_0_.rest_1_.refs_1_ = f32[8,1,600,128]{3,2,1,0:T(8,128)S(1)} async-done(((f32[8,1,600,128]{3,2,1,0:T(8,128)}), f32[8,1,600,128]{3,2,1,0:T(8,128)S(1)}, u32[]{:S(2)}, u32[]{:S(2)}) %all-to-all-start.1) | async-done | bytes 2457632 | tf_op jit(solution)/shard_map/all_to_all | solution.py:141
  85.6 1.4 copy-done.1
  87.1 3.7 %all-to-all-start.2 = ((f32[8,3,288,128]{3,2,1,0:T(8,128)}), f32[8,3,288,128]{3,2,1,0:T(8,128)S(1)}, u32[]{:S(2)}, u32[]{:S(2)}) async-start(f32[8,3,288,128]{3,2,1,0:T(8,128)} %follow.4), calls=%async_computation.2 | async-start | bytes 7077888 | tf_op jit(solution)/shard_map/all_to_all | solution.py:141
  90.7 5.3 %forward_physical.1 = (f32[2,2,64,16,128]{4,3,2,1,0:T(8,128)}, f32[2,64,1,128]{3,2,1,0:T(1,128)}, f32[2,2,2,64,128]{4,3,2,1,0:T(8,128)}, s32[68]{0:T(128)}) custom-call(s32[4]{0:T(128)} %pad_add_fusion.me_ref, f32[8,1,600,128]{3,2,1,0:T(8,128)} %copy-done.1, f32[8,1,600,128]{3,2,1,0:T(8,128)} %copy-done.1), custom_call_target="tpu_custom_call" | custom-call | tf_op jit(solution)/shard_map/forward_physical/pallas_call | solution.py:461
  96.0 11.2 %march.2 = (f32[8,2,256,128]{3,2,1,0:T(8,128)}, f32[2,2,64,16,128]{4,3,2,1,0:T(8,128)}, f32[2,2,64,128]{3,2,1,0:T(8,128)}, f32[64,128]{1,0:T(8,128)}) custom-call(s32[68]{0:T(128)} %get-tuple-element.26.table_ref, f32[8,2,256,128]{3,2,1,0:T(8,128)} %copy-done.2, f32[2,2,64,16,128]{4,3,2,1,0:T(8,128)} %get-tuple-element.27.rest_1_, ...), custom_call_target="tpu_custom_call" | custom-call | tf_op jit(solution)/shard_map/march/pallas_call | solution.py:656
  107.7 1.1 collective-permute-done.4
  108.7 0.8 add.62
  109.5 2.8 %collective-permute-start.7 = (f32[64,128]{1,0:T(8,128)S(1)}, f32[64,128]{1,0:T(8,128)S(1)}, u32[]{:S(2)}, u32[]{:S(2)}) collective-permute-start(f32[64,128]{1,0:T(8,128)S(1)} %add.62), channel_id=1, source_target_pairs={{0,24},{4,28},{8,16},{12,20},{16,8},{20,12},{24,0},{28,4},{1,25},{... | collective-permute-start | bytes 98312 | tf_op jit(solution)/shard_map/ppermute | solution.py:891
  113.0 20.8 %collective-permute-done.7 = f32[64,128]{1,0:T(8,128)S(1)} collective-permute-done((f32[64,128]{1,0:T(8,128)S(1)}, f32[64,128]{1,0:T(8,128)S(1)}, u32[]{:S(2)}, u32[]{:S(2)}) %collective-permute-start.7) | collective-permute-done | bytes 32800 | tf_op jit(solution)/shard_map/ppermute | solution.py:891
  133.8 0.6 add_add_fusion.1
  134.5 6.0 %collective-permute-start.10 = (f32[64,128]{1,0:T(8,128)}, f32[64,128]{1,0:T(8,128)}, u32[]{:S(2)}, u32[]{:S(2)}) collective-permute-start(f32[64,128]{1,0:T(8,128)} %add_add_fusion.1), channel_id=1, source_target_pairs={{0,3},{4,7},{8,11},{12,15},{16,19},{20,23},{24,27},{28,31}} | collective-permute-start | bytes 98312 | tf_op jit(solution)/shard_map/ppermute | solution.py:882
  140.5 1.9 collective-permute-start.9
  142.4 2.5 %collective-permute-start.8 = (f32[64,128]{1,0:T(8,128)}, f32[64,128]{1,0:T(8,128)}, u32[]{:S(2)}, u32[]{:S(2)}) collective-permute-start(f32[64,128]{1,0:T(8,128)} %add_add_fusion.1), channel_id=1, source_target_pairs={{0,1},{1,2},{2,3},{4,5},{5,6},{6,7},{8,9},{9,10},{10,11},{12,13},{... | collective-permute-start | bytes 98312 | tf_op jit(solution)/shard_map/ppermute | solution.py:882
  144.9 1.3 collective-permute-done.8
  146.2 1.4 add_add_fusion.rest_6_.refs_1_
  147.6 1.8 copy-done
  149.4 3.8 %all-to-all-start.4 = ((f32[8,2,256,128]{3,2,1,0:T(8,128)}), f32[8,2,256,128]{3,2,1,0:T(8,128)S(1)}, u32[]{:S(2)}, u32[]{:S(2)}) async-start(f32[8,2,256,128]{3,2,1,0:T(8,128)} %follow.5), calls=%async_computation.4 | async-start | bytes 4194304 | tf_op jit(solution)/shard_map/all_to_all | solution.py:141
  153.2 15.5 %march.3 = f32[8,3,256,128]{3,2,1,0:T(8,128)} custom-call(s32[68]{0:T(128)} %get-tuple-element.26.table_ref, f32[8,3,288,128]{3,2,1,0:T(8,128)} %copy-done, f32[2,2,64,16,128]{4,3,2,1,0:T(8,128)} %get-tuple-element.27.rest_1_, f32[2,64,1,128]{3,2,1,0:T(1,128)} %get-tuple-element.28.rest_2_, f32[8,3,288,128]{3,2,1,0:T(8,128)} %copy-done, ...), custom_call_target="tpu_custom_call" | custom-call | tf_op jit(solution)/shard_map/march/pallas_call | solution.py:656
  168.7 10.9 %all-to-all-done.4.rest_0_ = f32[8,2,256,128]{3,2,1,0:T(8,128)S(1)} async-done(((f32[8,2,256,128]{3,2,1,0:T(8,128)}), f32[8,2,256,128]{3,2,1,0:T(8,128)S(1)}, u32[]{:S(2)}, u32[]{:S(2)}) %all-to-all-start.4) | async-done | bytes 2097184 | tf_op jit(solution)/shard_map/all_to_all | solution.py:141
  179.6 1.3 copy-done.4
  180.9 3.6 %all-to-all-start.3 = ((f32[8,3,256,128]{3,2,1,0:T(8,128)}), f32[8,3,256,128]{3,2,1,0:T(8,128)S(1)}, u32[]{:S(2)}, u32[]{:S(2)}) async-start(f32[8,3,256,128]{3,2,1,0:T(8,128)} %march.3), calls=%async_computation.3 | async-start | bytes 6291456 | tf_op jit(solution)/shard_map/all_to_all | solution.py:141
  184.6 0.6 fusion.8
  185.2 6.8 %post.2 = (f32[2,5,256,512]{3,2,1,0:T(8,128)}, f32[2,256,512]{2,1,0:T(8,128)}, f32[2,512]{1,0:T(2,128)}) custom-call(s32[4]{0:T(128)} %pad_add_fusion.me_ref, f32[8,2,256,128]{3,2,1,0:T(8,128)} %copy-done.4, bf16[2,256,256]{2,1,0:T(8,128)(2,1)} %constant.96.rest_1_, f32[1,512]{1,0:T(1,128)} %bitcast.7, f32[1,512]{1,0:T(1,128)} %bitcast.6, ...), custom_call_target="tpu_custom_call" | custom-call | tf_op jit(solution)/shard_map/post/pallas_call | solution.py:811
  192.0 2.7 %collective-permute-start.13 = (f32[2,512]{1,0:T(2,128)}, f32[2,512]{1,0:T(2,128)S(1)}, u32[]{:S(2)}, u32[]{:S(2)}) collective-permute-start(f32[2,512]{1,0:T(2,128)} %get-tuple-element.35), channel_id=1, source_target_pairs={{0,3},{4,7},{8,11},{12,15},{16,19},{20,23},{24,27},{28,31}} | collective-permute-start | bytes 12296 | tf_op jit(solution)/shard_map/ppermute | solution.py:882
  194.7 1.7 collective-permute-start.12
  196.3 2.1 collective-permute-start.11
  198.5 1.5 collective-permute-done.11
  200.5 21.8 %all-to-all-done.3.rest_0_ = f32[8,3,256,128]{3,2,1,0:T(8,128)S(1)} async-done(((f32[8,3,256,128]{3,2,1,0:T(8,128)}), f32[8,3,256,128]{3,2,1,0:T(8,128)S(1)}, u32[]{:S(2)}, u32[]{:S(2)}) %all-to-all-start.3) | async-done | bytes 3145760 | tf_op jit(solution)/shard_map/all_to_all | solution.py:141
  222.4 1.6 copy-done.3
  224.0 7.9 %post.3 = f32[2,5,256,512]{3,2,1,0:T(8,128)} custom-call(s32[4]{0:T(128)} %pad_add_fusion.me_ref, f32[8,3,256,128]{3,2,1,0:T(8,128)} %copy-done.3, bf16[2,256,256]{2,1,0:T(8,128)(2,1)} %constant.96.rest_1_, f32[2,256,512]{2,1,0:T(8,128)} %get-tuple-element.34.rest_2_, f32[2,512]{1,0:T(2,128)} %add_add_fusion.2.rest_3_, ...), custom_call_target="tpu_custom_call", output_to_operand_aliasing={{}: (5, {})} | custom-call | tf_op jit(solution)/shard_map/post/pallas_call | solution.py:811
  (42 shorter events, 2.0 us)
Async XLA Ops:
  7.4 5.3 %copy-start.5 = (f32[1,2,256,512]{3,2,1,0:T(8,128)S(1)}, f32[1,2,256,512]{3,2,1,0:T(8,128)}, u32[]{:S(2)}) copy-start(f32[1,2,256,512]{3,2,1,0:T(8,128)} %constant_dynamic-slice_fusion.rest_0_) | copy-start | bytes 3145732
  7.4 42.4 %all-to-all-start = ((f32[8,2,256,128]{3,2,1,0:T(8,128)}), f32[8,2,256,128]{3,2,1,0:T(8,128)S(1)}, u32[]{:S(2)}, u32[]{:S(2)}) async-start(f32[8,2,256,128]{3,2,1,0:T(8,128)} %get-tuple-element.25), calls=%async_computation | async-start | bytes 4194304 | tf_op jit(solution)/shard_map/all_to_all | solution.py:141
  12.7 26.7 %collective-permute-start = (f32[1,2,256,512]{3,2,1,0:T(8,128)S(1)}, f32[1,2,256,512]{3,2,1,0:T(8,128)}, u32[]{:S(2)}, u32[]{:S(2)}) collective-permute-start(f32[1,2,256,512]{3,2,1,0:T(8,128)S(1)} %copy-done.5), channel_id=1, source_target_pairs={{0,1},{1,0},{2,3},{3,2},{4,5},{5,4},{6,7},{7,6},{8,9},{9,8},{10,11... | collective-permute-start | bytes 3145736 | tf_op jit(solution)/shard_map/ppermute | solution.py:916
  14.4 6.7 %copy-start.12 = (s32[512]{0:T(512)S(1)}, s32[512]{0:T(512)}, u32[]{:S(2)}) copy-start(s32[512]{0:T(512)} %param.10) | copy-start | bytes 6148
  16.1 6.7 %collective-permute-start.3 = (f32[2,512]{1,0:T(2,128)}, f32[2,512]{1,0:T(2,128)S(1)}, u32[]{:S(2)}, u32[]{:S(2)}) collective-permute-start(f32[2,512]{1,0:T(2,128)} %get-tuple-element.24), channel_id=1, source_target_pairs={{2,0},{3,1},{6,4},{7,5},{10,8},{11,9},{14,12},{15,13},{18,16},{19,... | collective-permute-start | bytes 12296 | tf_op jit(solution)/shard_map/ppermute | solution.py:882
  17.4 21.2 %collective-permute-start.1 = (f32[22,512]{1,0:T(8,128)}, f32[22,512]{1,0:T(8,128)S(1)}, u32[]{:S(2)}, u32[]{:S(2)}) collective-permute-start(f32[22,512]{1,0:T(8,128)} %get-tuple-element.22), channel_id=1, source_target_pairs={{0,1},{1,2},{2,3},{4,5},{5,6},{6,7},{8,9},{9,10},{10,11},{12,13},{... | collective-permute-start | bytes 135176 | tf_op jit(solution)/shard_map/ppermute | solution.py:882
  19.7 19.7 %collective-permute-start.2 = (f32[22,512]{1,0:T(8,128)}, f32[22,512]{1,0:T(8,128)S(1)}, u32[]{:S(2)}, u32[]{:S(2)}) collective-permute-start(f32[22,512]{1,0:T(8,128)} %get-tuple-element.23), channel_id=1, source_target_pairs={{1,0},{2,1},{3,2},{5,4},{6,5},{7,6},{9,8},{10,9},{11,10},{13,12},{... | collective-permute-start | bytes 135176 | tf_op jit(solution)/shard_map/ppermute | solution.py:882
  22.8 17.3 %copy-start.13 = (f32[2,512]{1,0:T(2,128)}, f32[2,512]{1,0:T(2,128)S(1)}, u32[]{:S(2)}) copy-start(f32[2,512]{1,0:T(2,128)S(1)} %collective-permute-done.3.past) | copy-start | bytes 12292
  38.6 1.6 copy-start.6
  39.5 0.7 copy-start.7
  49.9 1.4 copy-start.2
  51.3 34.4 %all-to-all-start.1 = ((f32[8,1,600,128]{3,2,1,0:T(8,128)}), f32[8,1,600,128]{3,2,1,0:T(8,128)S(1)}, u32[]{:S(2)}, u32[]{:S(2)}) async-start(f32[8,1,600,128]{3,2,1,0:T(8,128)} %follow.3), calls=%async_computation.1 | async-start | bytes 4915200 | tf_op jit(solution)/shard_map/all_to_all | solution.py:141
  85.6 1.4 copy-start.1
  87.1 60.6 %all-to-all-start.2 = ((f32[8,3,288,128]{3,2,1,0:T(8,128)}), f32[8,3,288,128]{3,2,1,0:T(8,128)S(1)}, u32[]{:S(2)}, u32[]{:S(2)}) async-start(f32[8,3,288,128]{3,2,1,0:T(8,128)} %follow.4), calls=%async_computation.2 | async-start | bytes 7077888 | tf_op jit(solution)/shard_map/all_to_all | solution.py:141
  107.2 1.5 collective-permute-start.4
  108.7 25.7 %copy-start.8 = (f32[64,128]{1,0:T(8,128)}, f32[64,128]{1,0:T(8,128)S(1)}, u32[]{:S(2)}) copy-start(f32[64,128]{1,0:T(8,128)S(1)} %collective-permute-done.4) | copy-start | bytes 98308
  109.5 24.3 %collective-permute-start.7 = (f32[64,128]{1,0:T(8,128)S(1)}, f32[64,128]{1,0:T(8,128)S(1)}, u32[]{:S(2)}, u32[]{:S(2)}) collective-permute-start(f32[64,128]{1,0:T(8,128)S(1)} %add.62), channel_id=1, source_target_pairs={{0,24},{4,28},{8,16},{12,20},{16,8},{20,12},{24,0},{28,4},{1,25},{... | collective-permute-start | bytes 98312 | tf_op jit(solution)/shard_map/ppermute | solution.py:891
  112.3 21.5 %collective-permute-start.6 = (f32[64,128]{1,0:T(8,128)S(1)}, f32[64,128]{1,0:T(8,128)S(1)}, u32[]{:S(2)}, u32[]{:S(2)}) collective-permute-start(f32[64,128]{1,0:T(8,128)S(1)} %add.62), channel_id=1, source_target_pairs={{0,16},{4,20},{8,24},{12,28},{16,0},{20,4},{24,8},{28,12},{1,17},{... | collective-permute-start | bytes 98312 | tf_op jit(solution)/shard_map/ppermute | solution.py:891
  112.8 21.0 %collective-permute-start.5 = (f32[64,128]{1,0:T(8,128)S(1)}, f32[64,128]{1,0:T(8,128)S(1)}, u32[]{:S(2)}, u32[]{:S(2)}) collective-permute-start(f32[64,128]{1,0:T(8,128)S(1)} %add.62), channel_id=1, source_target_pairs={{0,8},{4,12},{8,0},{12,4},{16,24},{20,28},{24,16},{28,20},{1,9},{5... | collective-permute-start | bytes 98312 | tf_op jit(solution)/shard_map/ppermute | solution.py:891
  133.8 6.7 %copy-start.9 = (f32[64,128]{1,0:T(8,128)}, f32[64,128]{1,0:T(8,128)S(1)}, u32[]{:S(2)}) copy-start(f32[64,128]{1,0:T(8,128)S(1)} %collective-permute-done.7) | copy-start | bytes 98308
  133.8 8.6 %copy-start.10 = (f32[64,128]{1,0:T(8,128)}, f32[64,128]{1,0:T(8,128)S(1)}, u32[]{:S(2)}) copy-start(f32[64,128]{1,0:T(8,128)S(1)} %collective-permute-done.6) | copy-start | bytes 98308
  133.8 8.6 %copy-start.11 = (f32[64,128]{1,0:T(8,128)}, f32[64,128]{1,0:T(8,128)S(1)}, u32[]{:S(2)}) copy-start(f32[64,128]{1,0:T(8,128)S(1)} %collective-permute-done.5) | copy-start | bytes 98308
  134.5 10.4 %collective-permute-start.10 = (f32[64,128]{1,0:T(8,128)}, f32[64,128]{1,0:T(8,128)}, u32[]{:S(2)}, u32[]{:S(2)}) collective-permute-start(f32[64,128]{1,0:T(8,128)} %add_add_fusion.1), channel_id=1, source_target_pairs={{0,3},{4,7},{8,11},{12,15},{16,19},{20,23},{24,27},{28,31}} | collective-permute-start | bytes 98312 | tf_op jit(solution)/shard_map/ppermute | solution.py:882
  140.5 4.4 %collective-permute-start.9 = (f32[64,128]{1,0:T(8,128)}, f32[64,128]{1,0:T(8,128)}, u32[]{:S(2)}, u32[]{:S(2)}) collective-permute-start(f32[64,128]{1,0:T(8,128)} %add_add_fusion.1), channel_id=1, source_target_pairs={{0,2},{1,3},{4,6},{5,7},{8,10},{9,11},{12,14},{13,15},{16,18},{17,... | collective-permute-start | bytes 98312 | tf_op jit(solution)/shard_map/ppermute | solution.py:882
  142.4 3.8 %collective-permute-start.8 = (f32[64,128]{1,0:T(8,128)}, f32[64,128]{1,0:T(8,128)}, u32[]{:S(2)}, u32[]{:S(2)}) collective-permute-start(f32[64,128]{1,0:T(8,128)} %add_add_fusion.1), channel_id=1, source_target_pairs={{0,1},{1,2},{2,3},{4,5},{5,6},{6,7},{8,9},{9,10},{10,11},{12,13},{... | collective-permute-start | bytes 98312 | tf_op jit(solution)/shard_map/ppermute | solution.py:882
  147.6 1.8 copy-start
  149.4 30.2 %all-to-all-start.4 = ((f32[8,2,256,128]{3,2,1,0:T(8,128)}), f32[8,2,256,128]{3,2,1,0:T(8,128)S(1)}, u32[]{:S(2)}, u32[]{:S(2)}) async-start(f32[8,2,256,128]{3,2,1,0:T(8,128)} %follow.5), calls=%async_computation.4 | async-start | bytes 4194304 | tf_op jit(solution)/shard_map/all_to_all | solution.py:141
  179.6 1.3 copy-start.4
  180.9 41.5 %all-to-all-start.3 = ((f32[8,3,256,128]{3,2,1,0:T(8,128)}), f32[8,3,256,128]{3,2,1,0:T(8,128)S(1)}, u32[]{:S(2)}, u32[]{:S(2)}) async-start(f32[8,3,256,128]{3,2,1,0:T(8,128)} %march.3), calls=%async_computation.3 | async-start | bytes 6291456 | tf_op jit(solution)/shard_map/all_to_all | solution.py:141
  192.0 6.5 %collective-permute-start.13 = (f32[2,512]{1,0:T(2,128)}, f32[2,512]{1,0:T(2,128)S(1)}, u32[]{:S(2)}, u32[]{:S(2)}) collective-permute-start(f32[2,512]{1,0:T(2,128)} %get-tuple-element.35), channel_id=1, source_target_pairs={{0,3},{4,7},{8,11},{12,15},{16,19},{20,23},{24,27},{28,31}} | collective-permute-start | bytes 12296 | tf_op jit(solution)/shard_map/ppermute | solution.py:882
  194.7 3.8 %collective-permute-start.12 = (f32[2,512]{1,0:T(2,128)}, f32[2,512]{1,0:T(2,128)S(1)}, u32[]{:S(2)}, u32[]{:S(2)}) collective-permute-start(f32[2,512]{1,0:T(2,128)} %get-tuple-element.35), channel_id=1, source_target_pairs={{0,2},{1,3},{4,6},{5,7},{8,10},{9,11},{12,14},{13,15},{16,18},{17,... | collective-permute-start | bytes 12296 | tf_op jit(solution)/shard_map/ppermute | solution.py:882
  196.3 3.6 %collective-permute-start.11 = (f32[2,512]{1,0:T(2,128)}, f32[2,512]{1,0:T(2,128)S(1)}, u32[]{:S(2)}, u32[]{:S(2)}) collective-permute-start(f32[2,512]{1,0:T(2,128)} %get-tuple-element.35), channel_id=1, source_target_pairs={{0,1},{1,2},{2,3},{4,5},{5,6},{6,7},{8,9},{9,10},{10,11},{12,13},{... | collective-permute-start | bytes 12296 | tf_op jit(solution)/shard_map/ppermute | solution.py:882
  222.4 1.6 copy-start.3

commit v3 on v2

--- a/solution.py
+++ b/solution.py
@@ -16,11 +16,13 @@
 COUPLING = 0.5
 HIGHEST = lax.Precision.HIGHEST
 ROW_BLOCKS = ("wall", "ckpt")
-VMEM = pltpu.CompilerParams(vmem_limit_bytes=56 * 1024 * 1024)
+VMEM = pltpu.CompilerParams(vmem_limit_bytes=64 * 1024 * 1024)
 F32 = jnp.float32
-CHUNKS = ((0, 2), (3, 4, 1))
+COST = pl.CostEstimate(flops=1, bytes_accessed=1, transcendentals=0)
+CHUNKS = ((0, 2, 3), (4, 1))
 INWARD = (True, True)
-STORED = True
+STORED = False
+WINDOW = 4
 OUTWARD = (True, True)
 
 
@@ -136,15 +138,25 @@
             return [jax.ShapeDtypeStruct((group, count, length, LANES), F32)]
         return [jax.ShapeDtypeStruct((count, length, LANES), F32)] * group
 
-    def exchange(self):
+    def exchange(self, earlier=()):
         if self.whole:
-            return Pieces(True, [lax.all_to_all(self.arrays[0], "mode", 0, 0, tiled=True)])
+            array = after(self.arrays[0], *earlier)
+            return Pieces(True, [lax.all_to_all(array, "mode", 0, 0, tiled=True)])
         group = len(self.arrays)
-        moved = [
-            lax.ppermute(self.arrays[k], "mode", [(i, i ^ k) for i in range(group)])
-            for k in range(1, group)
-        ]
-        return Pieces(False, [self.arrays[0]] + moved)
+        moved = list(self.arrays)
+        for n, k in enumerate(partners(group)):
+            array = after(moved[k], *earlier[n : n + 1])
+            moved[k] = lax.ppermute(array, "mode", [(i, i ^ k) for i in range(group)])
+        return Pieces(False, moved)
+
+    def in_order(self):
+        if self.whole:
+            return list(self.arrays)
+        return [self.arrays[k] for k in partners(len(self.arrays))]
+
+
+def partners(group):
+    return sorted(range(1, group), key=lambda k: (-bin(k >> 1).count("1"), k & 1, k))
 
 
 def field_at(fields):
@@ -268,6 +280,7 @@
         ),
         out_shape=out_shape,
         compiler_params=VMEM,
+        cost_estimate=COST,
         name="adjoint_prep",
     )(*operands)
     return Pieces(whole, arrays[: len(shapes)]), arrays[len(shapes) :]
@@ -276,7 +289,8 @@
 def forward_prep_kernel(
     sz, whole, chunk, me_ref, own, other, before, low, high, past, ends, freq, w_ref, *rest
 ):
-    outs, (planes, rims) = piece_refs(rest, whole, sz.group)
+    outs, (done, planes, rims) = piece_refs(rest, whole, sz.group)
+    done[...] = jnp.zeros_like(done)
     here = me_ref[1]
     body = slice(8, 8 + sz.block_rows)
     for g in range(sz.lane_groups):
@@ -341,17 +355,19 @@
                 pl.BlockSpec((1, 2, 8, sz.slots), lambda i, me: (0, 0, before, 0)),
             ]
             + [pl.BlockSpec(x.shape, lambda i, me, zeros=(0,) * x.ndim: zeros) for x in rest],
-            out_specs=Pieces(whole, shapes).specs(sz.group),
+            out_specs=Pieces(whole, shapes).specs(sz.group)
+            + [pl.BlockSpec((8, LANES), lambda i, me: (0, 0))],
             scratch_shapes=[
                 pltpu.VMEM((2, sz.lane_groups, sz.block_rows + 16, 2 * LANES), F32),
                 pltpu.VMEM((len(chunk), 2, 2, sz.lane_groups, sz.group, 2 * LANES), F32),
             ],
         ),
-        out_shape=shapes,
+        out_shape=shapes + [jax.ShapeDtypeStruct((8, LANES), F32)],
         compiler_params=VMEM,
+        cost_estimate=COST,
         name="forward_prep",
     )(me, forward, other, forward, *rest)
-    return Pieces(whole, arrays)
+    return Pieces(whole, arrays[:-1]), arrays[-1]
 
 
 def frequency(sz, table_ref, whole, k, j):
@@ -484,6 +500,7 @@
             jax.ShapeDtypeStruct((sz.group * sz.blocks + 4,), jnp.int32),
         ],
         compiler_params=VMEM,
+        cost_estimate=COST,
         name="forward_physical",
     )(me, *pieces.arrays, *pieces.arrays)
 
@@ -584,20 +601,24 @@
     last = table_ref[count + 3].astype(F32)
     near = rims[step, 0].reshape(2 * NF, LANES) * jnp.where(low, 1.0 - first, 1.0 - last)
     if not running:
-        pair_rims_out[0] = near.reshape(2, NF, LANES)
-        body = middle[:, :, 8 : 8 + sz.half, :]
-        pair_out[0] = body
-        value = jnp.sum(body, axis=2)
-        value = value + swap(value)
+
+        def sums_of():
+            pair_rims_out[0] = near.reshape(2, NF, LANES)
+            body = middle[:, :, 8 : 8 + sz.half, :]
+            pair_out[0] = body
+            value = jnp.sum(body, axis=2)
+            return value + swap(value)
 
         @pl.when(step == 0)
         def _():
+            value = sums_of()
             freq = lax.broadcasted_iota(jnp.int32, value.shape, 1)
             rate = 2.0 / NF * ((freq + NF // 2) % NF - NF // 2).astype(F32)
             sums[...] = rate * value
 
-        @pl.when(step != 0)
+        @pl.when(step == 1)
         def _():
+            value = sums_of()
             turned = dot3(jnp.concatenate([value[0], value[1]], axis=1), w_ref)
             re, im = sums[0] + turned[:, :LANES], sums[1] + turned[:, LANES:]
             total = jnp.where(low_half((NF, LANES)), re, im)
@@ -627,7 +648,9 @@
         return pl.BlockSpec(x.shape, lambda i, t, zeros=(0,) * len(x.shape): zeros)
 
     def by_field(shape):
-        return pl.BlockSpec((1,) + shape, lambda i, t, zeros=(0,) * len(shape): (i,) + zeros)
+        return pl.BlockSpec(
+            (1,) + shape, lambda i, t, zeros=(0,) * len(shape): (jnp.minimum(i, 1),) + zeros
+        )
 
     body = Pieces(pieces.whole, Pieces.shapes(pieces.whole, sz.group, fields, sz.body))
     in_specs = body.specs(sz.group) + [constant(phys), constant(next_phys)]
@@ -648,7 +671,7 @@
         operands += rims
         for shape in (full, (2, NF, LANES)):
             out_specs.append(by_field(shape))
-            out_shape.append(jax.ShapeDtypeStruct((fields,) + shape, F32))
+            out_shape.append(jax.ShapeDtypeStruct((2,) + shape, F32))
         out_shape.append(jax.ShapeDtypeStruct((NF, LANES), F32))
         out_specs.append(constant(out_shape[-1]))
     padded = pltpu.VMEM((2, NF, sz.padded, LANES), F32)
@@ -674,6 +697,7 @@
         ),
         out_shape=out_shape,
         compiler_params=VMEM,
+        cost_estimate=COST,
         name="march",
     )(*operands)
     return Pieces(whole_out, arrays[: len(shapes)]), arrays[len(shapes) :]
@@ -764,7 +788,7 @@
                 for c in range(2):
                     source[g, :, c * LANES : (c + 1) * LANES] = halves[c] * alpha_ref[:, at]
 
-            @pl.when(pl.program_id(0) != 0)
+            @pl.when(pl.program_id(0) == 1)
             def _():
                 both = [
                     source[g, :, c * LANES : (c + 1) * LANES] + halves[c] * beta_ref[:, at]
@@ -820,25 +844,13 @@
         out_shape=out_shape,
         input_output_aliases=aliases,
         compiler_params=VMEM,
+        cost_estimate=COST,
         name="post",
     )(*operands)
 
 
-def follow(pieces, earlier):
-    def kernel(*refs):
-        pass
-
-    count = len(pieces.arrays)
-    in_place = pl.BlockSpec(memory_space=pl.ANY)
-    arrays = pl.pallas_call(
-        kernel,
-        in_specs=[in_place] * (count + len(earlier)),
-        out_specs=[in_place] * count,
-        out_shape=[jax.ShapeDtypeStruct(x.shape, x.dtype) for x in pieces.arrays],
-        input_output_aliases={n: n for n in range(count)},
-        name="follow",
-    )(*pieces.arrays, *earlier)
-    return Pieces(pieces.whole, arrays)
+def after(value, *earlier):
+    return lax.optimization_barrier((value, *earlier))[0]
 
 
 def edge_kernel(first_ref, last_ref, before, middle, after, token, low, high, past):
@@ -915,7 +927,8 @@
     other = lax.dynamic_slice_in_dim(forward, (1 - here) * sz.block_rows, sz.block_rows, 2)
     moved = lax.ppermute(other, "ckpt", [(i, stations - 1 - i) for i in range(stations)])
 
-    pieces, (ends,) = adjoint_prep(sz, INWARD[0], place, adjoint, spread, chunks[0], other)
+    free = jnp.zeros_like(place) if INWARD[0] else place
+    pieces, (ends,) = adjoint_prep(sz, INWARD[0], free, adjoint, spread, chunks[0], spread)
     inward = [pieces.exchange()]
 
     low, high, past = edge_rows(sz, adjoint, forward, ends)
@@ -930,14 +943,15 @@
     freq = freq_index.reshape(sz.blocks, NK)[:, :1].astype(F32)
     freq = jnp.pad(jnp.broadcast_to(freq, (sz.blocks, LANES)), ((0, 8 - sz.blocks), (0, 0)))
 
-    stored = forward_prep(
+    stored, done = forward_prep(
         sz, STORED, place, forward, moved, (low, high, past), ends, freq, spread, chunks[0]
     )
     pieces, _ = adjoint_prep(
-        sz, INWARD[1], place, adjoint, spread, chunks[1], stored.arrays[0], (low, high)
+        sz, INWARD[1], place, adjoint, spread, chunks[1], done, (low, high)
     )
-    stored = follow(stored, inward[0].arrays).exchange()
-    inward.append(follow(pieces, stored.arrays).exchange())
+    stored = stored.exchange(inward[0].arrays if STORED else ())
+    got = stored.in_order()
+    inward.append(pieces.exchange(got if INWARD[1] else (got + got[-1:] * WINDOW)[WINDOW:]))
 
     phys, next_phys, rims, table = forward_physical(sz, place, stored, len(chunks[0]))
     turn = halves_of(complex_lanes(beta_matrix()))
@@ -945,9 +959,13 @@
         sz, OUTWARD[0], table, inward[0], phys, next_phys, len(chunks[0]), (rims, turn)
     )
     start, whole = nearer_sum_by_pairs(total, "mode")
+    got = inward[1].in_order()
+    if OUTWARD[0]:
+        back = [out.exchange([whole, *got])]
+    else:
+        back = [out.exchange([whole] * len(out.arrays))]
     start = start + nearer_sum(whole)
     running = (pair, pair_rims, start, turn)
-    back = [follow(out, [start, inward[1].arrays[0]]).exchange()]
     out, _ = march(
         sz,
         OUTWARD[1],
@@ -959,7 +977,8 @@
         row_scale=row_scale,
         running=running,
     )
-    back.append(out.exchange())
+    got = back[0].in_order()
+    back.append(out.exchange(got if OUTWARD[1] else (got + got[-1:] * WINDOW)[WINDOW:]))
 
     tri = jnp.asarray(np.tril(np.ones((sz.block_rows, sz.block_rows))), jnp.bfloat16)
     out, sums, total = post(

time: 233 us -> 197 us (0.85)
  waiting for transfers between devices: 99.2 us -> 66.6 us
  local copies, waits for them, and re-layouts: 14 us -> 3.01 us
  starting transfers between devices: 47.6 us -> 56 us
    all_to_all x5 -> x4, waiting for transfers between devices: 56.4 us -> 20.4 us  [exchange(): return Pieces(True, [lax.all_to_all(array, 'mode', 0, 0, tiled=True)])]
    ppermute x0 -> x7, waiting for transfers between devices: none -> 19.2 us  [exchange(): moved[k] = lax.ppermute(array, 'mode', [(i, i ^ k) for i in range(group)])]
    ppermute x3, waiting for transfers between devices: 20.8 us -> 5.37 us  [nearer_sum_by_pairs(): other = lax.ppermute(both, axis, [(i, i ^ k) for i in range(count)])]
    unnamed x29 -> x14, local copies, waits for them, and re-layouts: 10.9 us -> 1.63 us
    ppermute x0 -> x7, starting transfers between devices: none -> 7.57 us  [exchange(): moved[k] = lax.ppermute(array, 'mode', [(i, i ^ k) for i in range(group)])]
    all_to_all x5 -> x4, starting transfers between devices: 20.2 us -> 18.5 us  [exchange(): return Pieces(True, [lax.all_to_all(array, 'mode', 0, 0, tiled=True)])]
  transfers between devices with their start and end apart: 19 -> 25, of which waited for: 10 -> 12; matrix products, arithmetic and copies ran while one was open for 4% -> 2% of each run, Pallas kernels for 23% -> 28%
where the time goes in v3:
time: 197 us; the launch traced here: 196 us
  Pallas kernels  66.8 us (34%)
  waiting for transfers between devices  66.6 us (34%)
  starting transfers between devices  56 us (28%)
  other arithmetic  3.41 us (2%)
  local copies, waits for them, and re-layouts  3.01 us (2%)
    pallas_call x2, Pallas kernels, march(): pl.pallas_call(functools.partial(march_kernel, sz, pieces.whole, whole_ou...  26.7 us
    ppermute x9, starting transfers between devices, shifted(): lax.ppermute(value, axes, [(i, i + step) for i in range(count) if 0 <= i...  23.4 us
    ppermute x9, waiting for transfers between devices, shifted(): lax.ppermute(value, axes, [(i, i + step) for i in range(count) if 0 <= i...  20.5 us
    all_to_all x4, waiting for transfers between devices, exchange(): return Pieces(True, [lax.all_to_all(array, 'mode', 0, 0, tiled=True)])  20.4 us
    ppermute x7, waiting for transfers between devices, exchange(): moved[k] = lax.ppermute(array, 'mode', [(i, i ^ k) for i in range(group)])  19.2 us
    all_to_all x4, starting transfers between devices, exchange(): return Pieces(True, [lax.all_to_all(array, 'mode', 0, 0, tiled=True)])  18.5 us
    pallas_call x2, Pallas kernels, post(): pl.pallas_call(functools.partial(post_kernel, sz, pieces.whole, running,...  14.5 us
    pallas_call x2, Pallas kernels, adjoint_prep(): pl.pallas_call(functools.partial(adjoint_prep_kernel, sz, whole, with_rim...  11.4 us
  transfers between devices with their start and end apart: 25, of which 12 were waited for; matrix products, arithmetic and copies ran while one was open for 2% of the time, Pallas kernels for 28%

profile of v3, /device:TPU:0, one launch (start us, length us, event | category | flops | bytes accessed | tf_op | source)
XLA Modules:
  0.0 196.0 jit_solution(9654360924415847416)
XLA Ops:
  0.6 6.2 %adjoint_prep.2 = (f32[8,3,256,128]{3,2,1,0:T(8,128)}, f32[3,4,4,8,256]{4,3,2,1,0:T(8,128)}) custom-call(s32[4]{0:T(128)} %broadcast_9_me_ref.2.me_ref, f32[2,5,256,512]{3,2,1,0:T(8,128)} %x_ref.3, bf16[2,256,256]{2,1,0:T(8,128)(2,1)} %constant.83.w_ref.rest_0_, bf16[2,256,256]{2,1,0:T(8,128)(2,1)} %constant.83.w_ref.rest_0_), custom_call_target="tpu_custom_call" | custom-call | flops 1 | bytes 1 | tf_op jit(solution)/shard_map/adjoint_prep/pallas_call | solution.py:272
  6.7 5.3 %all-to-all-start.1 = ((f32[8,3,256,128]{3,2,1,0:T(8,128)}), f32[8,3,256,128]{3,2,1,0:T(8,128)}, u32[]{:S(2)}, u32[]{:S(2)}) async-start(f32[8,3,256,128]{3,2,1,0:T(8,128)} %get-tuple-element.50), calls=%async_computation.1 | async-start | bytes 6291456 | tf_op jit(solution)/shard_map/all_to_all | solution.py:144
  12.1 2.4 %collective-permute-start = (f32[1,2,256,512]{3,2,1,0:T(8,128)S(1)}, f32[1,2,256,512]{3,2,1,0:T(8,128)S(1)}, u32[]{:S(2)}, u32[]{:S(2)}) collective-permute-start(f32[1,2,256,512]{3,2,1,0:T(8,128)S(1)} %constant_dynamic-slice_fusion), channel_id=1, source_target_pairs={{0,1},{1,0},{2,3},{3,2},{4,5},{5,4},{6,7},{7,6},{8,9},{9,8},{10,11... | collective-permute-start | bytes 3145736 | tf_op jit(solution)/shard_map/ppermute | solution.py:928
  14.5 1.7 edge_rows.1
  16.2 1.3 collective-permute-start.3
  17.5 1.9 collective-permute-start.1
  19.5 1.3 collective-permute-start.2
  21.0 0.7 pad_add_fusion.me_ref
  21.7 1.3 collective-permute-done.3.past
  22.9 15.7 %collective-permute-done.1.low.rest_1_ = f32[22,512]{1,0:T(8,128)S(1)} collective-permute-done((f32[22,512]{1,0:T(8,128)}, f32[22,512]{1,0:T(8,128)S(1)}, u32[]{:S(2)}, u32[]{:S(2)}) %collective-permute-start.1) | collective-permute-done | bytes 45088 | tf_op jit(solution)/shard_map/ppermute | solution.py:894
  38.6 0.7 collective-permute-done.2.high.rest_2_
  39.4 0.6 copy-done.3
  40.0 1.0 copy-done.1
  41.0 0.7 broadcast_in_dim.21.freq
  41.6 7.3 %forward_prep.1 = (f32[1,632,128]{2,1,0:T(8,128)}, f32[1,632,128]{2,1,0:T(8,128)}, f32[1,632,128]{2,1,0:T(8,128)}, f32[1,632,128]{2,1,0:T(8,128)}, f32[1,632,128...) custom-call(s32[4]{0:T(128)} %pad_add_fusion.me_ref, ...), custom_call_target="tpu_custom_call" | custom-call | flops 1 | bytes 1 | tf_op jit(solution)/shard_map/forward_prep/pallas_call | solution.py:347
  48.9 1.7 collective-permute-start.5
  50.8 1.7 collective-permute-start.7
  52.5 2.6 %collective-permute-start.9 = (f32[1,632,128]{2,1,0:T(8,128)}, f32[1,632,128]{2,1,0:T(8,128)}, u32[]{:S(2)}, u32[]{:S(2)}) collective-permute-start(f32[1,632,128]{2,1,0:T(8,128)} %get-tuple-element.43), channel_id=1, source_target_pairs={{0,24},{4,28},{8,16},{12,20},{16,8},{20,12},{24,0},{28,4},{1,25},{... | collective-permute-start | bytes 970760 | tf_op jit(solution)/shard_map/ppermute | solution.py:149
  55.1 4.6 %collective-permute-done.5.rest_2_.rest_10_ = f32[1,632,128]{2,1,0:T(8,128)} collective-permute-done((f32[1,632,128]{2,1,0:T(8,128)}, f32[1,632,128]{2,1,0:T(8,128)}, u32[]{:S(2)}, u32[]{:S(2)}) %collective-permute-start.5) | collective-permute-done | bytes 323616 | tf_op jit(solution)/shard_map/ppermute | solution.py:149
  59.7 1.4 collective-permute-start.10
  61.1 5.3 %adjoint_prep.3 = f32[8,2,288,128]{3,2,1,0:T(8,128)} custom-call(s32[4]{0:T(128)} %pad_add_fusion.me_ref, f32[2,5,256,512]{3,2,1,0:T(8,128)} %x_ref.3, bf16[2,256,256]{2,1,0:T(8,128)(2,1)} %constant.83.w_ref.rest_0_, f32[8,128]{1,0:T(8,128)} %get-tuple-element.46.rest_0_, f32[22,512]{1,0:T(8,128)} %copy-done.2, f32[22,512]{1,0:T(8,128)} %copy-done.3), custom_call_target="tpu_custom_call" | custom-call | flops 1 | bytes 1 | tf_op jit(solution)/shard_map/adjoint_prep/pallas_call | solution.py:272
  66.4 14.6 %collective-permute-done.8.rest_5_.rest_13_ = f32[1,632,128]{2,1,0:T(8,128)} collective-permute-done((f32[1,632,128]{2,1,0:T(8,128)}, f32[1,632,128]{2,1,0:T(8,128)}, u32[]{:S(2)}, u32[]{:S(2)}) %collective-permute-start.8) | collective-permute-done | bytes 323616 | tf_op jit(solution)/shard_map/ppermute | solution.py:149
  81.0 4.4 %all-to-all-start = ((f32[8,2,288,128]{3,2,1,0:T(8,128)}), f32[8,2,288,128]{3,2,1,0:T(8,128)}, u32[]{:S(2)}, u32[]{:S(2)}) async-start(f32[8,2,288,128]{3,2,1,0:T(8,128)} %adjoint_prep.3), calls=%async_computation | async-start | bytes 4718592 | tf_op jit(solution)/shard_map/all_to_all | solution.py:144
  85.4 5.3 %forward_physical.1 = (f32[2,2,64,16,128]{4,3,2,1,0:T(8,128)}, f32[2,64,1,128]{3,2,1,0:T(1,128)}, f32[3,2,2,64,128]{4,3,2,1,0:T(8,128)}, s32[68]{0:T(128)}) custom-call(s32[4]{0:T(128)} %pad_add_fusion.me_ref, f32[1,632,128]{2,1,0:T(8,128)} %get-tuple-element.37.rest_0_.rest_8_, f32[1,632,128]{2,1,0:T(8,128)} %collective-permute-done.4.rest_1_.rest_9_, ...), custom_call_target="tpu_custom_call" | custom-call | flops 1 | bytes 1 | tf_op jit(solution)/shard_map/forward_physical/pallas_call | solution.py:477
  90.6 14.4 %march.2 = (f32[8,3,256,128]{3,2,1,0:T(8,128)}, f32[2,2,64,16,128]{4,3,2,1,0:T(8,128)}, f32[2,2,64,128]{3,2,1,0:T(8,128)}, f32[64,128]{1,0:T(8,128)}) custom-call(s32[68]{0:T(128)} %get-tuple-element.45.table_ref, f32[8,3,256,128]{3,2,1,0:T(8,128)} %all-to-all-done.1.rest_0_, f32[2,2,64,16,128]{4,3,2,1,0:T(8,128)} %get-tuple-element.48.rest_1_, ...), custom_call_target="tpu_custom_call" | custom-call | flops 1 | bytes 1 | tf_op jit(solution)/shard_map/march/pallas_call | solution.py:679
  105.0 0.6 collective-permute-start.11
  105.6 1.1 collective-permute-done.11
  106.7 0.8 add.62
  107.5 2.7 %collective-permute-start.14 = (f32[64,128]{1,0:T(8,128)S(1)}, f32[64,128]{1,0:T(8,128)S(1)}, u32[]{:S(2)}, u32[]{:S(2)}) collective-permute-start(f32[64,128]{1,0:T(8,128)S(1)} %add.62), channel_id=1, source_target_pairs={{0,24},{4,28},{8,16},{12,20},{16,8},{20,12},{24,0},{28,4},{1,25},{... | collective-permute-start | bytes 98312 | tf_op jit(solution)/shard_map/ppermute | solution.py:903
  110.9 5.0 %collective-permute-done.14 = f32[64,128]{1,0:T(8,128)S(1)} collective-permute-done((f32[64,128]{1,0:T(8,128)S(1)}, f32[64,128]{1,0:T(8,128)S(1)}, u32[]{:S(2)}, u32[]{:S(2)}) %collective-permute-start.14) | collective-permute-done | bytes 32800 | tf_op jit(solution)/shard_map/ppermute | solution.py:903
  116.3 4.5 %all-to-all-start.2 = ((f32[8,3,256,128]{3,2,1,0:T(8,128)}), f32[8,3,256,128]{3,2,1,0:T(8,128)}, u32[]{:S(2)}, u32[]{:S(2)}) async-start(f32[8,3,256,128]{3,2,1,0:T(8,128)} %get-tuple-element.56), calls=%async_computation.2 | async-start | bytes 6291456 | tf_op jit(solution)/shard_map/all_to_all | solution.py:144
  120.8 5.6 %collective-permute-start.17 = (f32[64,128]{1,0:T(8,128)S(1)}, f32[64,128]{1,0:T(8,128)S(1)}, u32[]{:S(2)}, u32[]{:S(2)}) collective-permute-start(f32[64,128]{1,0:T(8,128)S(1)} %add_add_fusion.1), channel_id=1, source_target_pairs={{0,3},{4,7},{8,11},{12,15},{16,19},{20,23},{24,27},{28,31}} | collective-permute-start | bytes 98312 | tf_op jit(solution)/shard_map/ppermute | solution.py:894
  126.4 1.3 collective-permute-start.16
  127.7 2.7 %collective-permute-start.15 = (f32[64,128]{1,0:T(8,128)S(1)}, f32[64,128]{1,0:T(8,128)S(1)}, u32[]{:S(2)}, u32[]{:S(2)}) collective-permute-start(f32[64,128]{1,0:T(8,128)S(1)} %add_add_fusion.1), channel_id=1, source_target_pairs={{0,1},{1,2},{2,3},{4,5},{5,6},{6,7},{8,9},{9,10},{10,11},{12,13},{... | collective-permute-start | bytes 98312 | tf_op jit(solution)/shard_map/ppermute | solution.py:894
  130.4 1.4 collective-permute-done.15
  131.8 0.6 add_add_fusion.rest_6_
  132.4 12.3 %march.3 = f32[8,2,256,128]{3,2,1,0:T(8,128)} custom-call(s32[68]{0:T(128)} %get-tuple-element.45.table_ref, f32[8,2,288,128]{3,2,1,0:T(8,128)} %all-to-all-done.rest_0_.rest_3_, f32[2,2,64,16,128]{4,3,2,1,0:T(8,128)} %get-tuple-element.48.rest_1_, f32[2,64,1,128]{3,2,1,0:T(1,128)} %get-tuple-element.49.rest_2_, ...), custom_call_target="tpu_custom_call" | custom-call | flops 1 | bytes 1 | tf_op jit(solution)/shard_map/march/pallas_call | solution.py:679
  144.7 14.0 %all-to-all-done.2.rest_0_ = f32[8,3,256,128]{3,2,1,0:T(8,128)} async-done(((f32[8,3,256,128]{3,2,1,0:T(8,128)}), f32[8,3,256,128]{3,2,1,0:T(8,128)}, u32[]{:S(2)}, u32[]{:S(2)}) %all-to-all-start.2) | async-done | bytes 3145760 | tf_op jit(solution)/shard_map/all_to_all | solution.py:144
  158.7 4.3 %all-to-all-start.3 = ((f32[8,2,256,128]{3,2,1,0:T(8,128)}), f32[8,2,256,128]{3,2,1,0:T(8,128)}, u32[]{:S(2)}, u32[]{:S(2)}) async-start(f32[8,2,256,128]{3,2,1,0:T(8,128)} %march.3), calls=%async_computation.3 | async-start | bytes 4194304 | tf_op jit(solution)/shard_map/all_to_all | solution.py:144
  163.1 0.6 fusion.8
  163.7 8.1 %post.2 = (f32[2,5,256,512]{3,2,1,0:T(8,128)}, f32[2,256,512]{2,1,0:T(8,128)}, f32[2,512]{1,0:T(2,128)}) custom-call(s32[4]{0:T(128)} %pad_add_fusion.me_ref, f32[8,3,256,128]{3,2,1,0:T(8,128)} %all-to-all-done.2.rest_0_, bf16[2,256,256]{2,1,0:T(8,128)(2,1)} %constant.97.rest_1_, f32[1,512]{1,0:T(1,128)} %bitcast.7, f32[1,512]{1,0:T(1,128)} %bitcast.6, ...), custom_call_target="tpu_custom_call" | custom-call | flops 1 | bytes 1 | tf_op jit(solution)/shard_map/post/pallas_call | solution.py:835
  171.8 5.6 %collective-permute-start.20 = (f32[2,512]{1,0:T(2,128)}, f32[2,512]{1,0:T(2,128)S(1)}, u32[]{:S(2)}, u32[]{:S(2)}) collective-permute-start(f32[2,512]{1,0:T(2,128)} %get-tuple-element.59), channel_id=1, source_target_pairs={{0,3},{4,7},{8,11},{12,15},{16,19},{20,23},{24,27},{28,31}} | collective-permute-start | bytes 12296 | tf_op jit(solution)/shard_map/ppermute | solution.py:894
  177.4 1.3 collective-permute-start.19
  178.7 2.5 %collective-permute-start.18 = (f32[2,512]{1,0:T(2,128)}, f32[2,512]{1,0:T(2,128)S(1)}, u32[]{:S(2)}, u32[]{:S(2)}) collective-permute-start(f32[2,512]{1,0:T(2,128)} %get-tuple-element.59), channel_id=1, source_target_pairs={{0,1},{1,2},{2,3},{4,5},{5,6},{6,7},{8,9},{9,10},{10,11},{12,13},{... | collective-permute-start | bytes 12296 | tf_op jit(solution)/shard_map/ppermute | solution.py:894
  181.2 1.5 collective-permute-done.18
  182.7 0.6 add_add_fusion.2.rest_3_
  183.3 6.4 %all-to-all-done.3.rest_0_ = f32[8,2,256,128]{3,2,1,0:T(8,128)} async-done(((f32[8,2,256,128]{3,2,1,0:T(8,128)}), f32[8,2,256,128]{3,2,1,0:T(8,128)}, u32[]{:S(2)}, u32[]{:S(2)}) %all-to-all-start.3) | async-done | bytes 2097184 | tf_op jit(solution)/shard_map/all_to_all | solution.py:144
  189.7 6.3 %post.3 = f32[2,5,256,512]{3,2,1,0:T(8,128)} custom-call(s32[4]{0:T(128)} %pad_add_fusion.me_ref, f32[8,2,256,128]{3,2,1,0:T(8,128)} %all-to-all-done.3.rest_0_, bf16[2,256,256]{2,1,0:T(8,128)(2,1)} %constant.97.rest_1_, f32[2,256,512]{2,1,0:T(8,128)} %get-tuple-element.58.rest_2_, f32[2,512]{1,0:T(2,128)} %add_add_fusion.2.rest_3_, ...), custom_call_target="tpu_custom_call", output_to_operand_aliasing={{}: (5, {})} | custom-call | flops 1 | bytes 1 | tf_op jit(solution)/shard_map/post/pallas_call | solution.py:835
  (37 shorter events, 2.3 us)
Async XLA Ops:
  6.7 5.3 %copy-start = (f32[1,2,512,512]{3,2,1,0:T(8,128)S(1)}, f32[1,2,512,512]{3,2,1,0:T(8,128)}, u32[]{:S(2)}) copy-start(f32[1,2,512,512]{3,2,1,0:T(8,128)} %before.3) | copy-start | bytes 6291460
  6.7 74.2 %all-to-all-start.1 = ((f32[8,3,256,128]{3,2,1,0:T(8,128)}), f32[8,3,256,128]{3,2,1,0:T(8,128)}, u32[]{:S(2)}, u32[]{:S(2)}) async-start(f32[8,3,256,128]{3,2,1,0:T(8,128)} %get-tuple-element.50), calls=%async_computation.1 | async-start | bytes 6291456 | tf_op jit(solution)/shard_map/all_to_all | solution.py:144
  12.1 27.2 %collective-permute-start = (f32[1,2,256,512]{3,2,1,0:T(8,128)S(1)}, f32[1,2,256,512]{3,2,1,0:T(8,128)S(1)}, u32[]{:S(2)}, u32[]{:S(2)}) collective-permute-start(f32[1,2,256,512]{3,2,1,0:T(8,128)S(1)} %constant_dynamic-slice_fusion), channel_id=1, source_target_pairs={{0,1},{1,0},{2,3},{3,2},{4,5},{5,4},{6,7},{7,6},{8,9},{9,8},{10,11... | collective-permute-start | bytes 3145736 | tf_op jit(solution)/shard_map/ppermute | solution.py:928
  14.5 6.3 %copy-start.4 = (s32[512]{0:T(512)S(1)}, s32[512]{0:T(512)}, u32[]{:S(2)}) copy-start(s32[512]{0:T(512)} %param.10) | copy-start | bytes 6148
  16.2 6.7 %collective-permute-start.3 = (f32[2,512]{1,0:T(2,128)}, f32[2,512]{1,0:T(2,128)S(1)}, u32[]{:S(2)}, u32[]{:S(2)}) collective-permute-start(f32[2,512]{1,0:T(2,128)} %get-tuple-element.36), channel_id=1, source_target_pairs={{2,0},{3,1},{6,4},{7,5},{10,8},{11,9},{14,12},{15,13},{18,16},{19,... | collective-permute-start | bytes 12296 | tf_op jit(solution)/shard_map/ppermute | solution.py:894
  17.5 21.1 %collective-permute-start.1 = (f32[22,512]{1,0:T(8,128)}, f32[22,512]{1,0:T(8,128)S(1)}, u32[]{:S(2)}, u32[]{:S(2)}) collective-permute-start(f32[22,512]{1,0:T(8,128)} %get-tuple-element.34), channel_id=1, source_target_pairs={{0,1},{1,2},{2,3},{4,5},{5,6},{6,7},{8,9},{9,10},{10,11},{12,13},{... | collective-permute-start | bytes 135176 | tf_op jit(solution)/shard_map/ppermute | solution.py:894
  19.5 19.9 %collective-permute-start.2 = (f32[22,512]{1,0:T(8,128)}, f32[22,512]{1,0:T(8,128)S(1)}, u32[]{:S(2)}, u32[]{:S(2)}) collective-permute-start(f32[22,512]{1,0:T(8,128)} %get-tuple-element.35), channel_id=1, source_target_pairs={{1,0},{2,1},{3,2},{5,4},{6,5},{7,6},{9,8},{10,9},{11,10},{13,12},{... | collective-permute-start | bytes 135176 | tf_op jit(solution)/shard_map/ppermute | solution.py:894
  22.9 16.4 %copy-start.6 = (f32[2,512]{1,0:T(2,128)}, f32[2,512]{1,0:T(2,128)S(1)}, u32[]{:S(2)}) copy-start(f32[2,512]{1,0:T(2,128)S(1)} %collective-permute-done.3.past) | copy-start | bytes 12292
  38.6 0.7 copy-start.2
  39.3 0.6 copy-start.3
  40.0 1.0 copy-start.1
  48.9 3.6 %collective-permute-start.4 = (f32[1,632,128]{2,1,0:T(8,128)}, f32[1,632,128]{2,1,0:T(8,128)}, u32[]{:S(2)}, u32[]{:S(2)}) collective-permute-start(f32[1,632,128]{2,1,0:T(8,128)} %get-tuple-element.38), channel_id=1, source_target_pairs={{0,4},{4,0},{8,12},{12,8},{16,20},{20,16},{24,28},{28,24},{1,5},{5... | collective-permute-start | bytes 970760 | tf_op jit(solution)/shard_map/ppermute | solution.py:149
  48.9 10.8 %collective-permute-start.5 = (f32[1,632,128]{2,1,0:T(8,128)}, f32[1,632,128]{2,1,0:T(8,128)}, u32[]{:S(2)}, u32[]{:S(2)}) collective-permute-start(f32[1,632,128]{2,1,0:T(8,128)} %get-tuple-element.39), channel_id=1, source_target_pairs={{0,8},{4,12},{8,0},{12,4},{16,24},{20,28},{24,16},{28,20},{1,9},{5... | collective-permute-start | bytes 970760 | tf_op jit(solution)/shard_map/ppermute | solution.py:149
  50.6 15.8 %collective-permute-start.6 = (f32[1,632,128]{2,1,0:T(8,128)}, f32[1,632,128]{2,1,0:T(8,128)}, u32[]{:S(2)}, u32[]{:S(2)}) collective-permute-start(f32[1,632,128]{2,1,0:T(8,128)} %get-tuple-element.40), channel_id=1, source_target_pairs={{0,12},{4,8},{8,4},{12,0},{16,28},{20,24},{24,20},{28,16},{1,13},{... | collective-permute-start | bytes 970760 | tf_op jit(solution)/shard_map/ppermute | solution.py:149
  50.8 15.6 %collective-permute-start.7 = (f32[1,632,128]{2,1,0:T(8,128)}, f32[1,632,128]{2,1,0:T(8,128)}, u32[]{:S(2)}, u32[]{:S(2)}) collective-permute-start(f32[1,632,128]{2,1,0:T(8,128)} %get-tuple-element.41), channel_id=1, source_target_pairs={{0,16},{4,20},{8,24},{12,28},{16,0},{20,4},{24,8},{28,12},{1,17},{... | collective-permute-start | bytes 970760 | tf_op jit(solution)/shard_map/ppermute | solution.py:149
  52.5 28.5 %collective-permute-start.8 = (f32[1,632,128]{2,1,0:T(8,128)}, f32[1,632,128]{2,1,0:T(8,128)}, u32[]{:S(2)}, u32[]{:S(2)}) collective-permute-start(f32[1,632,128]{2,1,0:T(8,128)} %get-tuple-element.42), channel_id=1, source_target_pairs={{0,20},{4,16},{8,28},{12,24},{16,4},{20,0},{24,12},{28,8},{1,21},{... | collective-permute-start | bytes 970760 | tf_op jit(solution)/shard_map/ppermute | solution.py:149
  52.5 28.5 %collective-permute-start.9 = (f32[1,632,128]{2,1,0:T(8,128)}, f32[1,632,128]{2,1,0:T(8,128)}, u32[]{:S(2)}, u32[]{:S(2)}) collective-permute-start(f32[1,632,128]{2,1,0:T(8,128)} %get-tuple-element.43), channel_id=1, source_target_pairs={{0,24},{4,28},{8,16},{12,20},{16,8},{20,12},{24,0},{28,4},{1,25},{... | collective-permute-start | bytes 970760 | tf_op jit(solution)/shard_map/ppermute | solution.py:149
  59.7 21.3 %collective-permute-start.10 = (f32[1,632,128]{2,1,0:T(8,128)}, f32[1,632,128]{2,1,0:T(8,128)}, u32[]{:S(2)}, u32[]{:S(2)}) collective-permute-start(f32[1,632,128]{2,1,0:T(8,128)} %get-tuple-element.44), channel_id=1, source_target_pairs={{0,28},{4,24},{8,20},{12,16},{16,12},{20,8},{24,4},{28,0},{1,29},{... | collective-permute-start | bytes 970760 | tf_op jit(solution)/shard_map/ppermute | solution.py:149
  81.0 35.4 %all-to-all-start = ((f32[8,2,288,128]{3,2,1,0:T(8,128)}), f32[8,2,288,128]{3,2,1,0:T(8,128)}, u32[]{:S(2)}, u32[]{:S(2)}) async-start(f32[8,2,288,128]{3,2,1,0:T(8,128)} %adjoint_prep.3), calls=%async_computation | async-start | bytes 4718592 | tf_op jit(solution)/shard_map/all_to_all | solution.py:144
  105.0 1.7 collective-permute-start.11
  107.5 8.5 %collective-permute-start.14 = (f32[64,128]{1,0:T(8,128)S(1)}, f32[64,128]{1,0:T(8,128)S(1)}, u32[]{:S(2)}, u32[]{:S(2)}) collective-permute-start(f32[64,128]{1,0:T(8,128)S(1)} %add.62), channel_id=1, source_target_pairs={{0,24},{4,28},{8,16},{12,20},{16,8},{20,12},{24,0},{28,4},{1,25},{... | collective-permute-start | bytes 98312 | tf_op jit(solution)/shard_map/ppermute | solution.py:903
  110.1 6.2 %collective-permute-start.13 = (f32[64,128]{1,0:T(8,128)S(1)}, f32[64,128]{1,0:T(8,128)S(1)}, u32[]{:S(2)}, u32[]{:S(2)}) collective-permute-start(f32[64,128]{1,0:T(8,128)S(1)} %add.62), channel_id=1, source_target_pairs={{0,16},{4,20},{8,24},{12,28},{16,0},{20,4},{24,8},{28,12},{1,17},{... | collective-permute-start | bytes 98312 | tf_op jit(solution)/shard_map/ppermute | solution.py:903
  110.6 5.7 %collective-permute-start.12 = (f32[64,128]{1,0:T(8,128)S(1)}, f32[64,128]{1,0:T(8,128)S(1)}, u32[]{:S(2)}, u32[]{:S(2)}) collective-permute-start(f32[64,128]{1,0:T(8,128)S(1)} %add.62), channel_id=1, source_target_pairs={{0,8},{4,12},{8,0},{12,4},{16,24},{20,28},{24,16},{28,20},{1,9},{5... | collective-permute-start | bytes 98312 | tf_op jit(solution)/shard_map/ppermute | solution.py:903
  116.3 42.4 %all-to-all-start.2 = ((f32[8,3,256,128]{3,2,1,0:T(8,128)}), f32[8,3,256,128]{3,2,1,0:T(8,128)}, u32[]{:S(2)}, u32[]{:S(2)}) async-start(f32[8,3,256,128]{3,2,1,0:T(8,128)} %get-tuple-element.56), calls=%async_computation.2 | async-start | bytes 6291456 | tf_op jit(solution)/shard_map/all_to_all | solution.py:144
  120.8 9.6 %collective-permute-start.17 = (f32[64,128]{1,0:T(8,128)S(1)}, f32[64,128]{1,0:T(8,128)S(1)}, u32[]{:S(2)}, u32[]{:S(2)}) collective-permute-start(f32[64,128]{1,0:T(8,128)S(1)} %add_add_fusion.1), channel_id=1, source_target_pairs={{0,3},{4,7},{8,11},{12,15},{16,19},{20,23},{24,27},{28,31}} | collective-permute-start | bytes 98312 | tf_op jit(solution)/shard_map/ppermute | solution.py:894
  126.4 4.0 %collective-permute-start.16 = (f32[64,128]{1,0:T(8,128)S(1)}, f32[64,128]{1,0:T(8,128)S(1)}, u32[]{:S(2)}, u32[]{:S(2)}) collective-permute-start(f32[64,128]{1,0:T(8,128)S(1)} %add_add_fusion.1), channel_id=1, source_target_pairs={{0,2},{1,3},{4,6},{5,7},{8,10},{9,11},{12,14},{13,15},{16,18},{17,... | collective-permute-start | bytes 98312 | tf_op jit(solution)/shard_map/ppermute | solution.py:894
  127.7 4.1 %collective-permute-start.15 = (f32[64,128]{1,0:T(8,128)S(1)}, f32[64,128]{1,0:T(8,128)S(1)}, u32[]{:S(2)}, u32[]{:S(2)}) collective-permute-start(f32[64,128]{1,0:T(8,128)S(1)} %add_add_fusion.1), channel_id=1, source_target_pairs={{0,1},{1,2},{2,3},{4,5},{5,6},{6,7},{8,9},{9,10},{10,11},{12,13},{... | collective-permute-start | bytes 98312 | tf_op jit(solution)/shard_map/ppermute | solution.py:894
  144.7 18.3 %copy-start.5 = (s32[512]{0:T(512)S(1)}, s32[512]{0:T(512)}, u32[]{:S(2)}) copy-start(s32[512]{0:T(512)} %param.10) | copy-start | bytes 6148
  158.7 31.0 %all-to-all-start.3 = ((f32[8,2,256,128]{3,2,1,0:T(8,128)}), f32[8,2,256,128]{3,2,1,0:T(8,128)}, u32[]{:S(2)}, u32[]{:S(2)}) async-start(f32[8,2,256,128]{3,2,1,0:T(8,128)} %march.3), calls=%async_computation.3 | async-start | bytes 4194304 | tf_op jit(solution)/shard_map/all_to_all | solution.py:144
  171.8 9.4 %collective-permute-start.20 = (f32[2,512]{1,0:T(2,128)}, f32[2,512]{1,0:T(2,128)S(1)}, u32[]{:S(2)}, u32[]{:S(2)}) collective-permute-start(f32[2,512]{1,0:T(2,128)} %get-tuple-element.59), channel_id=1, source_target_pairs={{0,3},{4,7},{8,11},{12,15},{16,19},{20,23},{24,27},{28,31}} | collective-permute-start | bytes 12296 | tf_op jit(solution)/shard_map/ppermute | solution.py:894
  177.4 3.8 %collective-permute-start.19 = (f32[2,512]{1,0:T(2,128)}, f32[2,512]{1,0:T(2,128)S(1)}, u32[]{:S(2)}, u32[]{:S(2)}) collective-permute-start(f32[2,512]{1,0:T(2,128)} %get-tuple-element.59), channel_id=1, source_target_pairs={{0,2},{1,3},{4,6},{5,7},{8,10},{9,11},{12,14},{13,15},{16,18},{17,... | collective-permute-start | bytes 12296 | tf_op jit(solution)/shard_map/ppermute | solution.py:894
  178.7 4.0 %collective-permute-start.18 = (f32[2,512]{1,0:T(2,128)}, f32[2,512]{1,0:T(2,128)S(1)}, u32[]{:S(2)}, u32[]{:S(2)}) collective-permute-start(f32[2,512]{1,0:T(2,128)} %get-tuple-element.59), channel_id=1, source_target_pairs={{0,1},{1,2},{2,3},{4,5},{5,6},{6,7},{8,9},{9,10},{10,11},{12,13},{... | collective-permute-start | bytes 12296 | tf_op jit(solution)/shard_map/ppermute | solution.py:894

commit v4 on v3

--- a/solution.py
+++ b/solution.py
@@ -227,11 +227,11 @@
         outs, (ends, planes) = piece_refs(rest, whole, sz.group)
     body = slice(8, 8 + sz.block_rows)
     row = 2 * field(pl.program_id(0))
-    for g in range(sz.lane_groups):
-        at = pl.ds(g * LANES, LANES)
-        planes[g, body, :] = dot3(
-            jnp.concatenate([x_ref[0, 0, :, at], x_ref[1, 0, :, at]], axis=1), w_ref
-        )
+    groups = [pl.ds(g * LANES, LANES) for g in range(sz.lane_groups)]
+    every = [jnp.concatenate([x_ref[c, 0, :, at] for c in range(2)], axis=1) for at in groups]
+    every = dot3(jnp.concatenate(every, axis=0), w_ref)
+    for g, at in enumerate(groups):
+        planes[g, body, :] = every[g * sz.block_rows : (g + 1) * sz.block_rows]
         if with_rims:
             step = low.shape[0] // 2 - 1
             planes[g, 6:8, :] = dot3(join_rows(low, (row, row + 1), step, at), w_ref)
@@ -293,10 +293,13 @@
     done[...] = jnp.zeros_like(done)
     here = me_ref[1]
     body = slice(8, 8 + sz.block_rows)
-    for g in range(sz.lane_groups):
-        at = pl.ds(g * LANES, LANES)
-        for x_ref, station in ((own, here), (other, 1 - here)):
-            planes[station, g, body, :] = dot3(join(x_ref.at[0], at), w_ref)
+    groups = [pl.ds(g * LANES, LANES) for g in range(sz.lane_groups)]
+    for x_ref, station in ((own, here), (other, 1 - here)):
+        every = dot3(jnp.concatenate([join(x_ref.at[0], at) for at in groups], axis=0), w_ref)
+        for g in range(sz.lane_groups):
+            rows = slice(g * sz.block_rows, (g + 1) * sz.block_rows)
+            planes[station, g, body, :] = every[rows]
+    for g, at in enumerate(groups):
         count = low.shape[0] - 2
         step = count // 2
         inner = here == 0
@@ -767,9 +770,10 @@
         outs = outs[1:]
     out = outs[0]
     join_pieces(sz, whole, me_ref[0], pieces, planes)
+    every = dot3(planes[...].reshape(-1, 2 * LANES), w_ref)
     for g in range(sz.lane_groups):
         at = pl.ds(g * LANES, LANES)
-        back = dot3(planes[g], w_ref)
+        back = every[g * sz.block_rows : (g + 1) * sz.block_rows]
         halves = [back[:, :LANES], back[:, LANES:]]
         for c in range(2):
             out[c, 0, :, at] = halves[c]
@@ -927,7 +931,7 @@
     other = lax.dynamic_slice_in_dim(forward, (1 - here) * sz.block_rows, sz.block_rows, 2)
     moved = lax.ppermute(other, "ckpt", [(i, stations - 1 - i) for i in range(stations)])
 
-    free = jnp.zeros_like(place) if INWARD[0] else place
+    free = jnp.asarray(np.arange(4, dtype=np.int32)) if INWARD[0] else place
     pieces, (ends,) = adjoint_prep(sz, INWARD[0], free, adjoint, spread, chunks[0], spread)
     inward = [pieces.exchange()]
 

time: 197 us -> 195 us (0.990)
  Pallas kernels: 66.8 us -> 64.1 us
    pallas_call x2, Pallas kernels: 14.5 us -> 11.7 us  [post(): pl.pallas_call(functools.partial(post_kernel, sz, pieces.whole, running,...]
  transfers between devices with their start and end apart: 25 -> 25, of which waited for: 12 -> 12; matrix products, arithmetic and copies ran while one was open for 2% -> 2% of each run, Pallas kernels for 28% -> 27%
where the time goes in v4:
time: 195 us; the launch traced here: 194 us
  waiting for transfers between devices  67.5 us (35%)
  Pallas kernels  64.1 us (33%)
  starting transfers between devices  56 us (29%)
  other arithmetic  3.41 us (2%)
  local copies, waits for them, and re-layouts  3.01 us (2%)
    pallas_call x2, Pallas kernels, march(): pl.pallas_call(functools.partial(march_kernel, sz, pieces.whole, whole_ou...  26.7 us
    ppermute x9, starting transfers between devices, shifted(): lax.ppermute(value, axes, [(i, i + step) for i in range(count) if 0 <= i...  23.4 us
    all_to_all x4, waiting for transfers between devices, exchange(): return Pieces(True, [lax.all_to_all(array, 'mode', 0, 0, tiled=True)])  21.7 us
    ppermute x9, waiting for transfers between devices, shifted(): lax.ppermute(value, axes, [(i, i + step) for i in range(count) if 0 <= i...  20.5 us
    ppermute x7, waiting for transfers between devices, exchange(): moved[k] = lax.ppermute(array, 'mode', [(i, i ^ k) for i in range(group)])  18.8 us
    all_to_all x4, starting transfers between devices, exchange(): return Pieces(True, [lax.all_to_all(array, 'mode', 0, 0, tiled=True)])  18.5 us
    pallas_call x2, Pallas kernels, adjoint_prep(): pl.pallas_call(functools.partial(adjoint_prep_kernel, sz, whole, with_rim...  11.7 us
    pallas_call x2, Pallas kernels, post(): pl.pallas_call(functools.partial(post_kernel, sz, pieces.whole, running,...  11.7 us
  transfers between devices with their start and end apart: 25, of which 12 were waited for; matrix products, arithmetic and copies ran while one was open for 2% of the time, Pallas kernels for 27%

profile of v4, /device:TPU:0, one launch (start us, length us, event | category | flops | bytes accessed | tf_op | source)
XLA Modules:
  0.0 194.4 jit_solution(17779793543191209693)
XLA Ops:
  0.6 6.0 %adjoint_prep.2 = (f32[8,3,256,128]{3,2,1,0:T(8,128)}, f32[3,4,4,8,256]{4,3,2,1,0:T(8,128)}) custom-call(s32[4]{0:T(128)} %call_exported.0.me_ref, f32[2,5,256,512]{3,2,1,0:T(8,128)} %x_ref.3, bf16[2,256,256]{2,1,0:T(8,128)(2,1)} %constant.84.w_ref.rest_0_, bf16[2,256,256]{2,1,0:T(8,128)(2,1)} %constant.84.w_ref.rest_0_), custom_call_target="tpu_custom_call" | custom-call | flops 1 | bytes 1 | tf_op jit(solution)/shard_map/adjoint_prep/pallas_call | solution.py:272
  6.6 5.3 %all-to-all-start.1 = ((f32[8,3,256,128]{3,2,1,0:T(8,128)}), f32[8,3,256,128]{3,2,1,0:T(8,128)}, u32[]{:S(2)}, u32[]{:S(2)}) async-start(f32[8,3,256,128]{3,2,1,0:T(8,128)} %get-tuple-element.50), calls=%async_computation.1 | async-start | bytes 6291456 | tf_op jit(solution)/shard_map/all_to_all | solution.py:144
  12.0 2.4 %collective-permute-start = (f32[1,2,256,512]{3,2,1,0:T(8,128)S(1)}, f32[1,2,256,512]{3,2,1,0:T(8,128)S(1)}, u32[]{:S(2)}, u32[]{:S(2)}) collective-permute-start(f32[1,2,256,512]{3,2,1,0:T(8,128)S(1)} %constant_dynamic-slice_fusion), channel_id=1, source_target_pairs={{0,1},{1,0},{2,3},{3,2},{4,5},{5,4},{6,7},{7,6},{8,9},{9,8},{10,11... | collective-permute-start | bytes 3145736 | tf_op jit(solution)/shard_map/ppermute | solution.py:932
  14.4 1.7 edge_rows.1
  16.1 1.3 collective-permute-start.3
  17.4 1.9 collective-permute-start.1
  19.3 1.3 collective-permute-start.2
  20.9 0.7 pad_add_fusion.me_ref
  21.5 1.3 collective-permute-done.3.past
  22.8 15.7 %collective-permute-done.1.low.rest_1_ = f32[22,512]{1,0:T(8,128)S(1)} collective-permute-done((f32[22,512]{1,0:T(8,128)}, f32[22,512]{1,0:T(8,128)S(1)}, u32[]{:S(2)}, u32[]{:S(2)}) %collective-permute-start.1) | collective-permute-done | bytes 45088 | tf_op jit(solution)/shard_map/ppermute | solution.py:898
  38.5 0.7 collective-permute-done.2.high.rest_2_
  39.2 0.6 copy-done.3
  39.8 1.0 copy-done.1
  40.8 0.7 broadcast_in_dim.21.freq
  41.5 7.2 %forward_prep.1 = (f32[1,632,128]{2,1,0:T(8,128)}, f32[1,632,128]{2,1,0:T(8,128)}, f32[1,632,128]{2,1,0:T(8,128)}, f32[1,632,128]{2,1,0:T(8,128)}, f32[1,632,128...) custom-call(s32[4]{0:T(128)} %pad_add_fusion.me_ref, ...), custom_call_target="tpu_custom_call" | custom-call | flops 1 | bytes 1 | tf_op jit(solution)/shard_map/forward_prep/pallas_call | solution.py:350
  48.7 1.7 collective-permute-start.5
  50.5 1.7 collective-permute-start.7
  52.3 2.6 %collective-permute-start.9 = (f32[1,632,128]{2,1,0:T(8,128)}, f32[1,632,128]{2,1,0:T(8,128)}, u32[]{:S(2)}, u32[]{:S(2)}) collective-permute-start(f32[1,632,128]{2,1,0:T(8,128)} %get-tuple-element.43), channel_id=1, source_target_pairs={{0,24},{4,28},{8,16},{12,20},{16,8},{20,12},{24,0},{28,4},{1,25},{... | collective-permute-start | bytes 970760 | tf_op jit(solution)/shard_map/ppermute | solution.py:149
  54.8 4.6 %collective-permute-done.5.rest_2_.rest_10_ = f32[1,632,128]{2,1,0:T(8,128)} collective-permute-done((f32[1,632,128]{2,1,0:T(8,128)}, f32[1,632,128]{2,1,0:T(8,128)}, u32[]{:S(2)}, u32[]{:S(2)}) %collective-permute-start.5) | collective-permute-done | bytes 323616 | tf_op jit(solution)/shard_map/ppermute | solution.py:149
  59.5 1.4 collective-permute-start.10
  60.9 5.6 %adjoint_prep.3 = f32[8,2,288,128]{3,2,1,0:T(8,128)} custom-call(s32[4]{0:T(128)} %pad_add_fusion.me_ref, f32[2,5,256,512]{3,2,1,0:T(8,128)} %x_ref.3, bf16[2,256,256]{2,1,0:T(8,128)(2,1)} %constant.84.w_ref.rest_0_, f32[8,128]{1,0:T(8,128)} %get-tuple-element.46.rest_0_, f32[22,512]{1,0:T(8,128)} %copy-done.2, f32[22,512]{1,0:T(8,128)} %copy-done.3), custom_call_target="tpu_custom_call" | custom-call | flops 1 | bytes 1 | tf_op jit(solution)/shard_map/adjoint_prep/pallas_call | solution.py:272
  66.6 14.2 %collective-permute-done.8.rest_5_.rest_13_ = f32[1,632,128]{2,1,0:T(8,128)} collective-permute-done((f32[1,632,128]{2,1,0:T(8,128)}, f32[1,632,128]{2,1,0:T(8,128)}, u32[]{:S(2)}, u32[]{:S(2)}) %collective-permute-start.8) | collective-permute-done | bytes 323616 | tf_op jit(solution)/shard_map/ppermute | solution.py:149
  80.7 4.4 %all-to-all-start = ((f32[8,2,288,128]{3,2,1,0:T(8,128)}), f32[8,2,288,128]{3,2,1,0:T(8,128)}, u32[]{:S(2)}, u32[]{:S(2)}) async-start(f32[8,2,288,128]{3,2,1,0:T(8,128)} %adjoint_prep.3), calls=%async_computation | async-start | bytes 4718592 | tf_op jit(solution)/shard_map/all_to_all | solution.py:144
  85.1 5.3 %forward_physical.1 = (f32[2,2,64,16,128]{4,3,2,1,0:T(8,128)}, f32[2,64,1,128]{3,2,1,0:T(1,128)}, f32[3,2,2,64,128]{4,3,2,1,0:T(8,128)}, s32[68]{0:T(128)}) custom-call(s32[4]{0:T(128)} %pad_add_fusion.me_ref, f32[1,632,128]{2,1,0:T(8,128)} %get-tuple-element.37.rest_0_.rest_8_, f32[1,632,128]{2,1,0:T(8,128)} %collective-permute-done.4.rest_1_.rest_9_, ...), custom_call_target="tpu_custom_call" | custom-call | flops 1 | bytes 1 | tf_op jit(solution)/shard_map/forward_physical/pallas_call | solution.py:480
  90.4 14.4 %march.2 = (f32[8,3,256,128]{3,2,1,0:T(8,128)}, f32[2,2,64,16,128]{4,3,2,1,0:T(8,128)}, f32[2,2,64,128]{3,2,1,0:T(8,128)}, f32[64,128]{1,0:T(8,128)}) custom-call(s32[68]{0:T(128)} %get-tuple-element.45.table_ref, f32[8,3,256,128]{3,2,1,0:T(8,128)} %all-to-all-done.1.rest_0_, f32[2,2,64,16,128]{4,3,2,1,0:T(8,128)} %get-tuple-element.48.rest_1_, ...), custom_call_target="tpu_custom_call" | custom-call | flops 1 | bytes 1 | tf_op jit(solution)/shard_map/march/pallas_call | solution.py:682
  104.8 0.6 collective-permute-start.11
  105.4 1.1 collective-permute-done.11
  106.5 0.8 add.62
  107.2 2.7 %collective-permute-start.14 = (f32[64,128]{1,0:T(8,128)S(1)}, f32[64,128]{1,0:T(8,128)S(1)}, u32[]{:S(2)}, u32[]{:S(2)}) collective-permute-start(f32[64,128]{1,0:T(8,128)S(1)} %add.62), channel_id=1, source_target_pairs={{0,24},{4,28},{8,16},{12,20},{16,8},{20,12},{24,0},{28,4},{1,25},{... | collective-permute-start | bytes 98312 | tf_op jit(solution)/shard_map/ppermute | solution.py:907
  110.7 5.0 %collective-permute-done.14 = f32[64,128]{1,0:T(8,128)S(1)} collective-permute-done((f32[64,128]{1,0:T(8,128)S(1)}, f32[64,128]{1,0:T(8,128)S(1)}, u32[]{:S(2)}, u32[]{:S(2)}) %collective-permute-start.14) | collective-permute-done | bytes 32800 | tf_op jit(solution)/shard_map/ppermute | solution.py:907
  116.1 4.5 %all-to-all-start.2 = ((f32[8,3,256,128]{3,2,1,0:T(8,128)}), f32[8,3,256,128]{3,2,1,0:T(8,128)}, u32[]{:S(2)}, u32[]{:S(2)}) async-start(f32[8,3,256,128]{3,2,1,0:T(8,128)} %get-tuple-element.56), calls=%async_computation.2 | async-start | bytes 6291456 | tf_op jit(solution)/shard_map/all_to_all | solution.py:144
  120.6 5.6 %collective-permute-start.17 = (f32[64,128]{1,0:T(8,128)S(1)}, f32[64,128]{1,0:T(8,128)S(1)}, u32[]{:S(2)}, u32[]{:S(2)}) collective-permute-start(f32[64,128]{1,0:T(8,128)S(1)} %add_add_fusion.1), channel_id=1, source_target_pairs={{0,3},{4,7},{8,11},{12,15},{16,19},{20,23},{24,27},{28,31}} | collective-permute-start | bytes 98312 | tf_op jit(solution)/shard_map/ppermute | solution.py:898
  126.2 1.3 collective-permute-start.16
  127.5 2.7 %collective-permute-start.15 = (f32[64,128]{1,0:T(8,128)S(1)}, f32[64,128]{1,0:T(8,128)S(1)}, u32[]{:S(2)}, u32[]{:S(2)}) collective-permute-start(f32[64,128]{1,0:T(8,128)S(1)} %add_add_fusion.1), channel_id=1, source_target_pairs={{0,1},{1,2},{2,3},{4,5},{5,6},{6,7},{8,9},{9,10},{10,11},{12,13},{... | collective-permute-start | bytes 98312 | tf_op jit(solution)/shard_map/ppermute | solution.py:898
  130.2 1.4 collective-permute-done.15
  131.6 0.6 add_add_fusion.rest_6_
  132.2 12.3 %march.3 = f32[8,2,256,128]{3,2,1,0:T(8,128)} custom-call(s32[68]{0:T(128)} %get-tuple-element.45.table_ref, f32[8,2,288,128]{3,2,1,0:T(8,128)} %all-to-all-done.rest_0_.rest_3_, f32[2,2,64,16,128]{4,3,2,1,0:T(8,128)} %get-tuple-element.48.rest_1_, f32[2,64,1,128]{3,2,1,0:T(1,128)} %get-tuple-element.49.rest_2_, ...), custom_call_target="tpu_custom_call" | custom-call | flops 1 | bytes 1 | tf_op jit(solution)/shard_map/march/pallas_call | solution.py:682
  144.5 14.0 %all-to-all-done.2.rest_0_ = f32[8,3,256,128]{3,2,1,0:T(8,128)} async-done(((f32[8,3,256,128]{3,2,1,0:T(8,128)}), f32[8,3,256,128]{3,2,1,0:T(8,128)}, u32[]{:S(2)}, u32[]{:S(2)}) %all-to-all-start.2) | async-done | bytes 3145760 | tf_op jit(solution)/shard_map/all_to_all | solution.py:144
  158.5 4.3 %all-to-all-start.3 = ((f32[8,2,256,128]{3,2,1,0:T(8,128)}), f32[8,2,256,128]{3,2,1,0:T(8,128)}, u32[]{:S(2)}, u32[]{:S(2)}) async-start(f32[8,2,256,128]{3,2,1,0:T(8,128)} %march.3), calls=%async_computation.3 | async-start | bytes 4194304 | tf_op jit(solution)/shard_map/all_to_all | solution.py:144
  162.8 0.6 fusion.8
  163.5 6.8 %post.2 = (f32[2,5,256,512]{3,2,1,0:T(8,128)}, f32[2,256,512]{2,1,0:T(8,128)}, f32[2,512]{1,0:T(2,128)}) custom-call(s32[4]{0:T(128)} %pad_add_fusion.me_ref, f32[8,3,256,128]{3,2,1,0:T(8,128)} %all-to-all-done.2.rest_0_, bf16[2,256,256]{2,1,0:T(8,128)(2,1)} %constant.98.rest_1_, f32[1,512]{1,0:T(1,128)} %bitcast.7, f32[1,512]{1,0:T(1,128)} %bitcast.6, ...), custom_call_target="tpu_custom_call" | custom-call | flops 1 | bytes 1 | tf_op jit(solution)/shard_map/post/pallas_call | solution.py:839
  170.2 5.6 %collective-permute-start.20 = (f32[2,512]{1,0:T(2,128)}, f32[2,512]{1,0:T(2,128)S(1)}, u32[]{:S(2)}, u32[]{:S(2)}) collective-permute-start(f32[2,512]{1,0:T(2,128)} %get-tuple-element.59), channel_id=1, source_target_pairs={{0,3},{4,7},{8,11},{12,15},{16,19},{20,23},{24,27},{28,31}} | collective-permute-start | bytes 12296 | tf_op jit(solution)/shard_map/ppermute | solution.py:898
  175.9 1.3 collective-permute-start.19
  177.2 2.5 %collective-permute-start.18 = (f32[2,512]{1,0:T(2,128)}, f32[2,512]{1,0:T(2,128)S(1)}, u32[]{:S(2)}, u32[]{:S(2)}) collective-permute-start(f32[2,512]{1,0:T(2,128)} %get-tuple-element.59), channel_id=1, source_target_pairs={{0,1},{1,2},{2,3},{4,5},{5,6},{6,7},{8,9},{9,10},{10,11},{12,13},{... | collective-permute-start | bytes 12296 | tf_op jit(solution)/shard_map/ppermute | solution.py:898
  179.7 1.5 collective-permute-done.18
  181.2 0.6 add_add_fusion.2.rest_3_
  181.8 7.7 %all-to-all-done.3.rest_0_ = f32[8,2,256,128]{3,2,1,0:T(8,128)} async-done(((f32[8,2,256,128]{3,2,1,0:T(8,128)}), f32[8,2,256,128]{3,2,1,0:T(8,128)}, u32[]{:S(2)}, u32[]{:S(2)}) %all-to-all-start.3) | async-done | bytes 2097184 | tf_op jit(solution)/shard_map/all_to_all | solution.py:144
  189.5 4.9 %post.3 = f32[2,5,256,512]{3,2,1,0:T(8,128)} custom-call(s32[4]{0:T(128)} %pad_add_fusion.me_ref, f32[8,2,256,128]{3,2,1,0:T(8,128)} %all-to-all-done.3.rest_0_, bf16[2,256,256]{2,1,0:T(8,128)(2,1)} %constant.98.rest_1_, f32[2,256,512]{2,1,0:T(8,128)} %get-tuple-element.58.rest_2_, f32[2,512]{1,0:T(2,128)} %add_add_fusion.2.rest_3_, ...), custom_call_target="tpu_custom_call", output_to_operand_aliasing={{}: (5, {})} | custom-call | flops 1 | bytes 1 | tf_op jit(solution)/shard_map/post/pallas_call | solution.py:839
  (37 shorter events, 2.2 us)
Async XLA Ops:
  6.6 5.3 %copy-start = (f32[1,2,512,512]{3,2,1,0:T(8,128)S(1)}, f32[1,2,512,512]{3,2,1,0:T(8,128)}, u32[]{:S(2)}) copy-start(f32[1,2,512,512]{3,2,1,0:T(8,128)} %before.3) | copy-start | bytes 6291460
  6.6 74.1 %all-to-all-start.1 = ((f32[8,3,256,128]{3,2,1,0:T(8,128)}), f32[8,3,256,128]{3,2,1,0:T(8,128)}, u32[]{:S(2)}, u32[]{:S(2)}) async-start(f32[8,3,256,128]{3,2,1,0:T(8,128)} %get-tuple-element.50), calls=%async_computation.1 | async-start | bytes 6291456 | tf_op jit(solution)/shard_map/all_to_all | solution.py:144
  12.0 27.2 %collective-permute-start = (f32[1,2,256,512]{3,2,1,0:T(8,128)S(1)}, f32[1,2,256,512]{3,2,1,0:T(8,128)S(1)}, u32[]{:S(2)}, u32[]{:S(2)}) collective-permute-start(f32[1,2,256,512]{3,2,1,0:T(8,128)S(1)} %constant_dynamic-slice_fusion), channel_id=1, source_target_pairs={{0,1},{1,0},{2,3},{3,2},{4,5},{5,4},{6,7},{7,6},{8,9},{9,8},{10,11... | collective-permute-start | bytes 3145736 | tf_op jit(solution)/shard_map/ppermute | solution.py:932
  14.4 6.3 %copy-start.4 = (s32[512]{0:T(512)S(1)}, s32[512]{0:T(512)}, u32[]{:S(2)}) copy-start(s32[512]{0:T(512)} %param.11) | copy-start | bytes 6148
  16.1 6.7 %collective-permute-start.3 = (f32[2,512]{1,0:T(2,128)}, f32[2,512]{1,0:T(2,128)S(1)}, u32[]{:S(2)}, u32[]{:S(2)}) collective-permute-start(f32[2,512]{1,0:T(2,128)} %get-tuple-element.36), channel_id=1, source_target_pairs={{2,0},{3,1},{6,4},{7,5},{10,8},{11,9},{14,12},{15,13},{18,16},{19,... | collective-permute-start | bytes 12296 | tf_op jit(solution)/shard_map/ppermute | solution.py:898
  17.4 21.1 %collective-permute-start.1 = (f32[22,512]{1,0:T(8,128)}, f32[22,512]{1,0:T(8,128)S(1)}, u32[]{:S(2)}, u32[]{:S(2)}) collective-permute-start(f32[22,512]{1,0:T(8,128)} %get-tuple-element.34), channel_id=1, source_target_pairs={{0,1},{1,2},{2,3},{4,5},{5,6},{6,7},{8,9},{9,10},{10,11},{12,13},{... | collective-permute-start | bytes 135176 | tf_op jit(solution)/shard_map/ppermute | solution.py:898
  19.3 19.9 %collective-permute-start.2 = (f32[22,512]{1,0:T(8,128)}, f32[22,512]{1,0:T(8,128)S(1)}, u32[]{:S(2)}, u32[]{:S(2)}) collective-permute-start(f32[22,512]{1,0:T(8,128)} %get-tuple-element.35), channel_id=1, source_target_pairs={{1,0},{2,1},{3,2},{5,4},{6,5},{7,6},{9,8},{10,9},{11,10},{13,12},{... | collective-permute-start | bytes 135176 | tf_op jit(solution)/shard_map/ppermute | solution.py:898
  22.8 16.4 %copy-start.6 = (f32[2,512]{1,0:T(2,128)}, f32[2,512]{1,0:T(2,128)S(1)}, u32[]{:S(2)}) copy-start(f32[2,512]{1,0:T(2,128)S(1)} %collective-permute-done.3.past) | copy-start | bytes 12292
  38.5 0.7 copy-start.2
  39.2 0.6 copy-start.3
  39.8 1.0 copy-start.1
  48.7 3.6 %collective-permute-start.4 = (f32[1,632,128]{2,1,0:T(8,128)}, f32[1,632,128]{2,1,0:T(8,128)}, u32[]{:S(2)}, u32[]{:S(2)}) collective-permute-start(f32[1,632,128]{2,1,0:T(8,128)} %get-tuple-element.38), channel_id=1, source_target_pairs={{0,4},{4,0},{8,12},{12,8},{16,20},{20,16},{24,28},{28,24},{1,5},{5... | collective-permute-start | bytes 970760 | tf_op jit(solution)/shard_map/ppermute | solution.py:149
  48.7 10.8 %collective-permute-start.5 = (f32[1,632,128]{2,1,0:T(8,128)}, f32[1,632,128]{2,1,0:T(8,128)}, u32[]{:S(2)}, u32[]{:S(2)}) collective-permute-start(f32[1,632,128]{2,1,0:T(8,128)} %get-tuple-element.39), channel_id=1, source_target_pairs={{0,8},{4,12},{8,0},{12,4},{16,24},{20,28},{24,16},{28,20},{1,9},{5... | collective-permute-start | bytes 970760 | tf_op jit(solution)/shard_map/ppermute | solution.py:149
  50.4 16.1 %collective-permute-start.6 = (f32[1,632,128]{2,1,0:T(8,128)}, f32[1,632,128]{2,1,0:T(8,128)}, u32[]{:S(2)}, u32[]{:S(2)}) collective-permute-start(f32[1,632,128]{2,1,0:T(8,128)} %get-tuple-element.40), channel_id=1, source_target_pairs={{0,12},{4,8},{8,4},{12,0},{16,28},{20,24},{24,20},{28,16},{1,13},{... | collective-permute-start | bytes 970760 | tf_op jit(solution)/shard_map/ppermute | solution.py:149
  50.5 16.0 %collective-permute-start.7 = (f32[1,632,128]{2,1,0:T(8,128)}, f32[1,632,128]{2,1,0:T(8,128)}, u32[]{:S(2)}, u32[]{:S(2)}) collective-permute-start(f32[1,632,128]{2,1,0:T(8,128)} %get-tuple-element.41), channel_id=1, source_target_pairs={{0,16},{4,20},{8,24},{12,28},{16,0},{20,4},{24,8},{28,12},{1,17},{... | collective-permute-start | bytes 970760 | tf_op jit(solution)/shard_map/ppermute | solution.py:149
  52.2 28.5 %collective-permute-start.8 = (f32[1,632,128]{2,1,0:T(8,128)}, f32[1,632,128]{2,1,0:T(8,128)}, u32[]{:S(2)}, u32[]{:S(2)}) collective-permute-start(f32[1,632,128]{2,1,0:T(8,128)} %get-tuple-element.42), channel_id=1, source_target_pairs={{0,20},{4,16},{8,28},{12,24},{16,4},{20,0},{24,12},{28,8},{1,21},{... | collective-permute-start | bytes 970760 | tf_op jit(solution)/shard_map/ppermute | solution.py:149
  52.3 28.5 %collective-permute-start.9 = (f32[1,632,128]{2,1,0:T(8,128)}, f32[1,632,128]{2,1,0:T(8,128)}, u32[]{:S(2)}, u32[]{:S(2)}) collective-permute-start(f32[1,632,128]{2,1,0:T(8,128)} %get-tuple-element.43), channel_id=1, source_target_pairs={{0,24},{4,28},{8,16},{12,20},{16,8},{20,12},{24,0},{28,4},{1,25},{... | collective-permute-start | bytes 970760 | tf_op jit(solution)/shard_map/ppermute | solution.py:149
  59.5 21.3 %collective-permute-start.10 = (f32[1,632,128]{2,1,0:T(8,128)}, f32[1,632,128]{2,1,0:T(8,128)}, u32[]{:S(2)}, u32[]{:S(2)}) collective-permute-start(f32[1,632,128]{2,1,0:T(8,128)} %get-tuple-element.44), channel_id=1, source_target_pairs={{0,28},{4,24},{8,20},{12,16},{16,12},{20,8},{24,4},{28,0},{1,29},{... | collective-permute-start | bytes 970760 | tf_op jit(solution)/shard_map/ppermute | solution.py:149
  80.7 35.4 %all-to-all-start = ((f32[8,2,288,128]{3,2,1,0:T(8,128)}), f32[8,2,288,128]{3,2,1,0:T(8,128)}, u32[]{:S(2)}, u32[]{:S(2)}) async-start(f32[8,2,288,128]{3,2,1,0:T(8,128)} %adjoint_prep.3), calls=%async_computation | async-start | bytes 4718592 | tf_op jit(solution)/shard_map/all_to_all | solution.py:144
  104.8 1.7 collective-permute-start.11
  107.2 8.5 %collective-permute-start.14 = (f32[64,128]{1,0:T(8,128)S(1)}, f32[64,128]{1,0:T(8,128)S(1)}, u32[]{:S(2)}, u32[]{:S(2)}) collective-permute-start(f32[64,128]{1,0:T(8,128)S(1)} %add.62), channel_id=1, source_target_pairs={{0,24},{4,28},{8,16},{12,20},{16,8},{20,12},{24,0},{28,4},{1,25},{... | collective-permute-start | bytes 98312 | tf_op jit(solution)/shard_map/ppermute | solution.py:907
  109.9 6.2 %collective-permute-start.13 = (f32[64,128]{1,0:T(8,128)S(1)}, f32[64,128]{1,0:T(8,128)S(1)}, u32[]{:S(2)}, u32[]{:S(2)}) collective-permute-start(f32[64,128]{1,0:T(8,128)S(1)} %add.62), channel_id=1, source_target_pairs={{0,16},{4,20},{8,24},{12,28},{16,0},{20,4},{24,8},{28,12},{1,17},{... | collective-permute-start | bytes 98312 | tf_op jit(solution)/shard_map/ppermute | solution.py:907
  110.4 5.7 %collective-permute-start.12 = (f32[64,128]{1,0:T(8,128)S(1)}, f32[64,128]{1,0:T(8,128)S(1)}, u32[]{:S(2)}, u32[]{:S(2)}) collective-permute-start(f32[64,128]{1,0:T(8,128)S(1)} %add.62), channel_id=1, source_target_pairs={{0,8},{4,12},{8,0},{12,4},{16,24},{20,28},{24,16},{28,20},{1,9},{5... | collective-permute-start | bytes 98312 | tf_op jit(solution)/shard_map/ppermute | solution.py:907
  116.1 42.4 %all-to-all-start.2 = ((f32[8,3,256,128]{3,2,1,0:T(8,128)}), f32[8,3,256,128]{3,2,1,0:T(8,128)}, u32[]{:S(2)}, u32[]{:S(2)}) async-start(f32[8,3,256,128]{3,2,1,0:T(8,128)} %get-tuple-element.56), calls=%async_computation.2 | async-start | bytes 6291456 | tf_op jit(solution)/shard_map/all_to_all | solution.py:144
  120.6 9.6 %collective-permute-start.17 = (f32[64,128]{1,0:T(8,128)S(1)}, f32[64,128]{1,0:T(8,128)S(1)}, u32[]{:S(2)}, u32[]{:S(2)}) collective-permute-start(f32[64,128]{1,0:T(8,128)S(1)} %add_add_fusion.1), channel_id=1, source_target_pairs={{0,3},{4,7},{8,11},{12,15},{16,19},{20,23},{24,27},{28,31}} | collective-permute-start | bytes 98312 | tf_op jit(solution)/shard_map/ppermute | solution.py:898
  126.2 4.0 %collective-permute-start.16 = (f32[64,128]{1,0:T(8,128)S(1)}, f32[64,128]{1,0:T(8,128)S(1)}, u32[]{:S(2)}, u32[]{:S(2)}) collective-permute-start(f32[64,128]{1,0:T(8,128)S(1)} %add_add_fusion.1), channel_id=1, source_target_pairs={{0,2},{1,3},{4,6},{5,7},{8,10},{9,11},{12,14},{13,15},{16,18},{17,... | collective-permute-start | bytes 98312 | tf_op jit(solution)/shard_map/ppermute | solution.py:898
  127.5 4.1 %collective-permute-start.15 = (f32[64,128]{1,0:T(8,128)S(1)}, f32[64,128]{1,0:T(8,128)S(1)}, u32[]{:S(2)}, u32[]{:S(2)}) collective-permute-start(f32[64,128]{1,0:T(8,128)S(1)} %add_add_fusion.1), channel_id=1, source_target_pairs={{0,1},{1,2},{2,3},{4,5},{5,6},{6,7},{8,9},{9,10},{10,11},{12,13},{... | collective-permute-start | bytes 98312 | tf_op jit(solution)/shard_map/ppermute | solution.py:898
  144.5 18.3 %copy-start.5 = (s32[512]{0:T(512)S(1)}, s32[512]{0:T(512)}, u32[]{:S(2)}) copy-start(s32[512]{0:T(512)} %param.11) | copy-start | bytes 6148
  158.5 31.0 %all-to-all-start.3 = ((f32[8,2,256,128]{3,2,1,0:T(8,128)}), f32[8,2,256,128]{3,2,1,0:T(8,128)}, u32[]{:S(2)}, u32[]{:S(2)}) async-start(f32[8,2,256,128]{3,2,1,0:T(8,128)} %march.3), calls=%async_computation.3 | async-start | bytes 4194304 | tf_op jit(solution)/shard_map/all_to_all | solution.py:144
  170.2 9.4 %collective-permute-start.20 = (f32[2,512]{1,0:T(2,128)}, f32[2,512]{1,0:T(2,128)S(1)}, u32[]{:S(2)}, u32[]{:S(2)}) collective-permute-start(f32[2,512]{1,0:T(2,128)} %get-tuple-element.59), channel_id=1, source_target_pairs={{0,3},{4,7},{8,11},{12,15},{16,19},{20,23},{24,27},{28,31}} | collective-permute-start | bytes 12296 | tf_op jit(solution)/shard_map/ppermute | solution.py:898
  175.9 3.8 %collective-permute-start.19 = (f32[2,512]{1,0:T(2,128)}, f32[2,512]{1,0:T(2,128)S(1)}, u32[]{:S(2)}, u32[]{:S(2)}) collective-permute-start(f32[2,512]{1,0:T(2,128)} %get-tuple-element.59), channel_id=1, source_target_pairs={{0,2},{1,3},{4,6},{5,7},{8,10},{9,11},{12,14},{13,15},{16,18},{17,... | collective-permute-start | bytes 12296 | tf_op jit(solution)/shard_map/ppermute | solution.py:898
  177.2 4.0 %collective-permute-start.18 = (f32[2,512]{1,0:T(2,128)}, f32[2,512]{1,0:T(2,128)S(1)}, u32[]{:S(2)}, u32[]{:S(2)}) collective-permute-start(f32[2,512]{1,0:T(2,128)} %get-tuple-element.59), channel_id=1, source_target_pairs={{0,1},{1,2},{2,3},{4,5},{5,6},{6,7},{8,9},{9,10},{10,11},{12,13},{... | collective-permute-start | bytes 12296 | tf_op jit(solution)/shard_map/ppermute | solution.py:898

commit v5 on v4

--- a/solution.py
+++ b/solution.py
@@ -229,7 +229,9 @@
     row = 2 * field(pl.program_id(0))
     groups = [pl.ds(g * LANES, LANES) for g in range(sz.lane_groups)]
     every = [jnp.concatenate([x_ref[c, 0, :, at] for c in range(2)], axis=1) for at in groups]
-    every = dot3(jnp.concatenate(every, axis=0), w_ref)
+    every = jnp.concatenate(every, axis=0)
+    if with_rims:
+        every = dot3(every, w_ref)
     for g, at in enumerate(groups):
         planes[g, body, :] = every[g * sz.block_rows : (g + 1) * sz.block_rows]
         if with_rims:
@@ -310,7 +312,7 @@
         row = jnp.where(inner, join_rows(high, (count,), 1, at), join_rows(past, (0,), 1, at))
         planes[1, g, 8 + sz.block_rows : 9 + sz.block_rows, :] = dot3(row, w_ref)
         far_low, far_high = (
-            dot3(jnp.concatenate([x_ref[c * step : (c + 1) * step, at] for c in range(2)], 1), w_ref)
+            jnp.concatenate([x_ref[c * step : (c + 1) * step, at] for c in range(2)], 1)
             for x_ref in (low, high)
         )
         for i, field in enumerate(chunk):
@@ -432,7 +434,7 @@
 def forward_kernel(sz, whole, chunk, me_ref, *rest):
     pieces, rest = piece_refs(rest, whole, sz.group)
     heads, rest = piece_refs(rest, whole, sz.group)
-    out, next_out, rims, table_ref, state, work, next_state, next_work = rest
+    w_ref, out, next_out, rims, table_ref, state, work, next_state, next_work = rest
     count = sz.group * sz.blocks
     for k in range(sz.group):
         place = k ^ me_ref[0] if whole else k
@@ -465,9 +467,12 @@
         for depth in range(2):
             base += sz.rims
             gather_rims(sz, table_ref, whole, pieces, rims.at[i, depth], base)
-
-
-def forward_physical(sz, me, pieces, chunk):
+            every = dot3(jnp.concatenate([rims[i, depth, 0], rims[i, depth, 1]], axis=1), w_ref)
+            for c in range(2):
+                rims[i, depth, c] = every[:, c * LANES : (c + 1) * LANES]
+
+
+def forward_physical(sz, me, pieces, chunk, w):
     full = (2, NF, sz.half, LANES)
     rims = (chunk, 2, 2, NF, LANES)
     if pieces.whole:
@@ -482,7 +487,9 @@
         grid_spec=pltpu.PrefetchScalarGridSpec(
             num_scalar_prefetch=1,
             grid=(1,),
-            in_specs=pieces.specs(sz.group) + heads,
+            in_specs=pieces.specs(sz.group)
+            + heads
+            + [pl.BlockSpec(w.shape, lambda i, t: (0, 0, 0))],
             out_specs=[
                 pl.BlockSpec((2,) + full, lambda i, t: (0, 0, 0, 0, 0)),
                 pl.BlockSpec((2, NF, 1, LANES), lambda i, t: (0, 0, 0, 0)),
@@ -505,7 +512,7 @@
         compiler_params=VMEM,
         cost_estimate=COST,
         name="forward_physical",
-    )(me, *pieces.arrays, *pieces.arrays)
+    )(me, *pieces.arrays, *pieces.arrays, w)
 
 
 def spread_rims(rims, state, n):
@@ -547,9 +554,9 @@
     running = row_scale is not None
     if running:
         all_rims, rest = rim_refs(rest, whole_in, sz.group)
-        pair, pair_rims, start, w_ref, *rest = rest
+        pair, pair_rims, start, w_ref, back_ref, *rest = rest
     else:
-        rims_in, w_ref, *rest = rest
+        rims_in, w_ref, spread_ref, *rest = rest
     outs, rest = piece_refs(rest, whole_out, sz.group)
     if not running:
         pair_out, pair_rims_out, total_out, *rest = rest
@@ -577,6 +584,13 @@
         couple(sz, next_state, rows, next_work, rows, next_phys, slice(0, 1), store)
 
     gather_pieces(sz, table_ref, whole_in, pieces, state, 8)
+    body = slice(8, 8 + sz.half)
+    if not running:
+        both = jnp.concatenate([state[0, :, body, :], state[1, :, body, :]], axis=2)
+        both = dot3(both.reshape(NF * sz.half, 2 * LANES), spread_ref)
+        for c in range(2):
+            lanes = slice(c * LANES, (c + 1) * LANES)
+            state[c, :, body, :] = both[:, lanes].reshape(NF, sz.half, LANES)
     near = rims[step, 0].reshape(2 * NF, LANES)
     place_edges(sz, state, near)
     advance(sz, state, work, phys.at[1], middle, 8)
@@ -607,9 +621,9 @@
 
         def sums_of():
             pair_rims_out[0] = near.reshape(2, NF, LANES)
-            body = middle[:, :, 8 : 8 + sz.half, :]
-            pair_out[0] = body
-            value = jnp.sum(body, axis=2)
+            rows = middle[:, :, body, :]
+            pair_out[0] = rows
+            value = jnp.sum(rows, axis=2)
             return value + swap(value)
 
         @pl.when(step == 0)
@@ -629,6 +643,11 @@
 
     place_edges(sz, middle, near)
     advance(sz, middle, work, phys.at[0], stepped, 0)
+    if running:
+        both = jnp.concatenate([stepped[0], stepped[1]], axis=2).reshape(NF * sz.half, 2 * LANES)
+        both = dot3(both, back_ref)
+        for c in range(2):
+            stepped[c] = both[:, c * LANES : (c + 1) * LANES].reshape(NF, sz.half, LANES)
     for k in range(sz.group):
         for j in range(sz.blocks):
             freq = frequency(sz, table_ref, whole_out, k, j)
@@ -758,7 +777,8 @@
 
 def post_kernel(sz, whole, running, row_scale, me_ref, *rest):
     pieces, rest = piece_refs(rest, whole, sz.group)
-    w_ref, rest = rest[0], rest[1:]
+    if running != "add":
+        w_ref, rest = rest[0], rest[1:]
     if running == "add":
         sums_ref, start_ref, rest = rest[0], rest[1], rest[2:]
     elif running == "make":
@@ -770,7 +790,9 @@
         outs = outs[1:]
     out = outs[0]
     join_pieces(sz, whole, me_ref[0], pieces, planes)
-    every = dot3(planes[...].reshape(-1, 2 * LANES), w_ref)
+    every = planes[...].reshape(-1, 2 * LANES)
+    if running != "add":
+        every = dot3(every, w_ref)
     for g in range(sz.lane_groups):
         at = pl.ds(g * LANES, LANES)
         back = every[g * sz.block_rows : (g + 1) * sz.block_rows]
@@ -812,7 +834,7 @@
     field = field_at(fields)
     w = halves_of(complex_lanes(span_matrix(-1) / NK))
     w_spec = pl.BlockSpec((2, 2 * LANES, 2 * LANES), lambda i, me: (0, 0, 0))
-    in_specs = pieces.specs(sz.group) + [w_spec]
+    in_specs = pieces.specs(sz.group) + [w_spec] * (running != "add")
     row_spec = pl.BlockSpec((1, sz.slots), lambda i, me: (0, 0))
     sums_spec = pl.BlockSpec((2, sz.block_rows, sz.slots), lambda i, me: (0, 0, 0))
     if running == "add":
@@ -825,7 +847,7 @@
     ]
     out_shape = [jax.ShapeDtypeStruct((2, 5, sz.block_rows, sz.slots), F32)]
     aliases = {}
-    operands = [me, *pieces.arrays, w, *extra]
+    operands = [me, *pieces.arrays, *([] if running == "add" else [w]), *extra]
     plane = pltpu.VMEM((sz.lane_groups, sz.block_rows, 2 * LANES), F32)
     if running == "make":
         out_specs.append(sums_spec)
@@ -957,10 +979,10 @@
     got = stored.in_order()
     inward.append(pieces.exchange(got if INWARD[1] else (got + got[-1:] * WINDOW)[WINDOW:]))
 
-    phys, next_phys, rims, table = forward_physical(sz, place, stored, len(chunks[0]))
+    phys, next_phys, rims, table = forward_physical(sz, place, stored, len(chunks[0]), spread)
     turn = halves_of(complex_lanes(beta_matrix()))
     out, (pair, pair_rims, total) = march(
-        sz, OUTWARD[0], table, inward[0], phys, next_phys, len(chunks[0]), (rims, turn)
+        sz, OUTWARD[0], table, inward[0], phys, next_phys, len(chunks[0]), (rims, turn, spread)
     )
     start, whole = nearer_sum_by_pairs(total, "mode")
     got = inward[1].in_order()
@@ -969,7 +991,8 @@
     else:
         back = [out.exchange([whole] * len(out.arrays))]
     start = start + nearer_sum(whole)
-    running = (pair, pair_rims, start, turn)
+    back_span = halves_of(complex_lanes(span_matrix(-1) / NK))
+    running = (pair, pair_rims, start, turn, back_span)
     out, _ = march(
         sz,
         OUTWARD[1],

time: 195 us -> 194 us (level)
  waiting for transfers between devices: 67.5 us -> 64.5 us
    pallas_call x2, Pallas kernels: 26.7 us -> 29.4 us  [march(): pl.pallas_call(functools.partial(march_kernel, sz, pieces.whole, whole_ou...]
  transfers between devices with their start and end apart: 25 -> 25, of which waited for: 12 -> 13; matrix products, arithmetic and copies ran while one was open for 2% -> 2% of each run, Pallas kernels for 27% -> 29%
where the time goes in v5:
time: 194 us; the launch traced here: 193 us
  Pallas kernels  66 us (34%)
  waiting for transfers between devices  64.5 us (33%)
  starting transfers between devices  56 us (29%)
  other arithmetic  3.41 us (2%)
  local copies, waits for them, and re-layouts  3.01 us (2%)
    pallas_call x2, Pallas kernels, march(): pl.pallas_call(functools.partial(march_kernel, sz, pieces.whole, whole_ou...  29.4 us
    ppermute x9, starting transfers between devices, shifted(): lax.ppermute(value, axes, [(i, i + step) for i in range(count) if 0 <= i...  23.4 us
    ppermute x9, waiting for transfers between devices, shifted(): lax.ppermute(value, axes, [(i, i + step) for i in range(count) if 0 <= i...  20.5 us
    all_to_all x4, waiting for transfers between devices, exchange(): return Pieces(True, [lax.all_to_all(array, 'mode', 0, 0, tiled=True)])  20.5 us
    ppermute x7, waiting for transfers between devices, exchange(): moved[k] = lax.ppermute(array, 'mode', [(i, i ^ k) for i in range(group)])  18.9 us
    all_to_all x4, starting transfers between devices, exchange(): return Pieces(True, [lax.all_to_all(array, 'mode', 0, 0, tiled=True)])  18.5 us
    pallas_call x2, Pallas kernels, adjoint_prep(): pl.pallas_call(functools.partial(adjoint_prep_kernel, sz, whole, with_rim...  11.4 us
    pallas_call x2, Pallas kernels, post(): pl.pallas_call(functools.partial(post_kernel, sz, pieces.whole, running,...  11.1 us
  transfers between devices with their start and end apart: 25, of which 13 were waited for; matrix products, arithmetic and copies ran while one was open for 2% of the time, Pallas kernels for 29%

profile of v5, /device:TPU:0, one launch (start us, length us, event | category | flops | bytes accessed | tf_op | source)
XLA Modules:
  0.0 193.1 jit_solution(8228308224092030251)
XLA Ops:
  0.6 5.8 %adjoint_prep.2 = (f32[8,3,256,128]{3,2,1,0:T(8,128)}, f32[3,4,4,8,256]{4,3,2,1,0:T(8,128)}) custom-call(s32[4]{0:T(128)} %call_exported.0.me_ref, f32[2,5,256,512]{3,2,1,0:T(8,128)} %x_ref.3, bf16[2,256,256]{2,1,0:T(8,128)(2,1)} %constant.84.w_ref.rest_0_.rest_16_.rest_5_, bf16[2,256,256]{2,1,0:T(8,128)(2,1)} %constant.84.w_ref.rest_0_.rest_16_.rest_5_), custom_call_target="tpu_custom_call" | custom-call | flops 1 | bytes 1 | tf_op jit(solution)/shard_map/adjoint_prep/pallas_call | solution.py:274
  6.3 5.3 %all-to-all-start.1 = ((f32[8,3,256,128]{3,2,1,0:T(8,128)}), f32[8,3,256,128]{3,2,1,0:T(8,128)}, u32[]{:S(2)}, u32[]{:S(2)}) async-start(f32[8,3,256,128]{3,2,1,0:T(8,128)} %get-tuple-element.50), calls=%async_computation.1 | async-start | bytes 6291456 | tf_op jit(solution)/shard_map/all_to_all | solution.py:144
  11.7 2.4 %collective-permute-start = (f32[1,2,256,512]{3,2,1,0:T(8,128)S(1)}, f32[1,2,256,512]{3,2,1,0:T(8,128)S(1)}, u32[]{:S(2)}, u32[]{:S(2)}) collective-permute-start(f32[1,2,256,512]{3,2,1,0:T(8,128)S(1)} %constant_dynamic-slice_fusion), channel_id=1, source_target_pairs={{0,1},{1,0},{2,3},{3,2},{4,5},{5,4},{6,7},{7,6},{8,9},{9,8},{10,11... | collective-permute-start | bytes 3145736 | tf_op jit(solution)/shard_map/ppermute | solution.py:954
  14.1 1.7 edge_rows.1
  15.8 1.3 collective-permute-start.3
  17.1 1.9 collective-permute-start.1
  19.0 1.3 collective-permute-start.2
  20.6 0.7 pad_add_fusion.me_ref
  21.3 1.3 collective-permute-done.3.past
  22.5 15.7 %collective-permute-done.1.low.rest_1_ = f32[22,512]{1,0:T(8,128)S(1)} collective-permute-done((f32[22,512]{1,0:T(8,128)}, f32[22,512]{1,0:T(8,128)S(1)}, u32[]{:S(2)}, u32[]{:S(2)}) %collective-permute-start.1) | collective-permute-done | bytes 45088 | tf_op jit(solution)/shard_map/ppermute | solution.py:920
  38.2 0.7 collective-permute-done.2.high.rest_2_
  39.6 1.0 copy-done.1
  40.6 0.7 broadcast_in_dim.21.freq
  41.2 6.2 %forward_prep.1 = (f32[1,632,128]{2,1,0:T(8,128)}, f32[1,632,128]{2,1,0:T(8,128)}, f32[1,632,128]{2,1,0:T(8,128)}, f32[1,632,128]{2,1,0:T(8,128)}, f32[1,632,128...) custom-call(s32[4]{0:T(128)} %pad_add_fusion.me_ref, ...), custom_call_target="tpu_custom_call" | custom-call | flops 1 | bytes 1 | tf_op jit(solution)/shard_map/forward_prep/pallas_call | solution.py:352
  47.4 1.7 collective-permute-start.5
  49.3 1.7 collective-permute-start.7
  51.0 2.6 %collective-permute-start.9 = (f32[1,632,128]{2,1,0:T(8,128)}, f32[1,632,128]{2,1,0:T(8,128)}, u32[]{:S(2)}, u32[]{:S(2)}) collective-permute-start(f32[1,632,128]{2,1,0:T(8,128)} %get-tuple-element.43), channel_id=1, source_target_pairs={{0,24},{4,28},{8,16},{12,20},{16,8},{20,12},{24,0},{28,4},{1,25},{... | collective-permute-start | bytes 970760 | tf_op jit(solution)/shard_map/ppermute | solution.py:149
  53.6 4.7 %collective-permute-done.5.rest_2_.rest_10_ = f32[1,632,128]{2,1,0:T(8,128)} collective-permute-done((f32[1,632,128]{2,1,0:T(8,128)}, f32[1,632,128]{2,1,0:T(8,128)}, u32[]{:S(2)}, u32[]{:S(2)}) %collective-permute-start.5) | collective-permute-done | bytes 323616 | tf_op jit(solution)/shard_map/ppermute | solution.py:149
  58.2 1.4 collective-permute-start.10
  59.6 5.6 %adjoint_prep.3 = f32[8,2,288,128]{3,2,1,0:T(8,128)} custom-call(s32[4]{0:T(128)} %pad_add_fusion.me_ref, f32[2,5,256,512]{3,2,1,0:T(8,128)} %x_ref.3, bf16[2,256,256]{2,1,0:T(8,128)(2,1)} %constant.84.w_ref.rest_0_.rest_16_.rest_5_, f32[8,128]{1,0:T(8,128)} %get-tuple-element.46.rest_0_, f32[22,512]{1,0:T(8,128)} %copy-done.2, f32[22,512]{1,0:T(8,128)} %copy-done.3), custom_call_target="tpu_custom_call" | custom-call | flops 1 | bytes 1 | tf_op jit(solution)/shard_map/adjoint_prep/pallas_call | solution.py:274
  65.3 14.2 %collective-permute-done.8.rest_5_.rest_13_ = f32[1,632,128]{2,1,0:T(8,128)} collective-permute-done((f32[1,632,128]{2,1,0:T(8,128)}, f32[1,632,128]{2,1,0:T(8,128)}, u32[]{:S(2)}, u32[]{:S(2)}) %collective-permute-start.8) | collective-permute-done | bytes 323616 | tf_op jit(solution)/shard_map/ppermute | solution.py:149
  79.5 4.4 %all-to-all-start = ((f32[8,2,288,128]{3,2,1,0:T(8,128)}), f32[8,2,288,128]{3,2,1,0:T(8,128)}, u32[]{:S(2)}, u32[]{:S(2)}) async-start(f32[8,2,288,128]{3,2,1,0:T(8,128)} %adjoint_prep.3), calls=%async_computation | async-start | bytes 4718592 | tf_op jit(solution)/shard_map/all_to_all | solution.py:144
  83.9 6.2 %forward_physical.1 = (f32[2,2,64,16,128]{4,3,2,1,0:T(8,128)}, f32[2,64,1,128]{3,2,1,0:T(1,128)}, f32[3,2,2,64,128]{4,3,2,1,0:T(8,128)}, s32[68]{0:T(128)}) custom-call(s32[4]{0:T(128)} %pad_add_fusion.me_ref, f32[1,632,128]{2,1,0:T(8,128)} %get-tuple-element.37.rest_0_.rest_8_, f32[1,632,128]{2,1,0:T(8,128)} %collective-permute-done.4.rest_1_.rest_9_, ...), custom_call_target="tpu_custom_call" | custom-call | flops 1 | bytes 1 | tf_op jit(solution)/shard_map/forward_physical/pallas_call | solution.py:485
  90.1 15.8 %march.2 = (f32[8,3,256,128]{3,2,1,0:T(8,128)}, f32[2,2,64,16,128]{4,3,2,1,0:T(8,128)}, f32[2,2,64,128]{3,2,1,0:T(8,128)}, f32[64,128]{1,0:T(8,128)}) custom-call(s32[68]{0:T(128)} %get-tuple-element.45.table_ref, f32[8,3,256,128]{3,2,1,0:T(8,128)} %all-to-all-done.1.rest_0_, f32[2,2,64,16,128]{4,3,2,1,0:T(8,128)} %get-tuple-element.48.rest_1_, ...), custom_call_target="tpu_custom_call" | custom-call | flops 1 | bytes 1 | tf_op jit(solution)/shard_map/march/pallas_call | solution.py:701
  105.9 0.6 collective-permute-start.11
  106.6 1.1 collective-permute-done.11
  107.6 0.8 add.62
  108.4 2.7 %collective-permute-start.14 = (f32[64,128]{1,0:T(8,128)S(1)}, f32[64,128]{1,0:T(8,128)S(1)}, u32[]{:S(2)}, u32[]{:S(2)}) collective-permute-start(f32[64,128]{1,0:T(8,128)S(1)} %add.62), channel_id=1, source_target_pairs={{0,24},{4,28},{8,16},{12,20},{16,8},{20,12},{24,0},{28,4},{1,25},{... | collective-permute-start | bytes 98312 | tf_op jit(solution)/shard_map/ppermute | solution.py:929
  111.9 2.3 %collective-permute-done.14 = f32[64,128]{1,0:T(8,128)S(1)} collective-permute-done((f32[64,128]{1,0:T(8,128)S(1)}, f32[64,128]{1,0:T(8,128)S(1)}, u32[]{:S(2)}, u32[]{:S(2)}) %collective-permute-start.14) | collective-permute-done | bytes 32800 | tf_op jit(solution)/shard_map/ppermute | solution.py:929
  114.2 0.8 collective-permute-done.13
  115.5 4.5 %all-to-all-start.2 = ((f32[8,3,256,128]{3,2,1,0:T(8,128)}), f32[8,3,256,128]{3,2,1,0:T(8,128)}, u32[]{:S(2)}, u32[]{:S(2)}) async-start(f32[8,3,256,128]{3,2,1,0:T(8,128)} %get-tuple-element.56), calls=%async_computation.2 | async-start | bytes 6291456 | tf_op jit(solution)/shard_map/all_to_all | solution.py:144
  120.0 5.6 %collective-permute-start.17 = (f32[64,128]{1,0:T(8,128)S(1)}, f32[64,128]{1,0:T(8,128)S(1)}, u32[]{:S(2)}, u32[]{:S(2)}) collective-permute-start(f32[64,128]{1,0:T(8,128)S(1)} %add_add_fusion.1), channel_id=1, source_target_pairs={{0,3},{4,7},{8,11},{12,15},{16,19},{20,23},{24,27},{28,31}} | collective-permute-start | bytes 98312 | tf_op jit(solution)/shard_map/ppermute | solution.py:920
  125.6 1.3 collective-permute-start.16
  126.9 2.7 %collective-permute-start.15 = (f32[64,128]{1,0:T(8,128)S(1)}, f32[64,128]{1,0:T(8,128)S(1)}, u32[]{:S(2)}, u32[]{:S(2)}) collective-permute-start(f32[64,128]{1,0:T(8,128)S(1)} %add_add_fusion.1), channel_id=1, source_target_pairs={{0,1},{1,2},{2,3},{4,5},{5,6},{6,7},{8,9},{9,10},{10,11},{12,13},{... | collective-permute-start | bytes 98312 | tf_op jit(solution)/shard_map/ppermute | solution.py:920
  129.6 1.4 collective-permute-done.15
  131.0 0.6 add_add_fusion.rest_6_
  131.6 13.6 %march.3 = f32[8,2,256,128]{3,2,1,0:T(8,128)} custom-call(s32[68]{0:T(128)} %get-tuple-element.45.table_ref, f32[8,2,288,128]{3,2,1,0:T(8,128)} %all-to-all-done.rest_0_.rest_3_, f32[2,2,64,16,128]{4,3,2,1,0:T(8,128)} %get-tuple-element.48.rest_1_, f32[2,64,1,128]{3,2,1,0:T(1,128)} %get-tuple-element.49.rest_2_, ...), custom_call_target="tpu_custom_call" | custom-call | flops 1 | bytes 1 | tf_op jit(solution)/shard_map/march/pallas_call | solution.py:701
  145.2 12.7 %all-to-all-done.2.rest_0_ = f32[8,3,256,128]{3,2,1,0:T(8,128)} async-done(((f32[8,3,256,128]{3,2,1,0:T(8,128)}), f32[8,3,256,128]{3,2,1,0:T(8,128)}, u32[]{:S(2)}, u32[]{:S(2)}) %all-to-all-start.2) | async-done | bytes 3145760 | tf_op jit(solution)/shard_map/all_to_all | solution.py:144
  157.9 4.3 %all-to-all-start.3 = ((f32[8,2,256,128]{3,2,1,0:T(8,128)}), f32[8,2,256,128]{3,2,1,0:T(8,128)}, u32[]{:S(2)}, u32[]{:S(2)}) async-start(f32[8,2,256,128]{3,2,1,0:T(8,128)} %march.3), calls=%async_computation.3 | async-start | bytes 4194304 | tf_op jit(solution)/shard_map/all_to_all | solution.py:144
  162.2 0.6 fusion.8
  162.8 6.8 %post.2 = (f32[2,5,256,512]{3,2,1,0:T(8,128)}, f32[2,256,512]{2,1,0:T(8,128)}, f32[2,512]{1,0:T(2,128)}) custom-call(s32[4]{0:T(128)} %pad_add_fusion.me_ref, f32[8,3,256,128]{3,2,1,0:T(8,128)} %all-to-all-done.2.rest_0_, bf16[2,256,256]{2,1,0:T(8,128)(2,1)} %constant.98.rest_8_.rest_1_, f32[1,512]{1,0:T(1,128)} %bitcast.7, f32[1,512]{1,0:T(1,128)} %bitcast.6, ...), custom_call_target="tpu_custom_call" | custom-call | flops 1 | bytes 1 | tf_op jit(solution)/shard_map/post/pallas_call | solution.py:861
  169.6 5.6 %collective-permute-start.20 = (f32[2,512]{1,0:T(2,128)}, f32[2,512]{1,0:T(2,128)S(1)}, u32[]{:S(2)}, u32[]{:S(2)}) collective-permute-start(f32[2,512]{1,0:T(2,128)} %get-tuple-element.59), channel_id=1, source_target_pairs={{0,3},{4,7},{8,11},{12,15},{16,19},{20,23},{24,27},{28,31}} | collective-permute-start | bytes 12296 | tf_op jit(solution)/shard_map/ppermute | solution.py:920
  175.2 1.3 collective-permute-start.19
  176.5 2.5 %collective-permute-start.18 = (f32[2,512]{1,0:T(2,128)}, f32[2,512]{1,0:T(2,128)S(1)}, u32[]{:S(2)}, u32[]{:S(2)}) collective-permute-start(f32[2,512]{1,0:T(2,128)} %get-tuple-element.59), channel_id=1, source_target_pairs={{0,1},{1,2},{2,3},{4,5},{5,6},{6,7},{8,9},{9,10},{10,11},{12,13},{... | collective-permute-start | bytes 12296 | tf_op jit(solution)/shard_map/ppermute | solution.py:920
  179.0 1.5 collective-permute-done.18
  180.5 0.6 add_add_fusion.2.rest_2_
  181.1 7.7 %all-to-all-done.3.rest_0_ = f32[8,2,256,128]{3,2,1,0:T(8,128)} async-done(((f32[8,2,256,128]{3,2,1,0:T(8,128)}), f32[8,2,256,128]{3,2,1,0:T(8,128)}, u32[]{:S(2)}, u32[]{:S(2)}) %all-to-all-start.3) | async-done | bytes 2097184 | tf_op jit(solution)/shard_map/all_to_all | solution.py:144
  188.9 4.3 %post.3 = f32[2,5,256,512]{3,2,1,0:T(8,128)} custom-call(s32[4]{0:T(128)} %pad_add_fusion.me_ref, f32[8,2,256,128]{3,2,1,0:T(8,128)} %all-to-all-done.3.rest_0_, f32[2,256,512]{2,1,0:T(8,128)} %get-tuple-element.58.rest_1_, f32[2,512]{1,0:T(2,128)} %add_add_fusion.2.rest_2_, f32[2,5,256,512]{3,2,1,0:T(8,128)} %get-tuple-element.60.rest_3_), custom_call_target="tpu_custom_call", output_to_operand_aliasing={{}: (4, {})} | custom-call | flops 1 | bytes 1 | tf_op jit(solution)/shard_map/post/pallas_call | solution.py:861
  (37 shorter events, 3.0 us)
Async XLA Ops:
  6.3 5.3 %copy-start = (f32[1,2,512,512]{3,2,1,0:T(8,128)S(1)}, f32[1,2,512,512]{3,2,1,0:T(8,128)}, u32[]{:S(2)}) copy-start(f32[1,2,512,512]{3,2,1,0:T(8,128)} %before.3) | copy-start | bytes 6291460
  6.3 73.2 %all-to-all-start.1 = ((f32[8,3,256,128]{3,2,1,0:T(8,128)}), f32[8,3,256,128]{3,2,1,0:T(8,128)}, u32[]{:S(2)}, u32[]{:S(2)}) async-start(f32[8,3,256,128]{3,2,1,0:T(8,128)} %get-tuple-element.50), calls=%async_computation.1 | async-start | bytes 6291456 | tf_op jit(solution)/shard_map/all_to_all | solution.py:144
  11.7 27.2 %collective-permute-start = (f32[1,2,256,512]{3,2,1,0:T(8,128)S(1)}, f32[1,2,256,512]{3,2,1,0:T(8,128)S(1)}, u32[]{:S(2)}, u32[]{:S(2)}) collective-permute-start(f32[1,2,256,512]{3,2,1,0:T(8,128)S(1)} %constant_dynamic-slice_fusion), channel_id=1, source_target_pairs={{0,1},{1,0},{2,3},{3,2},{4,5},{5,4},{6,7},{7,6},{8,9},{9,8},{10,11... | collective-permute-start | bytes 3145736 | tf_op jit(solution)/shard_map/ppermute | solution.py:954
  14.1 6.3 %copy-start.4 = (s32[512]{0:T(512)S(1)}, s32[512]{0:T(512)}, u32[]{:S(2)}) copy-start(s32[512]{0:T(512)} %param.11) | copy-start | bytes 6148
  15.8 6.7 %collective-permute-start.3 = (f32[2,512]{1,0:T(2,128)}, f32[2,512]{1,0:T(2,128)S(1)}, u32[]{:S(2)}, u32[]{:S(2)}) collective-permute-start(f32[2,512]{1,0:T(2,128)} %get-tuple-element.36), channel_id=1, source_target_pairs={{2,0},{3,1},{6,4},{7,5},{10,8},{11,9},{14,12},{15,13},{18,16},{19,... | collective-permute-start | bytes 12296 | tf_op jit(solution)/shard_map/ppermute | solution.py:920
  17.1 21.1 %collective-permute-start.1 = (f32[22,512]{1,0:T(8,128)}, f32[22,512]{1,0:T(8,128)S(1)}, u32[]{:S(2)}, u32[]{:S(2)}) collective-permute-start(f32[22,512]{1,0:T(8,128)} %get-tuple-element.34), channel_id=1, source_target_pairs={{0,1},{1,2},{2,3},{4,5},{5,6},{6,7},{8,9},{9,10},{10,11},{12,13},{... | collective-permute-start | bytes 135176 | tf_op jit(solution)/shard_map/ppermute | solution.py:920
  19.0 19.9 %collective-permute-start.2 = (f32[22,512]{1,0:T(8,128)}, f32[22,512]{1,0:T(8,128)S(1)}, u32[]{:S(2)}, u32[]{:S(2)}) collective-permute-start(f32[22,512]{1,0:T(8,128)} %get-tuple-element.35), channel_id=1, source_target_pairs={{1,0},{2,1},{3,2},{5,4},{6,5},{7,6},{9,8},{10,9},{11,10},{13,12},{... | collective-permute-start | bytes 135176 | tf_op jit(solution)/shard_map/ppermute | solution.py:920
  22.5 16.4 %copy-start.6 = (f32[2,512]{1,0:T(2,128)}, f32[2,512]{1,0:T(2,128)S(1)}, u32[]{:S(2)}) copy-start(f32[2,512]{1,0:T(2,128)S(1)} %collective-permute-done.3.past) | copy-start | bytes 12292
  38.2 0.7 copy-start.2
  38.9 0.6 copy-start.3
  39.6 1.0 copy-start.1
  47.4 3.6 %collective-permute-start.4 = (f32[1,632,128]{2,1,0:T(8,128)}, f32[1,632,128]{2,1,0:T(8,128)}, u32[]{:S(2)}, u32[]{:S(2)}) collective-permute-start(f32[1,632,128]{2,1,0:T(8,128)} %get-tuple-element.38), channel_id=1, source_target_pairs={{0,4},{4,0},{8,12},{12,8},{16,20},{20,16},{24,28},{28,24},{1,5},{5... | collective-permute-start | bytes 970760 | tf_op jit(solution)/shard_map/ppermute | solution.py:149
  47.4 10.8 %collective-permute-start.5 = (f32[1,632,128]{2,1,0:T(8,128)}, f32[1,632,128]{2,1,0:T(8,128)}, u32[]{:S(2)}, u32[]{:S(2)}) collective-permute-start(f32[1,632,128]{2,1,0:T(8,128)} %get-tuple-element.39), channel_id=1, source_target_pairs={{0,8},{4,12},{8,0},{12,4},{16,24},{20,28},{24,16},{28,20},{1,9},{5... | collective-permute-start | bytes 970760 | tf_op jit(solution)/shard_map/ppermute | solution.py:149
  49.2 16.1 %collective-permute-start.6 = (f32[1,632,128]{2,1,0:T(8,128)}, f32[1,632,128]{2,1,0:T(8,128)}, u32[]{:S(2)}, u32[]{:S(2)}) collective-permute-start(f32[1,632,128]{2,1,0:T(8,128)} %get-tuple-element.40), channel_id=1, source_target_pairs={{0,12},{4,8},{8,4},{12,0},{16,28},{20,24},{24,20},{28,16},{1,13},{... | collective-permute-start | bytes 970760 | tf_op jit(solution)/shard_map/ppermute | solution.py:149
  49.3 16.0 %collective-permute-start.7 = (f32[1,632,128]{2,1,0:T(8,128)}, f32[1,632,128]{2,1,0:T(8,128)}, u32[]{:S(2)}, u32[]{:S(2)}) collective-permute-start(f32[1,632,128]{2,1,0:T(8,128)} %get-tuple-element.41), channel_id=1, source_target_pairs={{0,16},{4,20},{8,24},{12,28},{16,0},{20,4},{24,8},{28,12},{1,17},{... | collective-permute-start | bytes 970760 | tf_op jit(solution)/shard_map/ppermute | solution.py:149
  51.0 28.5 %collective-permute-start.8 = (f32[1,632,128]{2,1,0:T(8,128)}, f32[1,632,128]{2,1,0:T(8,128)}, u32[]{:S(2)}, u32[]{:S(2)}) collective-permute-start(f32[1,632,128]{2,1,0:T(8,128)} %get-tuple-element.42), channel_id=1, source_target_pairs={{0,20},{4,16},{8,28},{12,24},{16,4},{20,0},{24,12},{28,8},{1,21},{... | collective-permute-start | bytes 970760 | tf_op jit(solution)/shard_map/ppermute | solution.py:149
  51.0 28.5 %collective-permute-start.9 = (f32[1,632,128]{2,1,0:T(8,128)}, f32[1,632,128]{2,1,0:T(8,128)}, u32[]{:S(2)}, u32[]{:S(2)}) collective-permute-start(f32[1,632,128]{2,1,0:T(8,128)} %get-tuple-element.43), channel_id=1, source_target_pairs={{0,24},{4,28},{8,16},{12,20},{16,8},{20,12},{24,0},{28,4},{1,25},{... | collective-permute-start | bytes 970760 | tf_op jit(solution)/shard_map/ppermute | solution.py:149
  58.2 21.3 %collective-permute-start.10 = (f32[1,632,128]{2,1,0:T(8,128)}, f32[1,632,128]{2,1,0:T(8,128)}, u32[]{:S(2)}, u32[]{:S(2)}) collective-permute-start(f32[1,632,128]{2,1,0:T(8,128)} %get-tuple-element.44), channel_id=1, source_target_pairs={{0,28},{4,24},{8,20},{12,16},{16,12},{20,8},{24,4},{28,0},{1,29},{... | collective-permute-start | bytes 970760 | tf_op jit(solution)/shard_map/ppermute | solution.py:149
  79.5 36.0 %all-to-all-start = ((f32[8,2,288,128]{3,2,1,0:T(8,128)}), f32[8,2,288,128]{3,2,1,0:T(8,128)}, u32[]{:S(2)}, u32[]{:S(2)}) async-start(f32[8,2,288,128]{3,2,1,0:T(8,128)} %adjoint_prep.3), calls=%async_computation | async-start | bytes 4718592 | tf_op jit(solution)/shard_map/all_to_all | solution.py:144
  105.9 1.7 collective-permute-start.11
  108.4 5.8 %collective-permute-start.14 = (f32[64,128]{1,0:T(8,128)S(1)}, f32[64,128]{1,0:T(8,128)S(1)}, u32[]{:S(2)}, u32[]{:S(2)}) collective-permute-start(f32[64,128]{1,0:T(8,128)S(1)} %add.62), channel_id=1, source_target_pairs={{0,24},{4,28},{8,16},{12,20},{16,8},{20,12},{24,0},{28,4},{1,25},{... | collective-permute-start | bytes 98312 | tf_op jit(solution)/shard_map/ppermute | solution.py:929
  111.1 3.9 %collective-permute-start.13 = (f32[64,128]{1,0:T(8,128)S(1)}, f32[64,128]{1,0:T(8,128)S(1)}, u32[]{:S(2)}, u32[]{:S(2)}) collective-permute-start(f32[64,128]{1,0:T(8,128)S(1)} %add.62), channel_id=1, source_target_pairs={{0,16},{4,20},{8,24},{12,28},{16,0},{20,4},{24,8},{28,12},{1,17},{... | collective-permute-start | bytes 98312 | tf_op jit(solution)/shard_map/ppermute | solution.py:929
  111.6 3.9 %collective-permute-start.12 = (f32[64,128]{1,0:T(8,128)S(1)}, f32[64,128]{1,0:T(8,128)S(1)}, u32[]{:S(2)}, u32[]{:S(2)}) collective-permute-start(f32[64,128]{1,0:T(8,128)S(1)} %add.62), channel_id=1, source_target_pairs={{0,8},{4,12},{8,0},{12,4},{16,24},{20,28},{24,16},{28,20},{1,9},{5... | collective-permute-start | bytes 98312 | tf_op jit(solution)/shard_map/ppermute | solution.py:929
  115.5 42.4 %all-to-all-start.2 = ((f32[8,3,256,128]{3,2,1,0:T(8,128)}), f32[8,3,256,128]{3,2,1,0:T(8,128)}, u32[]{:S(2)}, u32[]{:S(2)}) async-start(f32[8,3,256,128]{3,2,1,0:T(8,128)} %get-tuple-element.56), calls=%async_computation.2 | async-start | bytes 6291456 | tf_op jit(solution)/shard_map/all_to_all | solution.py:144
  120.0 9.6 %collective-permute-start.17 = (f32[64,128]{1,0:T(8,128)S(1)}, f32[64,128]{1,0:T(8,128)S(1)}, u32[]{:S(2)}, u32[]{:S(2)}) collective-permute-start(f32[64,128]{1,0:T(8,128)S(1)} %add_add_fusion.1), channel_id=1, source_target_pairs={{0,3},{4,7},{8,11},{12,15},{16,19},{20,23},{24,27},{28,31}} | collective-permute-start | bytes 98312 | tf_op jit(solution)/shard_map/ppermute | solution.py:920
  125.6 4.0 %collective-permute-start.16 = (f32[64,128]{1,0:T(8,128)S(1)}, f32[64,128]{1,0:T(8,128)S(1)}, u32[]{:S(2)}, u32[]{:S(2)}) collective-permute-start(f32[64,128]{1,0:T(8,128)S(1)} %add_add_fusion.1), channel_id=1, source_target_pairs={{0,2},{1,3},{4,6},{5,7},{8,10},{9,11},{12,14},{13,15},{16,18},{17,... | collective-permute-start | bytes 98312 | tf_op jit(solution)/shard_map/ppermute | solution.py:920
  126.9 4.1 %collective-permute-start.15 = (f32[64,128]{1,0:T(8,128)S(1)}, f32[64,128]{1,0:T(8,128)S(1)}, u32[]{:S(2)}, u32[]{:S(2)}) collective-permute-start(f32[64,128]{1,0:T(8,128)S(1)} %add_add_fusion.1), channel_id=1, source_target_pairs={{0,1},{1,2},{2,3},{4,5},{5,6},{6,7},{8,9},{9,10},{10,11},{12,13},{... | collective-permute-start | bytes 98312 | tf_op jit(solution)/shard_map/ppermute | solution.py:920
  145.2 17.1 %copy-start.5 = (s32[512]{0:T(512)S(1)}, s32[512]{0:T(512)}, u32[]{:S(2)}) copy-start(s32[512]{0:T(512)} %param.11) | copy-start | bytes 6148
  157.9 31.0 %all-to-all-start.3 = ((f32[8,2,256,128]{3,2,1,0:T(8,128)}), f32[8,2,256,128]{3,2,1,0:T(8,128)}, u32[]{:S(2)}, u32[]{:S(2)}) async-start(f32[8,2,256,128]{3,2,1,0:T(8,128)} %march.3), calls=%async_computation.3 | async-start | bytes 4194304 | tf_op jit(solution)/shard_map/all_to_all | solution.py:144
  169.6 9.4 %collective-permute-start.20 = (f32[2,512]{1,0:T(2,128)}, f32[2,512]{1,0:T(2,128)S(1)}, u32[]{:S(2)}, u32[]{:S(2)}) collective-permute-start(f32[2,512]{1,0:T(2,128)} %get-tuple-element.59), channel_id=1, source_target_pairs={{0,3},{4,7},{8,11},{12,15},{16,19},{20,23},{24,27},{28,31}} | collective-permute-start | bytes 12296 | tf_op jit(solution)/shard_map/ppermute | solution.py:920
  175.2 3.8 %collective-permute-start.19 = (f32[2,512]{1,0:T(2,128)}, f32[2,512]{1,0:T(2,128)S(1)}, u32[]{:S(2)}, u32[]{:S(2)}) collective-permute-start(f32[2,512]{1,0:T(2,128)} %get-tuple-element.59), channel_id=1, source_target_pairs={{0,2},{1,3},{4,6},{5,7},{8,10},{9,11},{12,14},{13,15},{16,18},{17,... | collective-permute-start | bytes 12296 | tf_op jit(solution)/shard_map/ppermute | solution.py:920
  176.5 4.0 %collective-permute-start.18 = (f32[2,512]{1,0:T(2,128)}, f32[2,512]{1,0:T(2,128)S(1)}, u32[]{:S(2)}, u32[]{:S(2)}) collective-permute-start(f32[2,512]{1,0:T(2,128)} %get-tuple-element.59), channel_id=1, source_target_pairs={{0,1},{1,2},{2,3},{4,5},{5,6},{6,7},{8,9},{9,10},{10,11},{12,13},{... | collective-permute-start | bytes 12296 | tf_op jit(solution)/shard_map/ppermute | solution.py:920

commit v6 on v5

--- a/solution.py
+++ b/solution.py
@@ -218,10 +218,9 @@
         put_rows(sz, out, place + depth * sz.rims, rows)
 
 
-def adjoint_prep_kernel(sz, whole, with_rims, field, me_ref, x_ref, w_ref, *rest):
-    _, *rest = rest
+def adjoint_prep_kernel(sz, whole, with_rims, field, me_ref, x_ref, _, *rest):
     if with_rims:
-        low, high, *rest = rest
+        w_ref, low, high, *rest = rest
         outs, (planes,) = piece_refs(rest, whole, sz.group)
     else:
         outs, (ends, planes) = piece_refs(rest, whole, sz.group)
@@ -259,14 +258,14 @@
     shapes = Pieces.shapes(whole, sz.group, count, sz.body + (2 * sz.rims if with_rims else 0))
     in_specs = [
         pl.BlockSpec((2, 1, sz.block_rows, sz.slots), lambda i, me: (0, field(i), 0, 0)),
-        pl.BlockSpec(w.shape, lambda i, me: (0, 0, 0)),
         pl.BlockSpec(memory_space=pl.ANY),
     ]
-    operands = [me, adjoint, w, after]
+    operands = [me, adjoint, after]
     out_specs, out_shape = Pieces(whole, shapes).specs(sz.group), list(shapes)
     if with_rims:
+        in_specs.append(pl.BlockSpec(w.shape, lambda i, me: (0, 0, 0)))
         in_specs += [pl.BlockSpec(x.shape, lambda i, me: (0, 0)) for x in edges]
-        operands += edges
+        operands += [w, *edges]
     else:
         ends = (4, sz.lane_groups, sz.group, 2 * LANES)
         out_specs.append(pl.BlockSpec((1,) + ends, lambda i, me: (i, 0, 0, 0, 0)))

time: 194 us -> 194 us (level)
  no operation moved by 1% of the time
where the time goes in v6:
time: 194 us; the launch traced here: 193 us
  Pallas kernels  65.9 us (34%)
  waiting for transfers between devices  64.5 us (33%)
  starting transfers between devices  56 us (29%)
  other arithmetic  3.41 us (2%)
  local copies, waits for them, and re-layouts  3.01 us (2%)
    pallas_call x2, Pallas kernels, march(): pl.pallas_call(functools.partial(march_kernel, sz, pieces.whole, whole_ou...  29.4 us
    ppermute x9, starting transfers between devices, shifted(): lax.ppermute(value, axes, [(i, i + step) for i in range(count) if 0 <= i...  23.4 us
    ppermute x9, waiting for transfers between devices, shifted(): lax.ppermute(value, axes, [(i, i + step) for i in range(count) if 0 <= i...  20.5 us
    all_to_all x4, waiting for transfers between devices, exchange(): return Pieces(True, [lax.all_to_all(array, 'mode', 0, 0, tiled=True)])  20.4 us
    ppermute x7, waiting for transfers between devices, exchange(): moved[k] = lax.ppermute(array, 'mode', [(i, i ^ k) for i in range(group)])  18.8 us
    all_to_all x4, starting transfers between devices, exchange(): return Pieces(True, [lax.all_to_all(array, 'mode', 0, 0, tiled=True)])  18.5 us
    pallas_call x2, Pallas kernels, adjoint_prep(): pl.pallas_call(functools.partial(adjoint_prep_kernel, sz, whole, with_rim...  11.4 us
    pallas_call x2, Pallas kernels, post(): pl.pallas_call(functools.partial(post_kernel, sz, pieces.whole, running,...  11.1 us
  transfers between devices with their start and end apart: 25, of which 13 were waited for; matrix products, arithmetic and copies ran while one was open for 2% of the time, Pallas kernels for 29%

profile of v6, /device:TPU:0, one launch (start us, length us, event | category | flops | bytes accessed | tf_op | source)
XLA Modules:
  0.0 193.1 jit_solution(6823255365042578427)
XLA Ops:
  0.6 5.7 %adjoint_prep.2 = (f32[8,3,256,128]{3,2,1,0:T(8,128)}, f32[3,4,4,8,256]{4,3,2,1,0:T(8,128)}) custom-call(s32[4]{0:T(128)} %call_exported.0.me_ref, f32[2,5,256,512]{3,2,1,0:T(8,128)} %x_ref.3, bf16[2,256,256]{2,1,0:T(8,128)(2,1)} %constant.84._.w_ref.rest_16_.rest_0_.rest_5_), custom_call_target="tpu_custom_call" | custom-call | flops 1 | bytes 1 | tf_op jit(solution)/shard_map/adjoint_prep/pallas_call | solution.py:273
  6.3 5.3 %all-to-all-start.1 = ((f32[8,3,256,128]{3,2,1,0:T(8,128)}), f32[8,3,256,128]{3,2,1,0:T(8,128)}, u32[]{:S(2)}, u32[]{:S(2)}) async-start(f32[8,3,256,128]{3,2,1,0:T(8,128)} %get-tuple-element.50), calls=%async_computation.1 | async-start | bytes 6291456 | tf_op jit(solution)/shard_map/all_to_all | solution.py:144
  11.7 2.4 %collective-permute-start = (f32[1,2,256,512]{3,2,1,0:T(8,128)S(1)}, f32[1,2,256,512]{3,2,1,0:T(8,128)S(1)}, u32[]{:S(2)}, u32[]{:S(2)}) collective-permute-start(f32[1,2,256,512]{3,2,1,0:T(8,128)S(1)} %constant_dynamic-slice_fusion), channel_id=1, source_target_pairs={{0,1},{1,0},{2,3},{3,2},{4,5},{5,4},{6,7},{7,6},{8,9},{9,8},{10,11... | collective-permute-start | bytes 3145736 | tf_op jit(solution)/shard_map/ppermute | solution.py:953
  14.1 1.7 edge_rows.1
  15.8 1.3 collective-permute-start.3
  17.1 1.9 collective-permute-start.1
  19.0 1.3 collective-permute-start.2
  20.5 0.7 pad_add_fusion.me_ref
  21.2 1.3 collective-permute-done.3.past
  22.5 15.7 %collective-permute-done.1.low.rest_1_ = f32[22,512]{1,0:T(8,128)S(1)} collective-permute-done((f32[22,512]{1,0:T(8,128)}, f32[22,512]{1,0:T(8,128)S(1)}, u32[]{:S(2)}, u32[]{:S(2)}) %collective-permute-start.1) | collective-permute-done | bytes 45088 | tf_op jit(solution)/shard_map/ppermute | solution.py:919
  38.2 0.7 collective-permute-done.2.high.rest_2_
  38.9 0.6 copy-done.3
  39.5 1.0 copy-done.1
  40.5 0.7 broadcast_in_dim.21.freq
  41.2 6.2 %forward_prep.1 = (f32[1,632,128]{2,1,0:T(8,128)}, f32[1,632,128]{2,1,0:T(8,128)}, f32[1,632,128]{2,1,0:T(8,128)}, f32[1,632,128]{2,1,0:T(8,128)}, f32[1,632,128...) custom-call(s32[4]{0:T(128)} %pad_add_fusion.me_ref, ...), custom_call_target="tpu_custom_call" | custom-call | flops 1 | bytes 1 | tf_op jit(solution)/shard_map/forward_prep/pallas_call | solution.py:351
  47.4 1.7 collective-permute-start.5
  49.2 1.7 collective-permute-start.7
  51.0 2.6 %collective-permute-start.9 = (f32[1,632,128]{2,1,0:T(8,128)}, f32[1,632,128]{2,1,0:T(8,128)}, u32[]{:S(2)}, u32[]{:S(2)}) collective-permute-start(f32[1,632,128]{2,1,0:T(8,128)} %get-tuple-element.43), channel_id=1, source_target_pairs={{0,24},{4,28},{8,16},{12,20},{16,8},{20,12},{24,0},{28,4},{1,25},{... | collective-permute-start | bytes 970760 | tf_op jit(solution)/shard_map/ppermute | solution.py:149
  53.5 4.6 %collective-permute-done.5.rest_2_.rest_10_ = f32[1,632,128]{2,1,0:T(8,128)} collective-permute-done((f32[1,632,128]{2,1,0:T(8,128)}, f32[1,632,128]{2,1,0:T(8,128)}, u32[]{:S(2)}, u32[]{:S(2)}) %collective-permute-start.5) | collective-permute-done | bytes 323616 | tf_op jit(solution)/shard_map/ppermute | solution.py:149
  58.2 1.4 collective-permute-start.10
  59.6 5.6 %adjoint_prep.3 = f32[8,2,288,128]{3,2,1,0:T(8,128)} custom-call(s32[4]{0:T(128)} %pad_add_fusion.me_ref, f32[2,5,256,512]{3,2,1,0:T(8,128)} %x_ref.3, f32[8,128]{1,0:T(8,128)} %get-tuple-element.46._, bf16[2,256,256]{2,1,0:T(8,128)(2,1)} %constant.84._.w_ref.rest_16_.rest_0_.rest_5_, f32[22,512]{1,0:T(8,128)} %copy-done.2, f32[22,512]{1,0:T(8,128)} %copy-done.3), custom_call_target="tpu_custom_call" | custom-call | flops 1 | bytes 1 | tf_op jit(solution)/shard_map/adjoint_prep/pallas_call | solution.py:273
  65.2 14.2 %collective-permute-done.8.rest_5_.rest_13_ = f32[1,632,128]{2,1,0:T(8,128)} collective-permute-done((f32[1,632,128]{2,1,0:T(8,128)}, f32[1,632,128]{2,1,0:T(8,128)}, u32[]{:S(2)}, u32[]{:S(2)}) %collective-permute-start.8) | collective-permute-done | bytes 323616 | tf_op jit(solution)/shard_map/ppermute | solution.py:149
  79.4 4.4 %all-to-all-start = ((f32[8,2,288,128]{3,2,1,0:T(8,128)}), f32[8,2,288,128]{3,2,1,0:T(8,128)}, u32[]{:S(2)}, u32[]{:S(2)}) async-start(f32[8,2,288,128]{3,2,1,0:T(8,128)} %adjoint_prep.3), calls=%async_computation | async-start | bytes 4718592 | tf_op jit(solution)/shard_map/all_to_all | solution.py:144
  83.8 6.2 %forward_physical.1 = (f32[2,2,64,16,128]{4,3,2,1,0:T(8,128)}, f32[2,64,1,128]{3,2,1,0:T(1,128)}, f32[3,2,2,64,128]{4,3,2,1,0:T(8,128)}, s32[68]{0:T(128)}) custom-call(s32[4]{0:T(128)} %pad_add_fusion.me_ref, f32[1,632,128]{2,1,0:T(8,128)} %get-tuple-element.37.rest_0_.rest_8_, f32[1,632,128]{2,1,0:T(8,128)} %collective-permute-done.4.rest_1_.rest_9_, ...), custom_call_target="tpu_custom_call" | custom-call | flops 1 | bytes 1 | tf_op jit(solution)/shard_map/forward_physical/pallas_call | solution.py:484
  90.1 15.8 %march.2 = (f32[8,3,256,128]{3,2,1,0:T(8,128)}, f32[2,2,64,16,128]{4,3,2,1,0:T(8,128)}, f32[2,2,64,128]{3,2,1,0:T(8,128)}, f32[64,128]{1,0:T(8,128)}) custom-call(s32[68]{0:T(128)} %get-tuple-element.45.table_ref, f32[8,3,256,128]{3,2,1,0:T(8,128)} %all-to-all-done.1.rest_0_, f32[2,2,64,16,128]{4,3,2,1,0:T(8,128)} %get-tuple-element.48.rest_1_, ...), custom_call_target="tpu_custom_call" | custom-call | flops 1 | bytes 1 | tf_op jit(solution)/shard_map/march/pallas_call | solution.py:700
  105.9 0.6 collective-permute-start.11
  106.5 1.1 collective-permute-done.11
  107.6 0.8 add.62
  108.4 2.7 %collective-permute-start.14 = (f32[64,128]{1,0:T(8,128)S(1)}, f32[64,128]{1,0:T(8,128)S(1)}, u32[]{:S(2)}, u32[]{:S(2)}) collective-permute-start(f32[64,128]{1,0:T(8,128)S(1)} %add.62), channel_id=1, source_target_pairs={{0,24},{4,28},{8,16},{12,20},{16,8},{20,12},{24,0},{28,4},{1,25},{... | collective-permute-start | bytes 98312 | tf_op jit(solution)/shard_map/ppermute | solution.py:928
  111.9 2.3 %collective-permute-done.14 = f32[64,128]{1,0:T(8,128)S(1)} collective-permute-done((f32[64,128]{1,0:T(8,128)S(1)}, f32[64,128]{1,0:T(8,128)S(1)}, u32[]{:S(2)}, u32[]{:S(2)}) %collective-permute-start.14) | collective-permute-done | bytes 32800 | tf_op jit(solution)/shard_map/ppermute | solution.py:928
  114.1 0.8 collective-permute-done.13
  115.4 4.5 %all-to-all-start.2 = ((f32[8,3,256,128]{3,2,1,0:T(8,128)}), f32[8,3,256,128]{3,2,1,0:T(8,128)}, u32[]{:S(2)}, u32[]{:S(2)}) async-start(f32[8,3,256,128]{3,2,1,0:T(8,128)} %get-tuple-element.56), calls=%async_computation.2 | async-start | bytes 6291456 | tf_op jit(solution)/shard_map/all_to_all | solution.py:144
  119.9 5.6 %collective-permute-start.17 = (f32[64,128]{1,0:T(8,128)S(1)}, f32[64,128]{1,0:T(8,128)S(1)}, u32[]{:S(2)}, u32[]{:S(2)}) collective-permute-start(f32[64,128]{1,0:T(8,128)S(1)} %add_add_fusion.1), channel_id=1, source_target_pairs={{0,3},{4,7},{8,11},{12,15},{16,19},{20,23},{24,27},{28,31}} | collective-permute-start | bytes 98312 | tf_op jit(solution)/shard_map/ppermute | solution.py:919
  125.5 1.3 collective-permute-start.16
  126.8 2.7 %collective-permute-start.15 = (f32[64,128]{1,0:T(8,128)S(1)}, f32[64,128]{1,0:T(8,128)S(1)}, u32[]{:S(2)}, u32[]{:S(2)}) collective-permute-start(f32[64,128]{1,0:T(8,128)S(1)} %add_add_fusion.1), channel_id=1, source_target_pairs={{0,1},{1,2},{2,3},{4,5},{5,6},{6,7},{8,9},{9,10},{10,11},{12,13},{... | collective-permute-start | bytes 98312 | tf_op jit(solution)/shard_map/ppermute | solution.py:919
  129.5 1.4 collective-permute-done.15
  130.9 0.6 add_add_fusion.rest_6_
  131.5 13.6 %march.3 = f32[8,2,256,128]{3,2,1,0:T(8,128)} custom-call(s32[68]{0:T(128)} %get-tuple-element.45.table_ref, f32[8,2,288,128]{3,2,1,0:T(8,128)} %all-to-all-done.rest_0_.rest_3_, f32[2,2,64,16,128]{4,3,2,1,0:T(8,128)} %get-tuple-element.48.rest_1_, f32[2,64,1,128]{3,2,1,0:T(1,128)} %get-tuple-element.49.rest_2_, ...), custom_call_target="tpu_custom_call" | custom-call | flops 1 | bytes 1 | tf_op jit(solution)/shard_map/march/pallas_call | solution.py:700
  145.1 12.7 %all-to-all-done.2.rest_0_ = f32[8,3,256,128]{3,2,1,0:T(8,128)} async-done(((f32[8,3,256,128]{3,2,1,0:T(8,128)}), f32[8,3,256,128]{3,2,1,0:T(8,128)}, u32[]{:S(2)}, u32[]{:S(2)}) %all-to-all-start.2) | async-done | bytes 3145760 | tf_op jit(solution)/shard_map/all_to_all | solution.py:144
  157.8 4.3 %all-to-all-start.3 = ((f32[8,2,256,128]{3,2,1,0:T(8,128)}), f32[8,2,256,128]{3,2,1,0:T(8,128)}, u32[]{:S(2)}, u32[]{:S(2)}) async-start(f32[8,2,256,128]{3,2,1,0:T(8,128)} %march.3), calls=%async_computation.3 | async-start | bytes 4194304 | tf_op jit(solution)/shard_map/all_to_all | solution.py:144
  162.2 0.6 fusion.8
  162.8 6.8 %post.2 = (f32[2,5,256,512]{3,2,1,0:T(8,128)}, f32[2,256,512]{2,1,0:T(8,128)}, f32[2,512]{1,0:T(2,128)}) custom-call(s32[4]{0:T(128)} %pad_add_fusion.me_ref, f32[8,3,256,128]{3,2,1,0:T(8,128)} %all-to-all-done.2.rest_0_, bf16[2,256,256]{2,1,0:T(8,128)(2,1)} %constant.98.rest_8_.rest_1_, f32[1,512]{1,0:T(1,128)} %bitcast.7, f32[1,512]{1,0:T(1,128)} %bitcast.6, ...), custom_call_target="tpu_custom_call" | custom-call | flops 1 | bytes 1 | tf_op jit(solution)/shard_map/post/pallas_call | solution.py:860
  169.6 5.6 %collective-permute-start.20 = (f32[2,512]{1,0:T(2,128)}, f32[2,512]{1,0:T(2,128)S(1)}, u32[]{:S(2)}, u32[]{:S(2)}) collective-permute-start(f32[2,512]{1,0:T(2,128)} %get-tuple-element.59), channel_id=1, source_target_pairs={{0,3},{4,7},{8,11},{12,15},{16,19},{20,23},{24,27},{28,31}} | collective-permute-start | bytes 12296 | tf_op jit(solution)/shard_map/ppermute | solution.py:919
  175.2 1.3 collective-permute-start.19
  176.5 2.5 %collective-permute-start.18 = (f32[2,512]{1,0:T(2,128)}, f32[2,512]{1,0:T(2,128)S(1)}, u32[]{:S(2)}, u32[]{:S(2)}) collective-permute-start(f32[2,512]{1,0:T(2,128)} %get-tuple-element.59), channel_id=1, source_target_pairs={{0,1},{1,2},{2,3},{4,5},{5,6},{6,7},{8,9},{9,10},{10,11},{12,13},{... | collective-permute-start | bytes 12296 | tf_op jit(solution)/shard_map/ppermute | solution.py:919
  179.0 1.5 collective-permute-done.18
  181.1 7.7 %all-to-all-done.3.rest_0_ = f32[8,2,256,128]{3,2,1,0:T(8,128)} async-done(((f32[8,2,256,128]{3,2,1,0:T(8,128)}), f32[8,2,256,128]{3,2,1,0:T(8,128)}, u32[]{:S(2)}, u32[]{:S(2)}) %all-to-all-start.3) | async-done | bytes 2097184 | tf_op jit(solution)/shard_map/all_to_all | solution.py:144
  188.8 4.3 %post.3 = f32[2,5,256,512]{3,2,1,0:T(8,128)} custom-call(s32[4]{0:T(128)} %pad_add_fusion.me_ref, f32[8,2,256,128]{3,2,1,0:T(8,128)} %all-to-all-done.3.rest_0_, f32[2,256,512]{2,1,0:T(8,128)} %get-tuple-element.58.rest_1_, f32[2,512]{1,0:T(2,128)} %add_add_fusion.2.rest_2_, f32[2,5,256,512]{3,2,1,0:T(8,128)} %get-tuple-element.60.rest_3_), custom_call_target="tpu_custom_call", output_to_operand_aliasing={{}: (4, {})} | custom-call | flops 1 | bytes 1 | tf_op jit(solution)/shard_map/post/pallas_call | solution.py:860
  (37 shorter events, 3.0 us)
Async XLA Ops:
  6.3 5.3 %copy-start = (f32[1,2,512,512]{3,2,1,0:T(8,128)S(1)}, f32[1,2,512,512]{3,2,1,0:T(8,128)}, u32[]{:S(2)}) copy-start(f32[1,2,512,512]{3,2,1,0:T(8,128)} %before.3) | copy-start | bytes 6291460
  6.3 73.2 %all-to-all-start.1 = ((f32[8,3,256,128]{3,2,1,0:T(8,128)}), f32[8,3,256,128]{3,2,1,0:T(8,128)}, u32[]{:S(2)}, u32[]{:S(2)}) async-start(f32[8,3,256,128]{3,2,1,0:T(8,128)} %get-tuple-element.50), calls=%async_computation.1 | async-start | bytes 6291456 | tf_op jit(solution)/shard_map/all_to_all | solution.py:144
  11.7 27.2 %collective-permute-start = (f32[1,2,256,512]{3,2,1,0:T(8,128)S(1)}, f32[1,2,256,512]{3,2,1,0:T(8,128)S(1)}, u32[]{:S(2)}, u32[]{:S(2)}) collective-permute-start(f32[1,2,256,512]{3,2,1,0:T(8,128)S(1)} %constant_dynamic-slice_fusion), channel_id=1, source_target_pairs={{0,1},{1,0},{2,3},{3,2},{4,5},{5,4},{6,7},{7,6},{8,9},{9,8},{10,11... | collective-permute-start | bytes 3145736 | tf_op jit(solution)/shard_map/ppermute | solution.py:953
  14.1 6.3 %copy-start.4 = (s32[512]{0:T(512)S(1)}, s32[512]{0:T(512)}, u32[]{:S(2)}) copy-start(s32[512]{0:T(512)} %param.11) | copy-start | bytes 6148
  15.8 6.7 %collective-permute-start.3 = (f32[2,512]{1,0:T(2,128)}, f32[2,512]{1,0:T(2,128)S(1)}, u32[]{:S(2)}, u32[]{:S(2)}) collective-permute-start(f32[2,512]{1,0:T(2,128)} %get-tuple-element.36), channel_id=1, source_target_pairs={{2,0},{3,1},{6,4},{7,5},{10,8},{11,9},{14,12},{15,13},{18,16},{19,... | collective-permute-start | bytes 12296 | tf_op jit(solution)/shard_map/ppermute | solution.py:919
  17.1 21.1 %collective-permute-start.1 = (f32[22,512]{1,0:T(8,128)}, f32[22,512]{1,0:T(8,128)S(1)}, u32[]{:S(2)}, u32[]{:S(2)}) collective-permute-start(f32[22,512]{1,0:T(8,128)} %get-tuple-element.34), channel_id=1, source_target_pairs={{0,1},{1,2},{2,3},{4,5},{5,6},{6,7},{8,9},{9,10},{10,11},{12,13},{... | collective-permute-start | bytes 135176 | tf_op jit(solution)/shard_map/ppermute | solution.py:919
  19.0 19.9 %collective-permute-start.2 = (f32[22,512]{1,0:T(8,128)}, f32[22,512]{1,0:T(8,128)S(1)}, u32[]{:S(2)}, u32[]{:S(2)}) collective-permute-start(f32[22,512]{1,0:T(8,128)} %get-tuple-element.35), channel_id=1, source_target_pairs={{1,0},{2,1},{3,2},{5,4},{6,5},{7,6},{9,8},{10,9},{11,10},{13,12},{... | collective-permute-start | bytes 135176 | tf_op jit(solution)/shard_map/ppermute | solution.py:919
  22.5 16.4 %copy-start.6 = (f32[2,512]{1,0:T(2,128)}, f32[2,512]{1,0:T(2,128)S(1)}, u32[]{:S(2)}) copy-start(f32[2,512]{1,0:T(2,128)S(1)} %collective-permute-done.3.past) | copy-start | bytes 12292
  38.2 0.7 copy-start.2
  38.9 0.6 copy-start.3
  39.5 1.0 copy-start.1
  47.4 3.6 %collective-permute-start.4 = (f32[1,632,128]{2,1,0:T(8,128)}, f32[1,632,128]{2,1,0:T(8,128)}, u32[]{:S(2)}, u32[]{:S(2)}) collective-permute-start(f32[1,632,128]{2,1,0:T(8,128)} %get-tuple-element.38), channel_id=1, source_target_pairs={{0,4},{4,0},{8,12},{12,8},{16,20},{20,16},{24,28},{28,24},{1,5},{5... | collective-permute-start | bytes 970760 | tf_op jit(solution)/shard_map/ppermute | solution.py:149
  47.4 10.8 %collective-permute-start.5 = (f32[1,632,128]{2,1,0:T(8,128)}, f32[1,632,128]{2,1,0:T(8,128)}, u32[]{:S(2)}, u32[]{:S(2)}) collective-permute-start(f32[1,632,128]{2,1,0:T(8,128)} %get-tuple-element.39), channel_id=1, source_target_pairs={{0,8},{4,12},{8,0},{12,4},{16,24},{20,28},{24,16},{28,20},{1,9},{5... | collective-permute-start | bytes 970760 | tf_op jit(solution)/shard_map/ppermute | solution.py:149
  49.1 16.1 %collective-permute-start.6 = (f32[1,632,128]{2,1,0:T(8,128)}, f32[1,632,128]{2,1,0:T(8,128)}, u32[]{:S(2)}, u32[]{:S(2)}) collective-permute-start(f32[1,632,128]{2,1,0:T(8,128)} %get-tuple-element.40), channel_id=1, source_target_pairs={{0,12},{4,8},{8,4},{12,0},{16,28},{20,24},{24,20},{28,16},{1,13},{... | collective-permute-start | bytes 970760 | tf_op jit(solution)/shard_map/ppermute | solution.py:149
  49.2 16.0 %collective-permute-start.7 = (f32[1,632,128]{2,1,0:T(8,128)}, f32[1,632,128]{2,1,0:T(8,128)}, u32[]{:S(2)}, u32[]{:S(2)}) collective-permute-start(f32[1,632,128]{2,1,0:T(8,128)} %get-tuple-element.41), channel_id=1, source_target_pairs={{0,16},{4,20},{8,24},{12,28},{16,0},{20,4},{24,8},{28,12},{1,17},{... | collective-permute-start | bytes 970760 | tf_op jit(solution)/shard_map/ppermute | solution.py:149
  50.9 28.5 %collective-permute-start.8 = (f32[1,632,128]{2,1,0:T(8,128)}, f32[1,632,128]{2,1,0:T(8,128)}, u32[]{:S(2)}, u32[]{:S(2)}) collective-permute-start(f32[1,632,128]{2,1,0:T(8,128)} %get-tuple-element.42), channel_id=1, source_target_pairs={{0,20},{4,16},{8,28},{12,24},{16,4},{20,0},{24,12},{28,8},{1,21},{... | collective-permute-start | bytes 970760 | tf_op jit(solution)/shard_map/ppermute | solution.py:149
  51.0 28.5 %collective-permute-start.9 = (f32[1,632,128]{2,1,0:T(8,128)}, f32[1,632,128]{2,1,0:T(8,128)}, u32[]{:S(2)}, u32[]{:S(2)}) collective-permute-start(f32[1,632,128]{2,1,0:T(8,128)} %get-tuple-element.43), channel_id=1, source_target_pairs={{0,24},{4,28},{8,16},{12,20},{16,8},{20,12},{24,0},{28,4},{1,25},{... | collective-permute-start | bytes 970760 | tf_op jit(solution)/shard_map/ppermute | solution.py:149
  58.2 21.3 %collective-permute-start.10 = (f32[1,632,128]{2,1,0:T(8,128)}, f32[1,632,128]{2,1,0:T(8,128)}, u32[]{:S(2)}, u32[]{:S(2)}) collective-permute-start(f32[1,632,128]{2,1,0:T(8,128)} %get-tuple-element.44), channel_id=1, source_target_pairs={{0,28},{4,24},{8,20},{12,16},{16,12},{20,8},{24,4},{28,0},{1,29},{... | collective-permute-start | bytes 970760 | tf_op jit(solution)/shard_map/ppermute | solution.py:149
  79.4 36.0 %all-to-all-start = ((f32[8,2,288,128]{3,2,1,0:T(8,128)}), f32[8,2,288,128]{3,2,1,0:T(8,128)}, u32[]{:S(2)}, u32[]{:S(2)}) async-start(f32[8,2,288,128]{3,2,1,0:T(8,128)} %adjoint_prep.3), calls=%async_computation | async-start | bytes 4718592 | tf_op jit(solution)/shard_map/all_to_all | solution.py:144
  105.9 1.7 collective-permute-start.11
  108.4 5.8 %collective-permute-start.14 = (f32[64,128]{1,0:T(8,128)S(1)}, f32[64,128]{1,0:T(8,128)S(1)}, u32[]{:S(2)}, u32[]{:S(2)}) collective-permute-start(f32[64,128]{1,0:T(8,128)S(1)} %add.62), channel_id=1, source_target_pairs={{0,24},{4,28},{8,16},{12,20},{16,8},{20,12},{24,0},{28,4},{1,25},{... | collective-permute-start | bytes 98312 | tf_op jit(solution)/shard_map/ppermute | solution.py:928
  111.0 3.9 %collective-permute-start.13 = (f32[64,128]{1,0:T(8,128)S(1)}, f32[64,128]{1,0:T(8,128)S(1)}, u32[]{:S(2)}, u32[]{:S(2)}) collective-permute-start(f32[64,128]{1,0:T(8,128)S(1)} %add.62), channel_id=1, source_target_pairs={{0,16},{4,20},{8,24},{12,28},{16,0},{20,4},{24,8},{28,12},{1,17},{... | collective-permute-start | bytes 98312 | tf_op jit(solution)/shard_map/ppermute | solution.py:928
  111.5 3.9 %collective-permute-start.12 = (f32[64,128]{1,0:T(8,128)S(1)}, f32[64,128]{1,0:T(8,128)S(1)}, u32[]{:S(2)}, u32[]{:S(2)}) collective-permute-start(f32[64,128]{1,0:T(8,128)S(1)} %add.62), channel_id=1, source_target_pairs={{0,8},{4,12},{8,0},{12,4},{16,24},{20,28},{24,16},{28,20},{1,9},{5... | collective-permute-start | bytes 98312 | tf_op jit(solution)/shard_map/ppermute | solution.py:928
  115.4 42.4 %all-to-all-start.2 = ((f32[8,3,256,128]{3,2,1,0:T(8,128)}), f32[8,3,256,128]{3,2,1,0:T(8,128)}, u32[]{:S(2)}, u32[]{:S(2)}) async-start(f32[8,3,256,128]{3,2,1,0:T(8,128)} %get-tuple-element.56), calls=%async_computation.2 | async-start | bytes 6291456 | tf_op jit(solution)/shard_map/all_to_all | solution.py:144
  119.9 9.6 %collective-permute-start.17 = (f32[64,128]{1,0:T(8,128)S(1)}, f32[64,128]{1,0:T(8,128)S(1)}, u32[]{:S(2)}, u32[]{:S(2)}) collective-permute-start(f32[64,128]{1,0:T(8,128)S(1)} %add_add_fusion.1), channel_id=1, source_target_pairs={{0,3},{4,7},{8,11},{12,15},{16,19},{20,23},{24,27},{28,31}} | collective-permute-start | bytes 98312 | tf_op jit(solution)/shard_map/ppermute | solution.py:919
  125.5 4.0 %collective-permute-start.16 = (f32[64,128]{1,0:T(8,128)S(1)}, f32[64,128]{1,0:T(8,128)S(1)}, u32[]{:S(2)}, u32[]{:S(2)}) collective-permute-start(f32[64,128]{1,0:T(8,128)S(1)} %add_add_fusion.1), channel_id=1, source_target_pairs={{0,2},{1,3},{4,6},{5,7},{8,10},{9,11},{12,14},{13,15},{16,18},{17,... | collective-permute-start | bytes 98312 | tf_op jit(solution)/shard_map/ppermute | solution.py:919
  126.8 4.1 %collective-permute-start.15 = (f32[64,128]{1,0:T(8,128)S(1)}, f32[64,128]{1,0:T(8,128)S(1)}, u32[]{:S(2)}, u32[]{:S(2)}) collective-permute-start(f32[64,128]{1,0:T(8,128)S(1)} %add_add_fusion.1), channel_id=1, source_target_pairs={{0,1},{1,2},{2,3},{4,5},{5,6},{6,7},{8,9},{9,10},{10,11},{12,13},{... | collective-permute-start | bytes 98312 | tf_op jit(solution)/shard_map/ppermute | solution.py:919
  145.1 17.1 %copy-start.5 = (s32[512]{0:T(512)S(1)}, s32[512]{0:T(512)}, u32[]{:S(2)}) copy-start(s32[512]{0:T(512)} %param.11) | copy-start | bytes 6148
  157.8 31.0 %all-to-all-start.3 = ((f32[8,2,256,128]{3,2,1,0:T(8,128)}), f32[8,2,256,128]{3,2,1,0:T(8,128)}, u32[]{:S(2)}, u32[]{:S(2)}) async-start(f32[8,2,256,128]{3,2,1,0:T(8,128)} %march.3), calls=%async_computation.3 | async-start | bytes 4194304 | tf_op jit(solution)/shard_map/all_to_all | solution.py:144
  169.6 9.4 %collective-permute-start.20 = (f32[2,512]{1,0:T(2,128)}, f32[2,512]{1,0:T(2,128)S(1)}, u32[]{:S(2)}, u32[]{:S(2)}) collective-permute-start(f32[2,512]{1,0:T(2,128)} %get-tuple-element.59), channel_id=1, source_target_pairs={{0,3},{4,7},{8,11},{12,15},{16,19},{20,23},{24,27},{28,31}} | collective-permute-start | bytes 12296 | tf_op jit(solution)/shard_map/ppermute | solution.py:919
  175.2 3.8 %collective-permute-start.19 = (f32[2,512]{1,0:T(2,128)}, f32[2,512]{1,0:T(2,128)S(1)}, u32[]{:S(2)}, u32[]{:S(2)}) collective-permute-start(f32[2,512]{1,0:T(2,128)} %get-tuple-element.59), channel_id=1, source_target_pairs={{0,2},{1,3},{4,6},{5,7},{8,10},{9,11},{12,14},{13,15},{16,18},{17,... | collective-permute-start | bytes 12296 | tf_op jit(solution)/shard_map/ppermute | solution.py:919
  176.5 4.0 %collective-permute-start.18 = (f32[2,512]{1,0:T(2,128)}, f32[2,512]{1,0:T(2,128)S(1)}, u32[]{:S(2)}, u32[]{:S(2)}) collective-permute-start(f32[2,512]{1,0:T(2,128)} %get-tuple-element.59), channel_id=1, source_target_pairs={{0,1},{1,2},{2,3},{4,5},{5,6},{6,7},{8,9},{9,10},{10,11},{12,13},{... | collective-permute-start | bytes 12296 | tf_op jit(solution)/shard_map/ppermute | solution.py:919
